TPU v7x, 32 devices: a whole 2x2x4 slice. The times are simulated.
32 devices in a mesh: lon: 4 (over y, core), lat: 8 (over z, x).
Axes of the slice: x: 2, y: 2, z: 4, core: 2. Of those that a mesh axis runs over, the one named last changes fastest.
Arguments:
- theta: float32 [16, 1024, 1024], P(None, 'lat', 'lon'), may hold values from -6 to 6
- kappa: float32 [1024, 1024], P('lat', 'lon'), may hold values from 0.03 to 0.24
- layer_weight: float32 [16], replicated, may hold values from 0.25 to 1.5
- diag: float32 [1024, 1024], P(('lon', 'lat')), may hold values from 0.2 to 2
- land_blocks: int32 [32, 32], replicated, may hold values 0 or 1
Outputs:
- new_theta: float32 [16, 1024, 1024], P(None, 'lat', 'lon')
- psi: float32 [1024, 1024], P(('lon', 'lat'))
All inputs are finite; a program needn't handle non-finite values.
Results may differ from a plain program's by a relative error of at most 0.0001.
Values sent between devices are 32-bit elements; how exact they have to be, the bound alone decides.
No kernel may reach another device: no remote copies, remote signals or barrier semaphores. Data moves between devices by JAX's collectives and lax.ppermute only.
A program may use at most 64 MiB of HBM per device.

v0:
```python
import jax
import jax.numpy as jnp
from jax import lax
from jax.sharding import PartitionSpec as P

CX = 256
CY = 128
BS = 32
ITERS = 4


def extended(cells, sides, width, closed):
    for axis, dim in sides:
        count = lax.axis_size(axis)
        ends = count if closed else count - 1
        head = lax.slice_in_dim(cells, 0, width, axis=dim)
        tail = lax.slice_in_dim(cells, cells.shape[dim] - width, cells.shape[dim], axis=dim)
        cells = jnp.concatenate(
            [
                lax.ppermute(tail, axis, [(i, (i + 1) % count) for i in range(ends)]),
                cells,
                lax.ppermute(head, axis, [((i + 1) % count, i) for i in range(ends)]),
            ],
            axis=dim,
        )
    return cells


def partner(shard, axis, distance):
    return lax.ppermute(shard, axis, [(i, i ^ 1 << distance) for i in range(lax.axis_size(axis))])


def cell_mask(table, row_start, row_count, col_start, col_count):
    row_cells = row_start + jnp.arange(row_count, dtype=jnp.int32)
    col_cells = col_start + jnp.arange(col_count, dtype=jnp.int32)
    row_hot = (
        row_cells[:, None] // BS == jnp.arange(table.shape[0], dtype=jnp.int32)[None, :]
    ).astype(jnp.float32)
    col_hot = (
        col_cells[:, None] // BS == jnp.arange(table.shape[1], dtype=jnp.int32)[None, :]
    ).astype(jnp.float32)
    partial_rows = jnp.dot(row_hot, table, precision=lax.Precision.HIGHEST)
    return jnp.dot(partial_rows, col_hot.T, precision=lax.Precision.HIGHEST)


def per_device(theta, kappa, layer_weight, diag, land_blocks):
    lat_count = lax.axis_size("lat")
    lon_bits = lax.axis_size("lon").bit_length() - 1
    joint_bits = lax.axis_size(("lon", "lat")).bit_length() - 1
    lon_index = lax.axis_index("lon")
    lat_index = lax.axis_index("lat")
    strip_index = lax.axis_index(("lon", "lat"))
    strip_width = CX // lat_count
    full_rows = CY * lat_count
    table = land_blocks.astype(jnp.float32)
    ocean_block = cell_mask(table, lat_index * CY, CY, lon_index * CX, CX)
    masked = ocean_block[None] * theta
    rows_padded = extended(masked, (("lat", 1),), 1, False)
    cols_padded = extended(masked, (("lon", 2),), 1, True)
    peer_row = masked[:, CY - 1, :]
    for bit_number in range(lon_bits):
        peer_row = partner(peer_row, "lon", bit_number)
    mirror_row = peer_row[:, ::-1]
    north_edge = jnp.where(lat_index == lat_count - 1, mirror_row, rows_padded[:, CY + 1, :])
    northern = jnp.concatenate([rows_padded[:, 2 : CY + 1, :], north_edge[:, None, :]], axis=1)
    beside_all = cols_padded[:, :, 2:] + cols_padded[:, :, :-2] + rows_padded[:, :-2, :] + northern
    new_theta = theta + ocean_block[None] * kappa[None] * (beside_all - 4.0 * masked)
    summed = jnp.einsum("k,kyx->xy", layer_weight, new_theta, precision=lax.Precision.HIGHEST)
    column_sum = lax.all_to_all(summed, "lat", split_axis=0, concat_axis=1, tiled=True)
    ocean_strip = cell_mask(table, 0, full_rows, strip_index * strip_width, strip_width).T
    forcing = ocean_strip * column_sum

    def operate(field):
        padded = extended(field, ((("lon", "lat"), 0),), 1, True)
        top_row = field[:, full_rows - 1]
        for bit_number in range(joint_bits):
            top_row = partner(top_row, ("lon", "lat"), bit_number)
        mirror_top = top_row[::-1]
        southern = jnp.concatenate([jnp.zeros_like(field[:, :1]), field[:, :-1]], axis=1)
        northward = jnp.concatenate([field[:, 1:], mirror_top[:, None]], axis=1)
        neighbours = padded[2:] + padded[:-2] + southern + northward
        return ocean_strip * ((4.0 + diag) * field - neighbours)

    def two_products(residual, applied):
        return lax.psum((jnp.sum(residual * residual), jnp.sum(residual * applied)), ("lon", "lat"))

    solution = jnp.zeros_like(forcing)
    residual = forcing
    applied = operate(residual)
    norm_now, product = two_products(residual, applied)
    step_size = norm_now / product
    direction = residual
    applied_dir = applied
    for iteration in range(ITERS):
        solution = solution + step_size * direction
        residual = residual - step_size * applied_dir
        if iteration + 1 < ITERS:
            applied = operate(residual)
            norm_next, product = two_products(residual, applied)
            beta_ratio = norm_next / norm_now
            step_size = norm_next / (product - beta_ratio * norm_next / step_size)
            direction = residual + beta_ratio * direction
            applied_dir = applied + beta_ratio * applied_dir
            norm_now = norm_next
    return (new_theta, solution)


def solution(mesh):
    placed = (P(None, "lat", "lon"), P("lat", "lon"), P(), P(("lon", "lat"), None), P())
    return jax.shard_map(
        per_device,
        mesh=mesh,
        in_specs=placed,
        out_specs=(P(None, "lat", "lon"), P(("lon", "lat"), None)),
        check_vma=False,
    )
```

profile of v0, /device:TPU:0, one launch (start us, length us, event | category | flops | bytes accessed | tf_op | source)
XLA Modules:
  0.0 294.3 jit_solution(11454768389864713319)
XLA Ops:
  1.6 1.3 fusion.57
  2.9 2.8 copy_multiply_fusion
  6.2 1.3 collective-permute-start.5
  7.5 5.0 %collective-permute-start.2 = (f32[16,1,256]{2,0,1:T(8,128)S(1)}, f32[16,1,256]{2,0,1:T(8,128)S(1)}, u32[]{:S(2)}, u32[]{:S(2)}) collective-permute-start(f32[16,1,256]{2,0,1:T(8,128)S(1)} %get-tuple-element.27), channel_id=1, source_target_pairs={{0,1},{1,2},{2,3},{3,4},{4,5},{5,6},{6,7},{8,9},{9,10},{10,11},{11... | collective-permute-start | bytes 49160 | tf_op jit(solution)/shard_map/ppermute | solution.py:20
  12.6 1.3 fusion.48
  13.9 1.6 copy.23
  15.5 1.6 collective-permute-start
  19.1 1.5 collective-permute-done.1
  20.7 1.4 copy.26
  22.3 7.5 %fusion.4 = f32[16,128,256]{2,0,1:T(8,128)S(1)} fusion(f32[16,128,256]{2,0,1:T(8,128)} %copy-done.1, f32[16,1,256]{2,0,1:T(8,128)S(1)} %collective-permute-done.2, f32[16,128,1]{2,0,1:T(8,128)} %copy.26, f32[16,128,1]{2,0,1:T(8,128)S(1)} %copy.24, f32[16,1,256]{2,0,1:T(8,128)S(1)} %fusion.34, f32[16,127,256]{2,0,1:T(8,128)S(1)} %slice-done, ...), kind=kLoop, calls=%fused_computation.5 | loop fusion | flops 5767168 | bytes 8552448 | tf_op jit(solution)/shard_map/add | solution.py:67
  29.8 1.3 copy-done.2
  33.1 5.7 %all-to-all-start = ((f32[8,32,128]{2,1,0:T(8,128)}), f32[8,32,128]{2,1,0:T(8,128)S(1)}, u32[]{:S(2)}, u32[]{:S(2)}) async-start(f32[8,32,128]{2,1,0:T(8,128)} %bitcast.6), calls=%async_computation | async-start | bytes 262144 | tf_op jit(solution)/shard_map/all_to_all | solution.py:69
  39.4 6.8 %all-to-all-done = f32[8,32,128]{2,1,0:T(8,128)S(1)} async-done(((f32[8,32,128]{2,1,0:T(8,128)}), f32[8,32,128]{2,1,0:T(8,128)S(1)}, u32[]{:S(2)}, u32[]{:S(2)}) %all-to-all-start) | async-done | bytes 131104 | tf_op jit(solution)/shard_map/all_to_all | solution.py:69
  46.9 3.3 %collective-permute-done.8 = f32[32]{0:T(128)S(1)} collective-permute-done((f32[32]{0:T(128)S(1)}, f32[32]{0:T(128)S(1)}, u32[]{:S(2)}, u32[]{:S(2)}) %collective-permute-start.8) | collective-permute-done | bytes 160 | tf_op jit(solution)/shard_map/ppermute | solution.py:30
  50.2 3.5 %collective-permute-done.9 = f32[32]{0:T(128)S(1)} collective-permute-done((f32[32]{0:T(128)S(1)}, f32[32]{0:T(128)S(1)}, u32[]{:S(2)}, u32[]{:S(2)}) %collective-permute-start.9) | collective-permute-done | bytes 160 | tf_op jit(solution)/shard_map/ppermute | solution.py:30
  54.1 4.0 %collective-permute-done.10 = f32[32]{0:T(128)S(1)} collective-permute-done((f32[32]{0:T(128)S(1)}, f32[32]{0:T(128)S(1)}, u32[]{:S(2)}, u32[]{:S(2)}) %collective-permute-start.10) | collective-permute-done | bytes 160 | tf_op jit(solution)/shard_map/ppermute | solution.py:30
  59.9 2.9 collective-permute-done.12
  63.0 1.8 collective-permute-done.7
  65.5 37.1 %all-reduce.7 = (f32[]{:T(128)}, f32[]{:T(128)}) all-reduce(f32[]{:T(128)} %get-tuple-element.13, f32[]{:T(128)} %get-tuple-element.12), channel_id=1, replica_groups=mesh['lon'=4,'lat'=8] {'lon','lat'}, use_global_device_ids=true, to_apply=%region_1.2 | all-reduce | flops 2 | bytes 16 | tf_op jit(solution)/shard_map/psum | solution.py:85
  104.2 2.3 collective-permute-start.15
  106.5 1.5 collective-permute-done.15
  108.0 2.9 collective-permute-start.16
  110.9 1.5 collective-permute-done.16
  112.4 2.1 collective-permute-start.17
  114.5 2.3 collective-permute-done.17
  116.8 1.5 collective-permute-start.18
  120.3 2.4 collective-permute-done.19
  122.9 2.1 collective-permute-done.14
  125.8 37.9 %all-reduce.6 = (f32[]{:T(128)}, f32[]{:T(128)}) all-reduce(f32[]{:T(128)} %get-tuple-element.11, f32[]{:T(128)} %get-tuple-element.10), channel_id=1, replica_groups=mesh['lon'=4,'lat'=8] {'lon','lat'}, use_global_device_ids=true, to_apply=%region_5.6 | all-reduce | flops 2 | bytes 16 | tf_op jit(solution)/shard_map/psum | solution.py:85
  168.2 2.3 collective-permute-start.22
  170.6 1.5 collective-permute-done.22
  172.1 2.1 collective-permute-start.23
  174.2 1.5 collective-permute-done.23
  175.7 2.1 collective-permute-start.24
  177.8 2.3 collective-permute-done.24
  180.1 1.5 collective-permute-start.25
  183.6 2.4 collective-permute-done.26
  186.2 2.1 collective-permute-done.21
  189.1 38.1 %all-reduce.5 = (f32[]{:T(128)}, f32[]{:T(128)}) all-reduce(f32[]{:T(128)} %get-tuple-element.9, f32[]{:T(128)} %get-tuple-element.8), channel_id=1, replica_groups=mesh['lon'=4,'lat'=8] {'lon','lat'}, use_global_device_ids=true, to_apply=%region_9.10 | all-reduce | flops 2 | bytes 16 | tf_op jit(solution)/shard_map/psum | solution.py:85
  231.2 2.3 collective-permute-start.29
  233.5 2.5 copy.33
  236.0 2.1 collective-permute-start.30
  238.2 1.5 collective-permute-done.30
  239.7 2.1 collective-permute-start.31
  241.8 2.3 collective-permute-done.31
  246.8 2.2 collective-permute-done.33
  249.2 2.1 collective-permute-done.28
  252.0 37.9 %all-reduce.4 = (f32[]{:T(128)}, f32[]{:T(128)}) all-reduce(f32[]{:T(128)} %get-tuple-element.7, f32[]{:T(128)} %get-tuple-element.6), channel_id=1, replica_groups=mesh['lon'=4,'lat'=8] {'lon','lat'}, use_global_device_ids=true, to_apply=%region_13.14 | all-reduce | flops 2 | bytes 16 | tf_op jit(solution)/shard_map/psum | solution.py:85
  (89 shorter events, 20.8 us)
Async XLA Ops:
  0.6 30.5 %copy-start = (f32[16]{0:T(128)S(1)}, f32[16]{0:T(128)}, u32[]{:S(2)}) copy-start(f32[16]{0:T(128)} %param.7) | copy-start | bytes 196
  5.7 12.9 %copy-start.1 = (f32[16,128,256]{2,0,1:T(8,128)}, f32[16,128,256]{2,0,1:T(8,128)S(1)}, u32[]{:S(2)}) copy-start(f32[16,128,256]{2,0,1:T(8,128)S(1)} %copy_multiply_fusion) | copy-start | bytes 6291460
  5.7 11.9 %collective-permute-start.3 = (f32[16,256]{1,0:T(8,128)S(1)}, f32[16,256]{1,0:T(8,128)S(1)}, u32[]{:S(2)}, u32[]{:S(2)}) collective-permute-start(f32[16,256]{1,0:T(8,128)S(1)} %get-tuple-element.26), channel_id=1, source_target_pairs={{0,8},{8,0},{16,24},{24,16},{1,9},{9,1},{17,25},{25,17},{2,10},{10... | collective-permute-start | bytes 49160 | tf_op jit(solution)/shard_map/ppermute | solution.py:30
  6.2 16.0 %collective-permute-start.5 = (f32[16,1,256]{2,0,1:T(8,128)S(1)}, f32[16,1,256]{2,0,1:T(8,128)S(1)}, u32[]{:S(2)}, u32[]{:S(2)}) collective-permute-start(f32[16,1,256]{2,0,1:T(8,128)S(1)} %get-tuple-element.25), channel_id=1, source_target_pairs={{1,0},{2,1},{3,2},{4,3},{5,4},{6,5},{7,6},{9,8},{10,9},{11,10},{12... | collective-permute-start | bytes 49160 | tf_op jit(solution)/shard_map/ppermute | solution.py:22
  7.5 14.7 %collective-permute-start.2 = (f32[16,1,256]{2,0,1:T(8,128)S(1)}, f32[16,1,256]{2,0,1:T(8,128)S(1)}, u32[]{:S(2)}, u32[]{:S(2)}) collective-permute-start(f32[16,1,256]{2,0,1:T(8,128)S(1)} %get-tuple-element.27), channel_id=1, source_target_pairs={{0,1},{1,2},{2,3},{3,4},{4,5},{5,6},{6,7},{8,9},{9,10},{10,11},{11... | collective-permute-start | bytes 49160 | tf_op jit(solution)/shard_map/ppermute | solution.py:20
  15.5 3.1 %collective-permute-start = (f32[16,128,1]{1,0,2:T(8,128)S(1)}, f32[16,128,1]{1,0,2:T(8,128)S(1)}, u32[]{:S(2)}, u32[]{:S(2)}) collective-permute-start(f32[16,128,1]{1,0,2:T(8,128)S(1)} %copy.23), channel_id=1, source_target_pairs={{8,0},{16,8},{24,16},{0,24},{9,1},{17,9},{25,17},{1,25},{10,2},{18... | collective-permute-start | bytes 24584 | tf_op jit(solution)/shard_map/ppermute | solution.py:22
  17.6 3.1 %collective-permute-start.1 = (f32[16,128,1]{1,0,2:T(8,128)S(1)}, f32[16,128,1]{1,0,2:T(8,128)S(1)}, u32[]{:S(2)}, u32[]{:S(2)}) collective-permute-start(f32[16,128,1]{1,0,2:T(8,128)S(1)} %copy.25), channel_id=1, source_target_pairs={{0,8},{8,16},{16,24},{24,0},{1,9},{9,17},{17,25},{25,1},{2,10},{10... | collective-permute-start | bytes 24584 | tf_op jit(solution)/shard_map/ppermute | solution.py:20
  17.6 4.5 %collective-permute-start.4 = (f32[16,256]{1,0:T(8,128)S(1)}, f32[16,256]{1,0:T(8,128)S(1)}, u32[]{:S(2)}, u32[]{:S(2)}) collective-permute-start(f32[16,256]{1,0:T(8,128)S(1)} %collective-permute-done.3), channel_id=1, source_target_pairs={{0,16},{8,24},{16,0},{24,8},{1,17},{9,25},{17,1},{25,9},{2,18},{10... | collective-permute-start | bytes 49160 | tf_op jit(solution)/shard_map/ppermute | solution.py:30
  18.6 3.7 %slice-start = ((f32[16,128,256]{2,0,1:T(8,128)}), f32[16,127,256]{2,0,1:T(8,128)S(1)}, s32[]{:S(2)}) async-start(f32[16,128,256]{2,0,1:T(8,128)} %copy-done.1), calls=%async_computation.1 | async-start | bytes 4161536 | tf_op jit(solution)/shard_map/slice | solution.py:65
  29.8 1.3 copy-start.2
  31.1 7.7 %copy-start.5 = (s32[32,32]{1,0:T(8,128)S(1)}, s32[32,32]{1,0:T(8,128)}, u32[]{:S(2)}) copy-start(s32[32,32]{1,0:T(8,128)} %param.9) | copy-start | bytes 12292
  31.1 33.7 %copy-start.4 = (f32[32,1024]{1,0:T(8,128)S(1)}, f32[32,1024]{1,0:T(8,128)}, u32[]{:S(2)}) copy-start(f32[32,1024]{1,0:T(8,128)} %param.8) | copy-start | bytes 393220
  33.1 13.0 %all-to-all-start = ((f32[8,32,128]{2,1,0:T(8,128)}), f32[8,32,128]{2,1,0:T(8,128)S(1)}, u32[]{:S(2)}, u32[]{:S(2)}) async-start(f32[8,32,128]{2,1,0:T(8,128)} %bitcast.6), calls=%async_computation | async-start | bytes 262144 | tf_op jit(solution)/shard_map/all_to_all | solution.py:69
  46.6 3.6 %collective-permute-start.8 = (f32[32]{0:T(128)S(1)}, f32[32]{0:T(128)S(1)}, u32[]{:S(2)}, u32[]{:S(2)}) collective-permute-start(f32[32]{0:T(128)S(1)} %slice_reduce_fusion.3), channel_id=1, source_target_pairs={{0,1},{1,0},{2,3},{3,2},{4,5},{5,4},{6,7},{7,6},{8,9},{9,8},{10,11... | collective-permute-start | bytes 392 | tf_op jit(solution)/shard_map/ppermute | solution.py:30
  50.2 3.5 %collective-permute-start.9 = (f32[32]{0:T(128)S(1)}, f32[32]{0:T(128)S(1)}, u32[]{:S(2)}, u32[]{:S(2)}) collective-permute-start(f32[32]{0:T(128)S(1)} %collective-permute-done.8), channel_id=1, source_target_pairs={{0,2},{1,3},{2,0},{3,1},{4,6},{5,7},{6,4},{7,5},{8,10},{9,11},{10,... | collective-permute-start | bytes 392 | tf_op jit(solution)/shard_map/ppermute | solution.py:30
  53.7 4.4 %collective-permute-start.10 = (f32[32]{0:T(128)S(1)}, f32[32]{0:T(128)S(1)}, u32[]{:S(2)}, u32[]{:S(2)}) collective-permute-start(f32[32]{0:T(128)S(1)} %collective-permute-done.9), channel_id=1, source_target_pairs={{0,4},{1,5},{2,6},{3,7},{4,0},{5,1},{6,2},{7,3},{8,12},{9,13},{10,... | collective-permute-start | bytes 392 | tf_op jit(solution)/shard_map/ppermute | solution.py:30
  54.1 8.9 %collective-permute-start.6 = (f32[1,1024]{1,0:T(1,128)S(1)}, f32[1,1024]{1,0:T(1,128)S(1)}, u32[]{:S(2)}, u32[]{:S(2)}) collective-permute-start(f32[1,1024]{1,0:T(1,128)S(1)} %get-tuple-element.42), channel_id=1, source_target_pairs={{1,0},{2,1},{3,2},{4,3},{5,4},{6,5},{7,6},{8,7},{9,8},{10,9},{11,1... | collective-permute-start | bytes 12296 | tf_op jit(solution)/shard_map/ppermute | solution.py:22
  58.2 1.1 collective-permute-start.11
  58.2 6.6 %collective-permute-start.7 = (f32[1,1024]{1,0:T(1,128)S(1)}, f32[1,1024]{1,0:T(1,128)S(1)}, u32[]{:S(2)}, u32[]{:S(2)}) collective-permute-start(f32[1,1024]{1,0:T(1,128)S(1)} %get-tuple-element.43), channel_id=1, source_target_pairs={{0,1},{1,2},{2,3},{3,4},{4,5},{5,6},{6,7},{7,8},{8,9},{9,10},{10,1... | collective-permute-start | bytes 12296 | tf_op jit(solution)/shard_map/ppermute | solution.py:20
  59.3 3.5 %collective-permute-start.12 = (f32[32]{0:T(128)S(1)}, f32[32]{0:T(128)S(1)}, u32[]{:S(2)}, u32[]{:S(2)}) collective-permute-start(f32[32]{0:T(128)S(1)} %collective-permute-done.11), channel_id=1, source_target_pairs={{0,16},{1,17},{2,18},{3,19},{4,20},{5,21},{6,22},{7,23},{8,24},{9,... | collective-permute-start | bytes 392 | tf_op jit(solution)/shard_map/ppermute | solution.py:30
  104.0 129.5 %copy-start.3 = (f32[16,128,256]{2,0,1:T(8,128)S(1)}, f32[16,128,256]{2,0,1:T(8,128)}, u32[]{:S(2)}) copy-start(f32[16,128,256]{2,0,1:T(8,128)} %copy-done.2) | copy-start | bytes 6291460
  104.2 3.9 %collective-permute-start.15 = (f32[32]{0:T(128)S(1)}, f32[32]{0:T(128)S(1)}, u32[]{:S(2)}, u32[]{:S(2)}) collective-permute-start(f32[32]{0:T(128)S(1)} %slice_reduce_fusion.2), channel_id=1, source_target_pairs={{0,1},{1,0},{2,3},{3,2},{4,5},{5,4},{6,7},{7,6},{8,9},{9,8},{10,11... | collective-permute-start | bytes 392 | tf_op jit(solution)/shard_map/ppermute | solution.py:30
  108.0 4.4 %collective-permute-start.16 = (f32[32]{0:T(128)S(1)}, f32[32]{0:T(128)S(1)}, u32[]{:S(2)}, u32[]{:S(2)}) collective-permute-start(f32[32]{0:T(128)S(1)} %collective-permute-done.15), channel_id=1, source_target_pairs={{0,2},{1,3},{2,0},{3,1},{4,6},{5,7},{6,4},{7,5},{8,10},{9,11},{10,... | collective-permute-start | bytes 392 | tf_op jit(solution)/shard_map/ppermute | solution.py:30
  112.4 4.4 %collective-permute-start.17 = (f32[32]{0:T(128)S(1)}, f32[32]{0:T(128)S(1)}, u32[]{:S(2)}, u32[]{:S(2)}) collective-permute-start(f32[32]{0:T(128)S(1)} %collective-permute-done.16), channel_id=1, source_target_pairs={{0,4},{1,5},{2,6},{3,7},{4,0},{5,1},{6,2},{7,3},{8,12},{9,13},{10,... | collective-permute-start | bytes 392 | tf_op jit(solution)/shard_map/ppermute | solution.py:30
  114.5 8.4 %collective-permute-start.13 = (f32[1,1024]{1,0:T(1,128)S(1)}, f32[1,1024]{1,0:T(1,128)S(1)}, u32[]{:S(2)}, u32[]{:S(2)}) collective-permute-start(f32[1,1024]{1,0:T(1,128)S(1)} %get-tuple-element.38), channel_id=1, source_target_pairs={{1,0},{2,1},{3,2},{4,3},{5,4},{6,5},{7,6},{8,7},{9,8},{10,9},{11,1... | collective-permute-start | bytes 12296 | tf_op jit(solution)/shard_map/ppermute | solution.py:22
  116.8 2.3 collective-permute-start.18
  118.4 6.6 %collective-permute-start.14 = (f32[1,1024]{1,0:T(1,128)S(1)}, f32[1,1024]{1,0:T(1,128)S(1)}, u32[]{:S(2)}, u32[]{:S(2)}) collective-permute-start(f32[1,1024]{1,0:T(1,128)S(1)} %get-tuple-element.39), channel_id=1, source_target_pairs={{0,1},{1,2},{2,3},{3,4},{4,5},{5,6},{6,7},{7,8},{8,9},{9,10},{10,1... | collective-permute-start | bytes 12296 | tf_op jit(solution)/shard_map/ppermute | solution.py:20
  119.2 3.5 %collective-permute-start.19 = (f32[32]{0:T(128)S(1)}, f32[32]{0:T(128)S(1)}, u32[]{:S(2)}, u32[]{:S(2)}) collective-permute-start(f32[32]{0:T(128)S(1)} %collective-permute-done.18), channel_id=1, source_target_pairs={{0,16},{1,17},{2,18},{3,19},{4,20},{5,21},{6,22},{7,23},{8,24},{9,... | collective-permute-start | bytes 392 | tf_op jit(solution)/shard_map/ppermute | solution.py:30
  168.2 3.9 %collective-permute-start.22 = (f32[32]{0:T(128)S(1)}, f32[32]{0:T(128)S(1)}, u32[]{:S(2)}, u32[]{:S(2)}) collective-permute-start(f32[32]{0:T(128)S(1)} %slice_reduce_fusion.1), channel_id=1, source_target_pairs={{0,1},{1,0},{2,3},{3,2},{4,5},{5,4},{6,7},{7,6},{8,9},{9,8},{10,11... | collective-permute-start | bytes 392 | tf_op jit(solution)/shard_map/ppermute | solution.py:30
  172.1 3.6 %collective-permute-start.23 = (f32[32]{0:T(128)S(1)}, f32[32]{0:T(128)S(1)}, u32[]{:S(2)}, u32[]{:S(2)}) collective-permute-start(f32[32]{0:T(128)S(1)} %collective-permute-done.22), channel_id=1, source_target_pairs={{0,2},{1,3},{2,0},{3,1},{4,6},{5,7},{6,4},{7,5},{8,10},{9,11},{10,... | collective-permute-start | bytes 392 | tf_op jit(solution)/shard_map/ppermute | solution.py:30
  175.7 4.4 %collective-permute-start.24 = (f32[32]{0:T(128)S(1)}, f32[32]{0:T(128)S(1)}, u32[]{:S(2)}, u32[]{:S(2)}) collective-permute-start(f32[32]{0:T(128)S(1)} %collective-permute-done.23), channel_id=1, source_target_pairs={{0,4},{1,5},{2,6},{3,7},{4,0},{5,1},{6,2},{7,3},{8,12},{9,13},{10,... | collective-permute-start | bytes 392 | tf_op jit(solution)/shard_map/ppermute | solution.py:30
  177.8 8.4 %collective-permute-start.20 = (f32[1,1024]{1,0:T(1,128)S(1)}, f32[1,1024]{1,0:T(1,128)S(1)}, u32[]{:S(2)}, u32[]{:S(2)}) collective-permute-start(f32[1,1024]{1,0:T(1,128)S(1)} %get-tuple-element.34), channel_id=1, source_target_pairs={{1,0},{2,1},{3,2},{4,3},{5,4},{6,5},{7,6},{8,7},{9,8},{10,9},{11,1... | collective-permute-start | bytes 12296 | tf_op jit(solution)/shard_map/ppermute | solution.py:22
  180.1 2.3 collective-permute-start.25
  181.7 6.7 %collective-permute-start.21 = (f32[1,1024]{1,0:T(1,128)S(1)}, f32[1,1024]{1,0:T(1,128)S(1)}, u32[]{:S(2)}, u32[]{:S(2)}) collective-permute-start(f32[1,1024]{1,0:T(1,128)S(1)} %get-tuple-element.35), channel_id=1, source_target_pairs={{0,1},{1,2},{2,3},{3,4},{4,5},{5,6},{6,7},{7,8},{8,9},{9,10},{10,1... | collective-permute-start | bytes 12296 | tf_op jit(solution)/shard_map/ppermute | solution.py:20
  182.5 3.5 %collective-permute-start.26 = (f32[32]{0:T(128)S(1)}, f32[32]{0:T(128)S(1)}, u32[]{:S(2)}, u32[]{:S(2)}) collective-permute-start(f32[32]{0:T(128)S(1)} %collective-permute-done.25), channel_id=1, source_target_pairs={{0,16},{1,17},{2,18},{3,19},{4,20},{5,21},{6,22},{7,23},{8,24},{9,... | collective-permute-start | bytes 392 | tf_op jit(solution)/shard_map/ppermute | solution.py:30
  231.2 4.9 %collective-permute-start.29 = (f32[32]{0:T(128)S(1)}, f32[32]{0:T(128)S(1)}, u32[]{:S(2)}, u32[]{:S(2)}) collective-permute-start(f32[32]{0:T(128)S(1)} %slice_reduce_fusion), channel_id=1, source_target_pairs={{0,1},{1,0},{2,3},{3,2},{4,5},{5,4},{6,7},{7,6},{8,9},{9,8},{10,11... | collective-permute-start | bytes 392 | tf_op jit(solution)/shard_map/ppermute | solution.py:30
  236.0 3.6 %collective-permute-start.30 = (f32[32]{0:T(128)S(1)}, f32[32]{0:T(128)S(1)}, u32[]{:S(2)}, u32[]{:S(2)}) collective-permute-start(f32[32]{0:T(128)S(1)} %collective-permute-done.29), channel_id=1, source_target_pairs={{0,2},{1,3},{2,0},{3,1},{4,6},{5,7},{6,4},{7,5},{8,10},{9,11},{10,... | collective-permute-start | bytes 392 | tf_op jit(solution)/shard_map/ppermute | solution.py:30
  239.7 4.4 %collective-permute-start.31 = (f32[32]{0:T(128)S(1)}, f32[32]{0:T(128)S(1)}, u32[]{:S(2)}, u32[]{:S(2)}) collective-permute-start(f32[32]{0:T(128)S(1)} %collective-permute-done.30), channel_id=1, source_target_pairs={{0,4},{1,5},{2,6},{3,7},{4,0},{5,1},{6,2},{7,3},{8,12},{9,13},{10,... | collective-permute-start | bytes 392 | tf_op jit(solution)/shard_map/ppermute | solution.py:30
  241.8 7.4 %collective-permute-start.27 = (f32[1,1024]{1,0:T(1,128)S(1)}, f32[1,1024]{1,0:T(1,128)S(1)}, u32[]{:S(2)}, u32[]{:S(2)}) collective-permute-start(f32[1,1024]{1,0:T(1,128)S(1)} %get-tuple-element.32), channel_id=1, source_target_pairs={{1,0},{2,1},{3,2},{4,3},{5,4},{6,5},{7,6},{8,7},{9,8},{10,9},{11,1... | collective-permute-start | bytes 12296 | tf_op jit(solution)/shard_map/ppermute | solution.py:22
  244.1 1.3 collective-permute-start.32
  244.6 6.6 %collective-permute-start.28 = (f32[1,1024]{1,0:T(1,128)S(1)}, f32[1,1024]{1,0:T(1,128)S(1)}, u32[]{:S(2)}, u32[]{:S(2)}) collective-permute-start(f32[1,1024]{1,0:T(1,128)S(1)} %get-tuple-element.33), channel_id=1, source_target_pairs={{0,1},{1,2},{2,3},{3,4},{4,5},{5,6},{6,7},{7,8},{8,9},{9,10},{10,1... | collective-permute-start | bytes 12296 | tf_op jit(solution)/shard_map/ppermute | solution.py:20
  245.4 3.5 %collective-permute-start.33 = (f32[32]{0:T(128)S(1)}, f32[32]{0:T(128)S(1)}, u32[]{:S(2)}, u32[]{:S(2)}) collective-permute-start(f32[32]{0:T(128)S(1)} %collective-permute-done.32), channel_id=1, source_target_pairs={{0,16},{1,17},{2,18},{3,19},{4,20},{5,21},{6,22},{7,23},{8,24},{9,... | collective-permute-start | bytes 392 | tf_op jit(solution)/shard_map/ppermute | solution.py:30
where the time goes:
time: 296 us; the launch traced here: 294 us
  blocking collectives  151 us (51%)
  waiting for transfers between devices  53.6 us (18%)
  starting transfers between devices  45.3 us (15%)
  other arithmetic  14.2 us (5%)
  between operations  14 us (5%)
  local copies, waits for them, and re-layouts  12 us (4%)
  matrix products  4.17 us (1%)
    psum x4, blocking collectives, two_products(): lax.psum((jnp.sum(residual * residual), jnp.sum(residual * applied)), ('l...  151 us
    ppermute x22, waiting for transfers between devices, partner(): lax.ppermute(shard, axis, [(i, i ^ 1 << distance) for i in range(lax.axis...  37.2 us
    ppermute x22, starting transfers between devices, partner(): lax.ppermute(shard, axis, [(i, i ^ 1 << distance) for i in range(lax.axis...  29.9 us
    ppermute x6, waiting for transfers between devices, extended(): lax.ppermute(tail, axis, [(i, (i + 1) % count) for i in range(ends)])  9.59 us
    add x1, other arithmetic, per_device(): theta + ocean_block[None] * kappa[None] * (beside_all - 4.0 * masked)  7.5 us
    all_to_all x1, waiting for transfers between devices, per_device(): lax.all_to_all(summed, 'lat', split_axis=0, concat_axis=1, tiled=True)  6.8 us
    ppermute x6, starting transfers between devices, extended(): lax.ppermute(tail, axis, [(i, (i + 1) % count) for i in range(ends)])  6.78 us
  transfers between devices with their start and end apart: 35, of which 25 were waited for; matrix products, arithmetic and copies ran while one was open for 3% of the time, Pallas kernels for 0%

commit v1 on v0

v1 whole, which is shorter than its diff:
```python
import functools

import jax
import jax.numpy as jnp
from jax import lax
from jax.experimental import pallas as pl
from jax.experimental.pallas import tpu as pltpu
from jax.sharding import PartitionSpec as P

ITERS = 4
EDGE = 8
HALO = ITERS
CENTRE = 5.1
WIDTH = 4.9
VMEM = pl.BlockSpec(memory_space=pltpu.VMEM)
SMEM = pl.BlockSpec(memory_space=pltpu.SMEM)
EXACT = lax.Precision.HIGHEST
PARAMS = pltpu.CompilerParams(vmem_limit_bytes=32 * 1024 * 1024)


def iota(shape, dim):
    return lax.broadcasted_iota(jnp.int32, shape, dim)


def ones_at(hit):
    return jnp.where(hit, 1.0, 0.0).astype(jnp.float32)


def mat(a, b, precision=None):
    return jnp.dot(a, b, precision=precision, preferred_element_type=jnp.float32)


def turn(x, shift, dim):
    return pltpu.roll(x, shift % x.shape[dim] if isinstance(shift, int) else shift, dim)


def beside(v):
    return turn(v, 1, 0) + turn(v, -1, 0) + turn(v, 1, 1) + turn(v, -1, 1)


def block_mask(table, row0, rows, col0, cols, cell):
    down, across = table.shape
    pick_rows = ones_at(lax.div(row0 + iota((rows, down), 0), cell) == iota((rows, down), 1))
    pick_cols = ones_at(lax.div(col0 + iota((across, cols), 1), cell) == iota((across, cols), 0))
    return mat(mat(pick_rows, table), pick_cols)


def sum_kernel(cell, levels, idx, weight, table, theta, kappa, tt, kt, pay_a, pay_b, ns_a, ns_b, acc, edges, tops, bottoms):
    step = pl.program_id(0)
    some, cy, cx = theta.shape

    @pl.when(step == 0)
    def _():
        acc[...] = jnp.zeros_like(acc)
        edges[...] = jnp.zeros_like(edges)

    lane = iota((cy, 128), 1)
    total = acc[...]
    sides = edges[...]
    for j in range(some):
        k = step * some + j
        th = theta[j]
        total = total + weight[k] * th
        sides = jnp.where(lane == k, turn(th[:, :128], k, 1), sides)
        sides = jnp.where(lane == levels + k, turn(th[:, cx - 128 :], levels + k + 1, 1), sides)
        tops[pl.ds(k, 1), :] = th[cy - 1 :, :]
        bottoms[pl.ds(k, 1), :] = th[:1, :]
    acc[...] = total
    edges[...] = sides

    @pl.when(step == pl.num_programs(0) - 1)
    def _():
        lon, lat = idx[0], idx[1]
        mask = block_mask(table[...], lat * cy, cy, lon * cx, cx, cell)
        t = mask * acc[...]
        ttv = t.T
        ktv = kappa[...].T
        tt[...] = ttv
        kt[...] = ktv
        sidest = (edges[...] * jnp.where(lane < levels, mask[:, :1], mask[:, cx - 1 :])).T
        even = lax.rem(lon, 2) == 0
        west = (ttv[:EDGE], ktv[:EDGE], sidest[:levels])
        east = (ttv[cx - EDGE :], ktv[cx - EDGE :], sidest[levels : 2 * levels])
        at = 0
        for w, e in zip(west, east):
            rows = w.shape[0]
            pay_a[at : at + rows, :] = jnp.where(even, e, w)
            pay_b[at : at + rows, :] = jnp.where(even, w, e)
            at += rows
        flip = ones_at(iota((cx, cx), 0) + iota((cx, cx), 1) == cx - 1)
        both = jnp.concatenate([t[cy - EDGE :], kappa[cy - EDGE :, :]], axis=0)
        turned = mat(both, flip, EXACT)
        for base in (0, EDGE):
            for c in range(cx // cy):
                for r in range(EDGE):
                    row = turned[base + EDGE - 1 - r : base + EDGE - r, c * cy : (c + 1) * cy]
                    pay_a[at + r : at + r + 1, :] = row
                    pay_b[at + r : at + r + 1, :] = row
                at += EDGE
        top = tops[...] * mask[cy - 1 :, :]
        bottom = bottoms[...] * mask[:1, :]
        even_row = lax.rem(lat, 2) == 0
        ns_a[...] = jnp.where(even_row, top, bottom)
        ns_b[...] = jnp.where(even_row, bottom, top)


def forcing_kernel(levels, last, width, idx, tt, kt, got_a, got_b, tops_m, tops_a, tops_b, out, *, at_m, at_a, at_b):
    cx, cy = tt.shape
    lon, lat = idx[0], idx[1]
    even = lax.rem(lon, 2) == 0
    nt = cx // cy

    def extended(own, at, which):
        a = got_a[at : at + EDGE, :]
        b = got_b[at : at + EDGE, :]
        rows = jnp.concatenate([jnp.where(even, b, a), own, jnp.where(even, a, b)], axis=0)

        def column(ref, start, tile):
            start = start + (which * nt + tile) * EDGE
            tile_rows = ref[start : start + EDGE, :]
            return jnp.concatenate([tile_rows, jnp.zeros((cy - EDGE, cy), jnp.float32)], axis=0).T

        a_first, b_first = column(tops_a, at_a, 0), column(tops_b, at_b, 0)
        a_last, b_last = column(tops_a, at_a, nt - 1), column(tops_b, at_b, nt - 1)
        left = jnp.where(even, b_last, a_last)[cy - EDGE :]
        right = jnp.where(even, a_first, b_first)[:EDGE]
        fold = jnp.concatenate([left] + [column(tops_m, at_m, c) for c in range(nt)] + [right], axis=0)
        return jnp.concatenate([rows, jnp.where(lat == last, fold, 0.0)], axis=1)

    t = extended(tt[...], 0, 0)
    k = extended(kt[...], EDGE, 1)
    f = t + k * (beside(t) - 4.0 * t)
    rows = cx + 2 * EDGE
    lane = iota((rows, cy), 1)
    t0, k0 = t[:, :cy], k[:, :cy]
    pack = jnp.where(lane == 0, t0, 0.0)
    pack = jnp.where(lane == 1, turn(t0, 2, 1), pack)
    pack = jnp.where(lane == 2, turn(k0, 2, 1), pack)
    pack = jnp.where(lane == 3, turn(k0, 4, 1), pack)
    pack = jnp.where((lane >= 4) & (lane < 8), turn(f[:, cy:], 4, 1), pack)
    wide = -(-rows // 128) * 128
    pack = jnp.concatenate([pack, jnp.zeros((wide - rows, cy), jnp.float32)], axis=0).T[:8]
    low = iota((EDGE, cy), 0) < HALO
    for d in range(cx // width):
        at = EDGE + d * width
        out[d, :width, :] = f[at : at + width, :cy]
        out[d, width : width + EDGE, :] = jnp.where(low, f[at + width : at + width + EDGE, :cy], f[at - EDGE : at, :cy])
        out[d, width + EDGE :, :] = turn(pack, -d * width, 1)[:, :128]


def strip_order(columns, width):
    low = iota((EDGE, columns.shape[1]), 0) < HALO
    ends = jnp.where(low, columns[EDGE + width : 2 * EDGE + width], columns[:EDGE])
    return jnp.concatenate([columns[EDGE : EDGE + width], ends], axis=0)


def krylov_kernel(cell, idx, table_t, got, diag, d_right, d_left, d_fold, basis, gram):
    count, chunk, cy = got.shape
    width, full = diag.shape
    rows = width + EDGE
    x0 = (idx[0] * count + idx[1]) * width
    across, down = table_t.shape
    nx = across * cell

    edges = jnp.concatenate([got[s, rows:, :] for s in range(count)], axis=0)
    if edges.shape[0] < 128:
        edges = jnp.concatenate([edges, jnp.zeros((128 - edges.shape[0], cy), jnp.float32)], axis=0)
    edges = strip_order(edges.T, width)
    from_south = edges * turn(edges, 9, 1)
    from_north = edges * turn(edges, -5, 1)
    lane = iota((rows, cy), 1)
    parts = []
    for s in range(count):
        part = got[s, :rows, :]
        if s > 0:
            part = part + jnp.where(lane == 0, turn(from_south, -(8 * s + 2), 1), 0.0)
        if s < count - 1:
            part = part + jnp.where(lane == cy - 1, turn(from_north, cy - 1 - (8 * s + 3), 1), 0.0)
        parts.append(part)
    parts.append(jnp.where(lane < HALO, turn(edges, -(8 * (count - 1) + 4), 1), 0.0))
    f = jnp.concatenate(parts, axis=1)

    place = iota((rows, across), 0)
    x = x0 + jnp.where(place < width + HALO, place, place - rows)
    x = jnp.where(x < 0, x + nx, jnp.where(x >= nx, x - nx, x))
    cells = iota((rows, across), 1)
    here = ones_at(lax.div(x, cell) == cells)
    there = ones_at(lax.div(nx - 1 - x, cell) == cells)
    up = ones_at(lax.div(iota((down, full), 1), cell) == iota((down, full), 0))
    above = ones_at((iota((down, cy), 0) == down - 1) & (iota((down, cy), 1) < HALO))
    t = table_t[...]
    mask = jnp.concatenate([mat(mat(here, t), up), mat(mat(there, t), above)], axis=1)

    low = iota((EDGE, full), 0) < HALO
    d_main = jnp.concatenate([diag[...], jnp.where(low, d_right[:, :full], d_left[:, :full])], axis=0)
    folds = jnp.concatenate([d_fold[...], d_right[:, full:], d_left[:, full:], jnp.zeros((128 - 3 * EDGE, 128), jnp.float32)], axis=0).T
    halo_low = iota((EDGE, 128), 0) < HALO
    d_ends = jnp.where(halo_low, turn(folds[:EDGE], -EDGE, 1), turn(folds[width - EDGE : width], -2 * EDGE, 1))
    d_all = jnp.concatenate([d_main, jnp.concatenate([folds[:width], d_ends], axis=0)], axis=1)

    near = mask * (1.0 / WIDTH)
    centre = near * ((4.0 - CENTRE) + jnp.where(mask > 0.0, d_all, 0.0))
    p = [mask * f]
    p.append(centre * p[0] - near * beside(p[0]))
    for j in range(2, ITERS + 1):
        p.append(2.0 * (centre * p[j - 1] - near * beside(p[j - 1])) - p[j - 2])
    for j in range(ITERS):
        basis[j] = p[j][:width, :full]
    sums = []
    for i in range(ITERS):
        for j in range(i, ITERS + 1):
            both = p[i][:width, :full] * p[j][:width, :full]
            both = sum(both[:, c : c + 128] for c in range(0, full, 128))
            sums.append(jnp.sum(both, axis=0, keepdims=True))
    sums = jnp.concatenate(sums + [jnp.zeros((128 - len(sums), 128), jnp.float32)], axis=0)
    gram[...] = jnp.broadcast_to(jnp.sum(sums.T, axis=0, keepdims=True), gram.shape)


def combine_kernel(gram, basis, psi):
    g = jnp.sum(gram[...], axis=0, keepdims=True)
    at = {}
    n = 0
    for i in range(ITERS):
        for j in range(i, ITERS + 1):
            at[i, j] = at[j, i] = g[:, n : n + 1]
            n += 1

    def applied(i, j):
        if j == 0:
            return CENTRE * at[i, 0] + WIDTH * at[i, 1]
        return CENTRE * at[i, j] + (0.5 * WIDTH) * (at[i, j + 1] + at[i, j - 1])

    low = {}
    pivot = []
    right = []
    for i in range(ITERS):
        row = []
        for j in range(i):
            value = applied(j, i)
            for k in range(j):
                value = value - row[k] * low[j, k]
            row.append(value)
            low[i, j] = value / pivot[j]
        value = applied(i, i)
        for k in range(i):
            value = value - row[k] * low[i, k]
        pivot.append(value)
        value = at[i, 0]
        for k in range(i):
            value = value - low[i, k] * right[k]
        right.append(value)
    c = [None] * ITERS
    for i in reversed(range(ITERS)):
        value = right[i] / pivot[i]
        for k in range(i + 1, ITERS):
            value = value - low[k, i] * c[k]
        c[i] = value
    total = c[0] * basis[0]
    for j in range(1, ITERS):
        total = total + c[j] * basis[j]
    psi[...] = total


def tracer_kernel(cell, levels, last, idx, table, theta, kappa, got_a, got_b, rows_a, rows_b, out, mask, coef, sides, north, south):
    step = pl.program_id(0)
    some, cy, cx = theta.shape
    lon, lat = idx[0], idx[1]

    @pl.when(step == 0)
    def _():
        ocean = block_mask(table[...], lat * cy, cy, lon * cx, cx, cell)
        mask[...] = ocean
        coef[...] = ocean * kappa[...]
        even = lax.rem(lon, 2) == 0
        a, b = got_a[2 * EDGE : 2 * EDGE + levels, :], got_b[2 * EDGE : 2 * EDGE + levels, :]
        both = jnp.concatenate([jnp.where(even, a, b), jnp.where(even, b, a), jnp.zeros((128 - 2 * levels, cy), jnp.float32)], axis=0)
        sides[...] = both.T
        even_row = lax.rem(lat, 2) == 0
        up = jnp.where(even_row, rows_a[...], rows_b[...])
        flip = ones_at(iota((cx, cx), 0) + iota((cx, cx), 1) == cx - 1)
        north[...] = jnp.where(lat == last, mat(up, flip, EXACT), up)
        south[...] = jnp.where(even_row, rows_b[...], rows_a[...])

    lane = iota((cy, cx), 1)
    row = iota((cy, cx), 0)
    spare = jnp.zeros((cy, cx - 128), jnp.float32)
    for j in range(some):
        k = step * some + j
        th = theta[j]
        m = mask[...] * th
        col = sides[...]
        from_east = jnp.concatenate([spare, turn(col, 127 - k, 1)], axis=1)
        from_west = jnp.concatenate([turn(col, 128 - levels - k, 1), spare], axis=1)
        east = jnp.where(lane == cx - 1, from_east, turn(m, -1, 1))
        west = jnp.where(lane == 0, from_west, turn(m, 1, 1))
        above = jnp.where(row == cy - 1, north[pl.ds(k, 1), :], turn(m, -1, 0))
        below = jnp.where(row == 0, south[pl.ds(k, 1), :], turn(m, 1, 0))
        out[j] = th + coef[...] * (east + west + above + below - 4.0 * m)


def per_device(theta, kappa, layer_weight, diag, land_blocks):
    lons, lats = lax.axis_size("lon"), lax.axis_size("lat")
    joint = ("lon", "lat")
    devices = lons * lats
    levels, cy, cx = theta.shape
    width, full = diag.shape
    cell = full // land_blocks.shape[0]
    last = lats - 1
    f32 = jnp.float32
    shape = lambda *dims: jax.ShapeDtypeStruct(dims, f32)
    idx = jnp.stack([lax.axis_index("lon"), lax.axis_index("lat")]).astype(jnp.int32)
    table = land_blocks.astype(f32)

    corner = diag[:, full - EDGE :][::-1, ::-1].T
    corner = jnp.pad(corner, ((0, 0), (0, 128 - width)))
    d_fold = lax.ppermute(corner, joint, [(i, devices - 1 - i) for i in range(devices)])
    d_east = jnp.concatenate([diag[width - EDGE :], d_fold], axis=1)
    d_west = jnp.concatenate([diag[:EDGE], d_fold], axis=1)
    d_left = lax.ppermute(d_east, joint, [(i, (i + 1) % devices) for i in range(devices)])
    d_right = lax.ppermute(d_west, joint, [((i + 1) % devices, i) for i in range(devices)])

    some = 4
    nt = cx // cy
    head = 2 * EDGE + levels
    own = 2 * nt * EDGE
    block = pl.BlockSpec((some, cy, cx), lambda s: (s, 0, 0))
    tt, kt, pay_a, pay_b, ns_a, ns_b = pl.pallas_call(
        functools.partial(sum_kernel, cell, levels),
        grid=(levels // some,),
        in_specs=[SMEM, SMEM, VMEM, block, VMEM],
        out_specs=[VMEM] * 6,
        out_shape=[shape(cx, cy), shape(cx, cy), shape(head + own, cy), shape(head + own, cy), shape(levels, cx), shape(levels, cx)],
        scratch_shapes=[pltpu.VMEM((cy, cx), f32), pltpu.VMEM((cy, 128), f32), pltpu.VMEM((levels, cx), f32), pltpu.VMEM((levels, cx), f32)],
        compiler_params=PARAMS,
        name="level_sum",
    )(idx, layer_weight, table, theta, kappa)

    pairs_b = [(i, (i + 1) % lons if i % 2 else (i - 1) % lons) for i in range(lons)]
    mirror = [(i, lons - 1 - i) for i in range(lons)]
    got_a = lax.ppermute(pay_a, "lon", [(i, i ^ 1) for i in range(lons)])
    if pairs_b == mirror:
        got_b = lax.ppermute(jnp.concatenate([pay_b, got_a[head:]], axis=0), "lon", pairs_b)
        folds = (got_b, got_b, pay_b)
        places = dict(at_m=head, at_a=head + own, at_b=head)
    else:
        got_b = lax.ppermute(pay_b, "lon", pairs_b)
        got_m = lax.ppermute(jnp.concatenate([pay_b[head:], got_a[head:], got_b[head:]], axis=0), "lon", mirror)
        folds = (got_m, got_m, got_m)
        places = dict(at_m=0, at_a=own, at_b=2 * own)
    chunks = pl.pallas_call(
        functools.partial(forcing_kernel, levels, last, width, **places),
        in_specs=[SMEM] + [VMEM] * 7,
        out_specs=VMEM,
        out_shape=shape(lats, width + 2 * EDGE, cy),
        compiler_params=PARAMS,
        name="forcing",
    )(idx, tt, kt, got_a, got_b, *folds)
    got = lax.all_to_all(chunks, "lat", split_axis=0, concat_axis=0, tiled=True)

    def flat(lon, lat):
        return lon * lats + lat

    first, second = [], []
    for lon in range(lons):
        for lat in range(lats):
            first.append((flat(lon, lat), flat(lon, lat ^ 1)))
            to = lat + 1 if lat % 2 else lat - 1
            if to == lats:
                second.append((flat(lon, lat), flat(lons - 1 - lon, lat)))
            elif to >= 0:
                second.append((flat(lon, lat), flat(lon, to)))
    rows_a = lax.ppermute(ns_a, joint, first)
    rows_b = lax.ppermute(ns_b, joint, second)
    new_theta = pl.pallas_call(
        functools.partial(tracer_kernel, cell, levels, last),
        grid=(levels // some,),
        in_specs=[SMEM, VMEM, block] + [VMEM] * 5,
        out_specs=block,
        out_shape=shape(levels, cy, cx),
        scratch_shapes=[pltpu.VMEM((cy, cx), f32), pltpu.VMEM((cy, cx), f32), pltpu.VMEM((cy, 128), f32), pltpu.VMEM((levels, cx), f32), pltpu.VMEM((levels, cx), f32)],
        compiler_params=PARAMS,
        cost_estimate=pl.CostEstimate(flops=12 * levels * cy * cx, bytes_accessed=8 * levels * cy * cx, transcendentals=0),
        name="tracer",
    )(idx, table, theta, kappa, got_a, got_b, rows_a, rows_b)

    basis, gram = pl.pallas_call(
        functools.partial(krylov_kernel, cell),
        in_specs=[SMEM] + [VMEM] * 6,
        out_specs=[VMEM, VMEM],
        out_shape=[shape(ITERS, width, full), shape(devices, 128)],
        compiler_params=PARAMS,
        name="krylov",
    )(idx, table.T, got, diag, d_right, d_left, d_fold)
    gram = lax.all_to_all(gram, joint, split_axis=0, concat_axis=0, tiled=True)
    psi = pl.pallas_call(
        combine_kernel,
        in_specs=[VMEM, VMEM],
        out_specs=VMEM,
        out_shape=shape(width, full),
        compiler_params=PARAMS,
        name="combine",
    )(gram, basis)
    return new_theta, psi


def solution(mesh):
    return jax.shard_map(
        per_device,
        mesh=mesh,
        in_specs=(P(None, "lat", "lon"), P("lat", "lon"), P(), P(("lon", "lat"), None), P()),
        out_specs=(P(None, "lat", "lon"), P(("lon", "lat"), None)),
        check_vma=False,
    )
```

time: 296 us -> 48.9 us (0.17)
  the two profiles are of different devices: /device:TPU:0 before, /device:TPU:8 now
where the time goes in v1:
time: 48.9 us; the launch traced here: 48.6 us
  starting transfers between devices  22.4 us (46%)
  Pallas kernels  11.8 us (24%)
  waiting for transfers between devices  9.34 us (19%)
  local copies, waits for them, and re-layouts  4.3 us (9%)
  between operations  0.71 us (1%)
    all_to_all x1, starting transfers between devices, per_device(): got = lax.all_to_all(chunks, 'lat', split_axis=0, concat_axis=0, tiled=True)  6.06 us
    all_to_all x1, starting transfers between devices, per_device(): gram = lax.all_to_all(gram, joint, split_axis=0, concat_axis=0, tiled=True)  5.8 us
    ppermute x1, waiting for transfers between devices, per_device(): rows_b = lax.ppermute(ns_b, joint, second)  4.24 us
    pallas_call x1, Pallas kernels, per_device(): pl.pallas_call(functools.partial(tracer_kernel, cell, levels, last), grid...  4.15 us
    unnamed x14, local copies, waits for them, and re-layouts  4.06 us
    ppermute x1, waiting for transfers between devices, per_device(): lax.ppermute(d_east, joint, [(i, (i + 1) % devices) for i in range(device...  3.11 us
    ppermute x1, starting transfers between devices, per_device(): lax.ppermute(corner, joint, [(i, devices - 1 - i) for i in range(devices)])  2.49 us
    pallas_call x1, Pallas kernels, per_device(): pl.pallas_call(functools.partial(krylov_kernel, cell), in_specs=[SMEM] +...  2.16 us
  transfers between devices with their start and end apart: 9, of which 6 were waited for; matrix products, arithmetic and copies ran while one was open for 0% of the time, Pallas kernels for 12%

profile of v1, /device:TPU:8, one launch (start us, length us, event | category | flops | bytes accessed | tf_op | source)
XLA Modules:
  0.0 48.6 jit_solution(4324048592424117847)
XLA Ops:
  0.6 0.0 copy-start.4
  0.6 0.8 %copy.11 = s32[32,32]{0,1:T(8,128)S(1)} copy(s32[32,32]{1,0:T(8,128)} %param.9) | data formatting | bytes 8192 | tf_op args[4]
  1.5 0.1 copy.13.table
  1.5 0.1 pad_add_fusion.idx
  1.6 0.0 copy-start
  1.6 1.6 %copy-done = f32[16,128,256]{2,1,0:T(8,128)S(1)} copy-done((f32[16,128,256]{2,1,0:T(8,128)S(1)}, f32[16,128,256]{2,1,0:T(8,128)}, u32[]{:S(2)}) %copy-start) | copy-done | bytes 2097176
  3.2 0.0 copy-start.2
  3.2 0.9 %copy-done.2 = f32[128,256]{1,0:T(8,128)S(1)} copy-done((f32[128,256]{1,0:T(8,128)S(1)}, f32[128,256]{1,0:T(8,128)}, u32[]{:S(2)}) %copy-start.2) | copy-done | bytes 131096
  4.1 0.0 copy-start.5
  4.1 0.7 %copy-done.5 = f32[16]{0:T(128)S(1)} copy-done((f32[16]{0:T(128)S(1)}, f32[16]{0:T(128)}, u32[]{:S(2)}) %copy-start.5) | copy-done | bytes 88
  4.8 0.0 copy-start.1
  4.8 0.0 copy-start.3
  4.8 1.9 %level_sum.1 = (f32[256,128]{1,0:T(8,128)S(1)}, f32[256,128]{1,0:T(8,128)S(1)}, f32[64,128]{1,0:T(8,128)S(1)}, f32[64,128]{1,0:T(8,128)S(1)}, f32[16,256]{1,0:T(8,128)S(1)}, /*index=5*/f32[16,256]{1,0:T(8,128)S(1)}) custom-call(s32[2]{0:T(128)S(1)} %pad_add_fusion.idx, f32[16]{0:T(128)S(1)} %copy-done.5, f32[32,32]{1,0:T(8,128)S(1)} %copy.13.table, ...), custom_call_target="tpu_custom_call" | custom-call | tf_op jit(solution)/shard_map/level_sum/pallas_call | solution.py:327
  6.7 0.1 collective-permute-start
  6.8 1.2 %collective-permute-done.got_a = f32[64,128]{1,0:T(8,128)S(1)} collective-permute-done((f32[64,128]{1,0:T(8,128)S(1)}, f32[64,128]{1,0:T(8,128)S(1)}, u32[]{:S(2)}, u32[]{:S(2)}) %collective-permute-start) | collective-permute-done | bytes 32800 | tf_op jit(solution)/shard_map/ppermute | solution.py:340
  8.0 1.3 %collective-permute-start.1 = (f32[96,128]{1,0:T(8,128)S(1)}, f32[96,128]{1,0:T(8,128)S(1)}, u32[]{:S(2)}, u32[]{:S(2)}) collective-permute-start(f32[96,128]{1,0:T(8,128)S(1)} %pad_maximum_fusion.2), channel_id=1, source_target_pairs={{0,24},{8,16},{16,8},{24,0},{1,25},{9,17},{17,9},{25,1},{2,26},{10... | collective-permute-start | bytes 147464 | tf_op jit(solution)/shard_map/ppermute | solution.py:342
  9.3 0.0 copy-done.4
  9.3 0.1 slice.14
  9.4 0.1 copy.16
  9.4 0.1 rev.3
  9.5 2.5 %collective-permute-start.4 = (f32[8,128]{1,0:T(8,128)S(1)}, f32[8,128]{1,0:T(8,128)S(1)}, u32[]{:S(2)}, u32[]{:S(2)}) collective-permute-start(f32[8,128]{1,0:T(8,128)S(1)} %pad.4), channel_id=1, source_target_pairs={{0,31},{1,30},{2,29},{3,28},{4,27},{5,26},{6,25},{7,24},{8,23},{9,... | collective-permute-start | bytes 12296 | tf_op jit(solution)/shard_map/ppermute | solution.py:316
  12.0 0.0 collective-permute-done.1.got_b.tops_m.tops_a
  12.0 1.9 %forcing.1 = f32[8,48,128]{2,1,0:T(8,128)} custom-call(s32[2]{0:T(128)S(1)} %pad_add_fusion.idx, f32[256,128]{1,0:T(8,128)S(1)} %get-tuple-element.14.tt, f32[256,128]{1,0:T(8,128)S(1)} %get-tuple-element.15.kt, f32[64,128]{1,0:T(8,128)S(1)} %collective-permute-done.got_a, f32[96,128]{1,0:T(8,128)S(1)} %collective-permute-done.1.got_b.tops_m.tops_a, ...), custom_call_target="tpu_custom_call" | custom-call | tf_op jit(solution)/shard_map/forcing/pallas_call | solution.py:350
  13.9 6.1 %all-to-all-start = ((f32[8,48,128]{2,1,0:T(8,128)}), f32[8,48,128]{2,1,0:T(8,128)S(1)}, u32[]{:S(2)}, u32[]{:S(2)}) async-start(f32[8,48,128]{2,1,0:T(8,128)} %forcing.1), calls=%async_computation | async-start | bytes 393216 | tf_op jit(solution)/shard_map/all_to_all | solution.py:358
  20.0 0.0 collective-permute-done.4.d_fold
  20.0 1.5 %collective-permute-start.6 = (f32[8,1152]{1,0:T(8,128)S(1)}, f32[8,1152]{1,0:T(8,128)S(1)}, u32[]{:S(2)}, u32[]{:S(2)}) collective-permute-start(f32[8,1152]{1,0:T(8,128)S(1)} %get-tuple-element.22), channel_id=1, source_target_pairs={{0,1},{1,2},{2,3},{3,4},{4,5},{5,6},{6,7},{7,8},{8,9},{9,10},{10,1... | collective-permute-start | bytes 110600 | tf_op jit(solution)/shard_map/ppermute | solution.py:319
  21.5 1.5 %collective-permute-start.5 = (f32[8,1152]{1,0:T(8,128)S(1)}, f32[8,1152]{1,0:T(8,128)S(1)}, u32[]{:S(2)}, u32[]{:S(2)}) collective-permute-start(f32[8,1152]{1,0:T(8,128)S(1)} %get-tuple-element.23), channel_id=1, source_target_pairs={{1,0},{2,1},{3,2},{4,3},{5,4},{6,5},{7,6},{8,7},{9,8},{10,9},{11,1... | collective-permute-start | bytes 110600 | tf_op jit(solution)/shard_map/ppermute | solution.py:320
  23.0 3.1 %collective-permute-done.6.d_left = f32[8,1152]{1,0:T(8,128)S(1)} collective-permute-done((f32[8,1152]{1,0:T(8,128)S(1)}, f32[8,1152]{1,0:T(8,128)S(1)}, u32[]{:S(2)}, u32[]{:S(2)}) %collective-permute-start.6) | collective-permute-done | bytes 36896 | tf_op jit(solution)/shard_map/ppermute | solution.py:319
  26.1 0.4 collective-permute-done.5.d_right
  26.5 0.3 all-to-all-done.got
  26.7 2.2 %krylov.1 = (f32[4,32,1024]{2,1,0:T(8,128)S(1)}, f32[32,128]{1,0:T(8,128)}) custom-call(s32[2]{0:T(128)S(1)} %pad_add_fusion.idx, f32[32,32]{1,0:T(8,128)S(1)} %get-tuple-element.20.table_t, f32[8,48,128]{2,1,0:T(8,128)S(1)} %all-to-all-done.got, f32[32,1024]{1,0:T(8,128)S(1)} %copy-done.4, f32[8,1152]{1,0:T(8,128)S(1)} %collective-permute-done.5.d_right, ...), custom_call_target="tpu_custom_call" | custom-call | tf_op jit(solution)/shard_map/krylov/pallas_call | solution.py:386
  28.9 5.8 %all-to-all-start.1 = ((f32[32,1,128]{2,1,0:T(1,128)}), f32[32,1,128]{2,1,0:T(1,128)S(1)}, u32[]{:S(2)}, u32[]{:S(2)}) async-start(f32[32,1,128]{2,1,0:T(1,128)} %bitcast.5), calls=%async_computation.1 | async-start | bytes 32768 | tf_op jit(solution)/shard_map/all_to_all | solution.py:394
  34.7 1.5 %collective-permute-start.2 = (f32[16,256]{1,0:T(8,128)S(1)}, f32[16,256]{1,0:T(8,128)S(1)}, u32[]{:S(2)}, u32[]{:S(2)}) collective-permute-start(f32[16,256]{1,0:T(8,128)S(1)} %get-tuple-element.12), channel_id=1, source_target_pairs={{0,1},{1,0},{2,3},{3,2},{4,5},{5,4},{6,7},{7,6},{8,9},{9,8},{10,11... | collective-permute-start | bytes 49160 | tf_op jit(solution)/shard_map/ppermute | solution.py:372
  36.2 2.1 %collective-permute-start.3 = (f32[16,256]{1,0:T(8,128)S(1)}, f32[16,256]{1,0:T(8,128)S(1)}, u32[]{:S(2)}, u32[]{:S(2)}) collective-permute-start(f32[16,256]{1,0:T(8,128)S(1)} %get-tuple-element.13), channel_id=1, source_target_pairs={{1,2},{2,1},{3,4},{4,3},{5,6},{6,5},{7,31},{9,10},{10,9},{11,12},{... | collective-permute-start | bytes 49160 | tf_op jit(solution)/shard_map/ppermute | solution.py:373
  38.4 0.1 collective-permute-done.2.rows_a
  38.5 4.2 %collective-permute-done.3.rows_b = f32[16,256]{1,0:T(8,128)S(1)} collective-permute-done((f32[16,256]{1,0:T(8,128)S(1)}, f32[16,256]{1,0:T(8,128)S(1)}, u32[]{:S(2)}, u32[]{:S(2)}) %collective-permute-start.3) | collective-permute-done | bytes 16416 | tf_op jit(solution)/shard_map/ppermute | solution.py:373
  42.8 0.0 copy-done.1
  42.8 0.0 copy-done.3
  42.8 4.1 %tracer.1 = f32[16,128,256]{2,1,0:T(8,128)} custom-call(s32[2]{0:T(128)S(1)} %pad_add_fusion.idx, f32[32,32]{1,0:T(8,128)S(1)} %copy.13.table, f32[16,128,256]{2,1,0:T(8,128)S(1)} %copy-done.1, f32[128,256]{1,0:T(8,128)S(1)} %copy-done.3, f32[64,128]{1,0:T(8,128)S(1)} %collective-permute-done.got_a, ...), custom_call_target="tpu_custom_call" | custom-call | flops 6291456 | bytes 4194304 | tf_op jit(solution)/shard_map/tracer/pallas_call | solution.py:374
  46.9 0.0 all-to-all-done.1
  46.9 1.7 %combine.1 = f32[32,1024]{1,0:T(8,128)} custom-call(f32[32,128]{1,0:T(8,128)S(1)} %bitcast.9, f32[4,32,1024]{2,1,0:T(8,128)S(1)} %get-tuple-element.17.basis), custom_call_target="tpu_custom_call" | custom-call | tf_op jit(solution)/shard_map/combine/pallas_call | solution.py:395
  (6 shorter events, 0.0 us)
Async XLA Ops:
  0.6 8.7 %copy-start.4 = (f32[32,1024]{1,0:T(8,128)S(1)}, f32[32,1024]{1,0:T(8,128)}, u32[]{:S(2)}) copy-start(f32[32,1024]{1,0:T(8,128)} %diag.1) | copy-start | bytes 393220
  1.6 1.6 %copy-start = (f32[16,128,256]{2,1,0:T(8,128)S(1)}, f32[16,128,256]{2,1,0:T(8,128)}, u32[]{:S(2)}) copy-start(f32[16,128,256]{2,1,0:T(8,128)} %theta.3) | copy-start | bytes 6291460
  3.2 0.9 %copy-start.2 = (f32[128,256]{1,0:T(8,128)S(1)}, f32[128,256]{1,0:T(8,128)}, u32[]{:S(2)}) copy-start(f32[128,256]{1,0:T(8,128)} %kappa.3) | copy-start | bytes 393220
  4.1 0.7 %copy-start.5 = (f32[16]{0:T(128)S(1)}, f32[16]{0:T(128)}, u32[]{:S(2)}) copy-start(f32[16]{0:T(128)} %weight.1) | copy-start | bytes 196
  4.8 38.0 %copy-start.1 = (f32[16,128,256]{2,1,0:T(8,128)S(1)}, f32[16,128,256]{2,1,0:T(8,128)}, u32[]{:S(2)}) copy-start(f32[16,128,256]{2,1,0:T(8,128)} %theta.3) | copy-start | bytes 6291460
  4.8 38.0 %copy-start.3 = (f32[128,256]{1,0:T(8,128)S(1)}, f32[128,256]{1,0:T(8,128)}, u32[]{:S(2)}) copy-start(f32[128,256]{1,0:T(8,128)} %kappa.3) | copy-start | bytes 393220
  6.7 1.3 %collective-permute-start = (f32[64,128]{1,0:T(8,128)S(1)}, f32[64,128]{1,0:T(8,128)S(1)}, u32[]{:S(2)}, u32[]{:S(2)}) collective-permute-start(f32[64,128]{1,0:T(8,128)S(1)} %get-tuple-element.10), channel_id=1, source_target_pairs={{0,8},{8,0},{16,24},{24,16},{1,9},{9,1},{17,25},{25,17},{2,10},{10... | collective-permute-start | bytes 98312 | tf_op jit(solution)/shard_map/ppermute | solution.py:340
  8.0 4.0 %collective-permute-start.1 = (f32[96,128]{1,0:T(8,128)S(1)}, f32[96,128]{1,0:T(8,128)S(1)}, u32[]{:S(2)}, u32[]{:S(2)}) collective-permute-start(f32[96,128]{1,0:T(8,128)S(1)} %pad_maximum_fusion.2), channel_id=1, source_target_pairs={{0,24},{8,16},{16,8},{24,0},{1,25},{9,17},{17,9},{25,1},{2,26},{10... | collective-permute-start | bytes 147464 | tf_op jit(solution)/shard_map/ppermute | solution.py:342
  9.5 10.4 %collective-permute-start.4 = (f32[8,128]{1,0:T(8,128)S(1)}, f32[8,128]{1,0:T(8,128)S(1)}, u32[]{:S(2)}, u32[]{:S(2)}) collective-permute-start(f32[8,128]{1,0:T(8,128)S(1)} %pad.4), channel_id=1, source_target_pairs={{0,31},{1,30},{2,29},{3,28},{4,27},{5,26},{6,25},{7,24},{8,23},{9,... | collective-permute-start | bytes 12296 | tf_op jit(solution)/shard_map/ppermute | solution.py:316
  13.9 12.8 %all-to-all-start = ((f32[8,48,128]{2,1,0:T(8,128)}), f32[8,48,128]{2,1,0:T(8,128)S(1)}, u32[]{:S(2)}, u32[]{:S(2)}) async-start(f32[8,48,128]{2,1,0:T(8,128)} %forcing.1), calls=%async_computation | async-start | bytes 393216 | tf_op jit(solution)/shard_map/all_to_all | solution.py:358
  20.0 6.1 %collective-permute-start.6 = (f32[8,1152]{1,0:T(8,128)S(1)}, f32[8,1152]{1,0:T(8,128)S(1)}, u32[]{:S(2)}, u32[]{:S(2)}) collective-permute-start(f32[8,1152]{1,0:T(8,128)S(1)} %get-tuple-element.22), channel_id=1, source_target_pairs={{0,1},{1,2},{2,3},{3,4},{4,5},{5,6},{6,7},{7,8},{8,9},{9,10},{10,1... | collective-permute-start | bytes 110600 | tf_op jit(solution)/shard_map/ppermute | solution.py:319
  21.5 4.9 %collective-permute-start.5 = (f32[8,1152]{1,0:T(8,128)S(1)}, f32[8,1152]{1,0:T(8,128)S(1)}, u32[]{:S(2)}, u32[]{:S(2)}) collective-permute-start(f32[8,1152]{1,0:T(8,128)S(1)} %get-tuple-element.23), channel_id=1, source_target_pairs={{1,0},{2,1},{3,2},{4,3},{5,4},{6,5},{7,6},{8,7},{9,8},{10,9},{11,1... | collective-permute-start | bytes 110600 | tf_op jit(solution)/shard_map/ppermute | solution.py:320
  28.9 18.0 %all-to-all-start.1 = ((f32[32,1,128]{2,1,0:T(1,128)}), f32[32,1,128]{2,1,0:T(1,128)S(1)}, u32[]{:S(2)}, u32[]{:S(2)}) async-start(f32[32,1,128]{2,1,0:T(1,128)} %bitcast.5), calls=%async_computation.1 | async-start | bytes 32768 | tf_op jit(solution)/shard_map/all_to_all | solution.py:394
  34.7 3.8 %collective-permute-start.2 = (f32[16,256]{1,0:T(8,128)S(1)}, f32[16,256]{1,0:T(8,128)S(1)}, u32[]{:S(2)}, u32[]{:S(2)}) collective-permute-start(f32[16,256]{1,0:T(8,128)S(1)} %get-tuple-element.12), channel_id=1, source_target_pairs={{0,1},{1,0},{2,3},{3,2},{4,5},{5,4},{6,7},{7,6},{8,9},{9,8},{10,11... | collective-permute-start | bytes 49160 | tf_op jit(solution)/shard_map/ppermute | solution.py:372
  36.2 6.5 %collective-permute-start.3 = (f32[16,256]{1,0:T(8,128)S(1)}, f32[16,256]{1,0:T(8,128)S(1)}, u32[]{:S(2)}, u32[]{:S(2)}) collective-permute-start(f32[16,256]{1,0:T(8,128)S(1)} %get-tuple-element.13), channel_id=1, source_target_pairs={{1,2},{2,1},{3,4},{4,3},{5,6},{6,5},{7,31},{9,10},{10,9},{11,12},{... | collective-permute-start | bytes 49160 | tf_op jit(solution)/shard_map/ppermute | solution.py:373

commit v2 on v1

v2 whole, which is shorter than its diff:
```python
import functools

import jax
import jax.numpy as jnp
from jax import lax
from jax.experimental import pallas as pl
from jax.experimental.pallas import tpu as pltpu
from jax.sharding import PartitionSpec as P

ITERS = 4
EDGE = 8
HALO = ITERS
RIM = HALO - 1
CENTRE = 5.1
WIDTH = 4.9
VMEM = pl.BlockSpec(memory_space=pltpu.VMEM)
SMEM = pl.BlockSpec(memory_space=pltpu.SMEM)
HBM = pl.BlockSpec(memory_space=pltpu.HBM)
EXACT = lax.Precision.HIGHEST
PARAMS = pltpu.CompilerParams(vmem_limit_bytes=32 * 1024 * 1024)


def in_hbm(x):
    return pltpu.with_memory_space_constraint(x, pltpu.HBM)


def iota(shape, dim):
    return lax.broadcasted_iota(jnp.int32, shape, dim)


def ones_at(hit):
    return jnp.where(hit, 1.0, 0.0).astype(jnp.float32)


def mat(a, b, precision=None):
    return jnp.dot(a, b, precision=precision, preferred_element_type=jnp.float32)


def turn(x, shift, dim):
    return pltpu.roll(x, shift % x.shape[dim] if isinstance(shift, int) else shift, dim)


def beside(v):
    return turn(v, 1, 0) + turn(v, -1, 0) + turn(v, 1, 1) + turn(v, -1, 1)


def block_mask(table, row0, rows, col0, cols, cell):
    down, across = table.shape
    pick_rows = ones_at(lax.div(row0 + iota((rows, down), 0), cell) == iota((rows, down), 1))
    pick_cols = ones_at(lax.div(col0 + iota((across, cols), 1), cell) == iota((across, cols), 0))
    return mat(mat(pick_rows, table), pick_cols)


def sum_kernel(cell, weight_hbm, table_hbm, theta_hbm, kappa_hbm, diag_hbm, theta, ocean, coef, tt, kt, pay_a, pay_b, row_a, row_b, kappa, corner, rim, table, weight, sems):
    levels, cy, cx = theta.shape
    width, full = diag_hbm.shape
    copies = [
        pltpu.make_async_copy(table_hbm, table, sems.at[0]),
        pltpu.make_async_copy(weight_hbm, weight, sems.at[1]),
        pltpu.make_async_copy(kappa_hbm, kappa, sems.at[2]),
        pltpu.make_async_copy(diag_hbm.at[:, pl.ds(full - 128, 128)], corner, sems.at[3]),
        pltpu.make_async_copy(diag_hbm.at[pl.ds(0, EDGE)], rim.at[0], sems.at[4]),
        pltpu.make_async_copy(diag_hbm.at[pl.ds(width - EDGE, EDGE)], rim.at[1], sems.at[5]),
    ]
    pieces = 4
    some = levels // pieces
    for n in range(pieces):
        copies.append(pltpu.make_async_copy(theta_hbm.at[pl.ds(n * some, some)], theta.at[pl.ds(n * some, some)], sems.at[6 + n]))
    for copy in copies:
        copy.start()
    lon, lat = lax.axis_index("lon"), lax.axis_index("lat")
    even = lax.rem(lon, 2) == 0
    even_row = lax.rem(lat, 2) == 0
    copies[0].wait()
    mask = block_mask(table[...].astype(jnp.float32), lat * cy, cy, lon * cx, cx, cell)
    copies[3].wait()
    column = jnp.concatenate([corner[...], jnp.zeros((128 - width, 128), jnp.float32)], axis=0).T
    column = turn(column[128 - EDGE :], lon * width, 1)
    copies[4].wait()
    copies[5].wait()
    at = cx // cy * levels
    for c in range(full // cy):
        w = rim[0, :RIM, c * cy : (c + 1) * cy]
        e = rim[1, EDGE - RIM :, c * cy : (c + 1) * cy]
        row_a[at : at + RIM, :] = jnp.where(even_row, e, w)
        row_b[at : at + RIM, :] = jnp.where(even_row, w, e)
        at += RIM
    copies[2].wait()
    kappas = kappa[...]
    ocean[...] = mask
    coef[...] = mask * kappas
    ktv = kappas.T
    kt[...] = ktv

    lane = iota((cy, 128), 1)
    total = jnp.zeros((cy, cx), jnp.float32)
    sides = jnp.zeros((cy, 128), jnp.float32)
    copies[1].wait()
    for n in range(pieces):
        copies[6 + n].wait()
        for k in range(n * some, n * some + some):
            th = theta[k]
            total = total + weight[k] * th
            sides = jnp.where(lane == k, turn(th[:, :128], k, 1), sides)
            sides = jnp.where(lane == levels + k, turn(th[:, cx - 128 :], levels + k + 1, 1), sides)
    t = mask * total
    ttv = t.T
    tt[...] = ttv
    sidest = (sides * jnp.where(lane < levels, mask[:, :1], mask[:, cx - 1 :])).T
    west = (ttv[:EDGE], ktv[:EDGE], sidest[:levels])
    east = (ttv[cx - EDGE :], ktv[cx - EDGE :], sidest[levels : 2 * levels])
    at = 0
    for w, e in zip(west, east):
        rows = w.shape[0]
        pay_a[at : at + rows, :] = jnp.where(even, e, w)
        pay_b[at : at + rows, :] = jnp.where(even, w, e)
        at += rows
    flip = ones_at(iota((cx, cx), 0) + iota((cx, cx), 1) == cx - 1)
    both = jnp.concatenate([t[cy - EDGE :], kappas[cy - EDGE :, :]], axis=0)
    turned = mat(both, flip, EXACT)
    nt = cx // cy
    for base, to in ((0, at), (EDGE, at + EDGE)):
        for r in range(EDGE):
            row = turned[base + EDGE - 1 - r : base + EDGE - r]
            pay_a[to + r : to + r + 1, :] = jnp.where(even, row[:, :cy], row[:, cx - cy :])
            for c in range(nt):
                to_b = at + (base // EDGE * nt + c) * EDGE + r
                pay_b[to_b : to_b + 1, :] = row[:, c * cy : (c + 1) * cy]
    pay_a[at + 2 * EDGE :, :] = column
    at += 2 * nt * EDGE
    pay_b[at : at + EDGE, :] = column
    at += EDGE
    top = theta[:, cy - 1, :] * mask[cy - 1 :, :]
    bottom = theta[:, 0, :] * mask[:1, :]
    for c in range(nt):
        t, b = top[:, c * cy : (c + 1) * cy], bottom[:, c * cy : (c + 1) * cy]
        row_a[c * levels : (c + 1) * levels, :] = jnp.where(even_row, t, b)
        row_b[c * levels : (c + 1) * levels, :] = jnp.where(even_row, b, t)
        pay_b[at + c * levels : at + (c + 1) * levels, :] = t


def forcing_kernel(last, width, places, tt, kt, got_a, got_b, tops_m, tops_a, tops_b, *rest):
    *corners, out = rest
    at_m, at_a, at_b, at_corners = places
    cx, cy = tt.shape
    lon, lat = lax.axis_index("lon"), lax.axis_index("lat")
    even = lax.rem(lon, 2) == 0
    nt = cx // cy

    stack = []
    for which in (0, 1):
        a = tops_a[at_a + which * EDGE : at_a + (which + 1) * EDGE, :]
        b_first = tops_b[at_b + which * nt * EDGE : at_b + (which * nt + 1) * EDGE, :]
        b_last = tops_b[at_b + (which * nt + nt - 1) * EDGE : at_b + (which * nt + nt) * EDGE, :]
        stack.append(jnp.where(even, b_last, a))
        for c in range(nt):
            stack.append(tops_m[at_m + (which * nt + c) * EDGE : at_m + (which * nt + c + 1) * EDGE, :])
        stack.append(jnp.where(even, a, b_first))
    used = len(stack) * EDGE
    stack = jnp.concatenate(stack + [jnp.zeros((cy - used, cy), jnp.float32)], axis=0).T
    fold_lane = (iota((cy, cy), 1) < EDGE) & (lat == last)

    def extended(own, at, which):
        a = got_a[at : at + EDGE, :]
        b = got_b[at : at + EDGE, :]
        rows = jnp.concatenate([jnp.where(even, b, a), own, jnp.where(even, a, b)], axis=0)
        first = which * (nt + 2)
        tiles = [jnp.where(fold_lane, turn(stack, -(first + n) * EDGE, 1), 0.0) for n in range(nt + 2)]
        fold = jnp.concatenate([tiles[0][cy - EDGE :]] + tiles[1:-1] + [tiles[-1][:EDGE]], axis=0)
        return jnp.concatenate([rows, fold], axis=1)

    t = extended(tt[...], 0, 0)
    k = extended(kt[...], EDGE, 1)
    f = t + k * (beside(t) - 4.0 * t)
    rows = cx + 2 * EDGE
    lane = iota((rows, cy), 1)
    t0, k0 = t[:, :cy], k[:, :cy]
    pack = jnp.where(lane == 0, t0, 0.0)
    pack = jnp.where(lane == 1, turn(t0, 2, 1), pack)
    pack = jnp.where(lane == 2, turn(k0, 2, 1), pack)
    pack = jnp.where(lane == 3, turn(k0, 4, 1), pack)
    pack = jnp.where((lane >= 4) & (lane < 8), turn(f[:, cy:], 4, 1), pack)
    wide = -(-rows // 128) * 128
    pack = jnp.concatenate([pack, jnp.zeros((wide - rows, cy), jnp.float32)], axis=0).T[:8]
    low = iota((EDGE, cy), 0) < HALO
    corner = sum(ref[at : at + EDGE, :] for ref, at in zip(corners, at_corners))
    corner = jnp.where(low, turn(turn(corner, HALO, 0), 64, 1), corner)
    in_pack = iota((EDGE, cy), 1) < 64
    for d in range(cx // width):
        at = EDGE + d * width
        out[d, :width, :] = f[at : at + width, :cy]
        out[d, width : width + EDGE, :] = jnp.where(low, f[at + width : at + width + EDGE, :cy], f[at - EDGE : at, :cy])
        out[d, width + EDGE :, :] = jnp.where(in_pack, turn(pack, -d * width, 1)[:, :128], corner)


def strip_order(columns, width):
    low = iota((EDGE, columns.shape[1]), 0) < HALO
    ends = jnp.where(low, columns[EDGE + width : 2 * EDGE + width], columns[:EDGE])
    return jnp.concatenate([columns[EDGE : EDGE + width], ends], axis=0)


def krylov_kernel(cell, start, table, got, diag, rows_a, rows_b, basis, gram):
    count, chunk, cy = got.shape
    width, full = diag.shape
    rows = width + EDGE
    lon, lat = lax.axis_index("lon"), lax.axis_index("lat")
    x0 = (lon * count + lat) * width
    down, across = table.shape
    nx = across * cell
    lons = nx // (count * width)

    edges = jnp.concatenate([got[s, rows:, :] for s in range(count)], axis=0)
    if edges.shape[0] < 128:
        edges = jnp.concatenate([edges, jnp.zeros((128 - edges.shape[0], cy), jnp.float32)], axis=0)
    edges = strip_order(edges.T, width)
    from_south = edges * turn(edges, 9, 1)
    from_north = edges * turn(edges, -5, 1)
    lane = iota((rows, cy), 1)
    parts = []
    for s in range(count):
        part = got[s, :rows, :]
        if s > 0:
            part = part + jnp.where(lane == 0, turn(from_south, -(8 * s + 2), 1), 0.0)
        if s < count - 1:
            part = part + jnp.where(lane == cy - 1, turn(from_north, cy - 1 - (8 * s + 3), 1), 0.0)
        parts.append(part)
    parts.append(jnp.where(lane < HALO, turn(edges, -(8 * (count - 1) + 4), 1), 0.0))
    f = jnp.concatenate(parts, axis=1)

    place = iota((rows, across), 0)
    x = x0 + jnp.where(place < width + HALO, place, place - rows)
    x = jnp.where(x < 0, x + nx, jnp.where(x >= nx, x - nx, x))
    cells = iota((rows, across), 1)
    here = ones_at(lax.div(x, cell) == cells)
    there = ones_at(lax.div(nx - 1 - x, cell) == cells)
    up = ones_at(lax.div(iota((down, full), 1), cell) == iota((down, full), 0))
    above = ones_at((iota((down, cy), 0) == down - 1) & (iota((down, cy), 1) < HALO))
    land = table[...].astype(jnp.float32)
    pick = lax.dot_general(jnp.concatenate([here, there], axis=0), land, (((1,), (1,)), ((), ())), preferred_element_type=jnp.float32)
    mask = jnp.concatenate([mat(pick[:rows], up), mat(pick[rows:], above)], axis=1)

    even_row = lax.rem(lat, 2) == 0
    rim = full // cy * RIM
    d_a, d_b = rows_a[start : start + rim, :], rows_b[start : start + rim, :]
    d_east, d_west = jnp.where(even_row, d_a, d_b), jnp.where(even_row, d_b, d_a)
    unused = jnp.zeros((EDGE - 2 * RIM, cy), jnp.float32)
    d_ends = [
        jnp.concatenate([d_east[c * RIM : (c + 1) * RIM], unused, d_west[c * RIM : (c + 1) * RIM]], axis=0) for c in range(full // cy)
    ]
    d_main = jnp.concatenate([diag[...], jnp.concatenate(d_ends, axis=1)], axis=0)

    mine = lon * count + lat
    total = lons * count
    tiles = []
    for strip in (total - 1 - mine, lax.rem(2 * total - 2 - mine, total), lax.rem(total - mine, total)):
        tile = got[lax.rem(strip, count)][rows:, :]
        tile = jnp.where(iota((EDGE, 128), 1) < 64, turn(turn(tile, HALO, 0), 64, 1), tile)
        tiles.append(turn(tile, lax.rem(128 - lax.div(strip, count) * width, 128), 1))
    here = iota((128, 128), 0)
    there = iota((128, 128), 1)
    picks = [
        (here + there == width - 1) & (there < width),
        (here + there == 2 * width - 1) & (there >= width) & (there < width + HALO),
        (here + there == rows - 1) & (there >= rows - HALO) & (there < rows),
    ]
    fold = sum(mat(tile, ones_at(pick), EXACT) for tile, pick in zip(tiles, picks))
    fold = [fold[EDGE - 1 - r : EDGE - r] for r in range(HALO)] + [jnp.zeros((128 - HALO, 128), jnp.float32)]
    d_all = jnp.concatenate([d_main, jnp.concatenate(fold, axis=0).T[:rows]], axis=1)

    near = mask * (1.0 / WIDTH)
    centre = near * ((4.0 - CENTRE) + d_all)
    p = [mask * f]
    p.append(centre * p[0] - near * beside(p[0]))
    for j in range(2, ITERS + 1):
        p.append(2.0 * (centre * p[j - 1] - near * beside(p[j - 1])) - p[j - 2])
    for j in range(ITERS):
        basis[j] = p[j][:width, :full]
    sums = []
    for i in range(ITERS):
        for j in range(i, ITERS + 1):
            both = p[i][:width, :full] * p[j][:width, :full]
            both = sum(both[:, c : c + 128] for c in range(0, full, 128))
            sums.append(jnp.sum(both, axis=0, keepdims=True))
    sums = jnp.concatenate(sums + [jnp.zeros((128 - len(sums), 128), jnp.float32)], axis=0)
    gram[...] = jnp.broadcast_to(jnp.sum(sums.T, axis=0, keepdims=True), gram.shape)


def combine_kernel(gram, basis, psi):
    g = jnp.sum(gram[...], axis=0, keepdims=True)
    pairs = [(i, j) for i in range(ITERS) for j in range(i, ITERS + 1)]
    at = {}
    for n, (i, j) in enumerate(pairs):
        at[i, j] = at[j, i] = jnp.broadcast_to(g[:, n : n + 1], (8, 128))

    def applied(i, j):
        if j == 0:
            return CENTRE * at[i, 0] + WIDTH * at[i, 1]
        return CENTRE * at[i, j] + (0.5 * WIDTH) * (at[i, j + 1] + at[i, j - 1])

    a = {(i, j): applied(i, j) for i in range(ITERS) for j in range(i, ITERS)}
    b = [at[i, 0] for i in range(ITERS)]
    inverse = []
    for k in range(ITERS):
        inverse.append(1.0 / a[k, k])
        for i in range(k + 1, ITERS):
            factor = a[k, i] * inverse[k]
            for j in range(i, ITERS):
                a[i, j] = a[i, j] - factor * a[k, j]
            b[i] = b[i] - factor * b[k]
    c = [None] * ITERS
    for i in reversed(range(ITERS)):
        value = b[i]
        for j in range(i + 1, ITERS):
            value = value - a[i, j] * c[j]
        c[i] = value * inverse[i]
    total = c[0][:1, :1] * basis[0]
    for j in range(1, ITERS):
        total = total + c[j][:1, :1] * basis[j]
    psi[...] = total


def tracer_kernel(last, start, theta, ocean, coef, got_a, got_b, rows_a, rows_b, fold, out_hbm, out, sems):
    levels, cy, cx = theta.shape
    lon, lat = lax.axis_index("lon"), lax.axis_index("lat")
    even = lax.rem(lon, 2) == 0
    a, b = got_a[2 * EDGE : 2 * EDGE + levels, :], got_b[2 * EDGE : 2 * EDGE + levels, :]
    both = jnp.concatenate([jnp.where(even, a, b), jnp.where(even, b, a), jnp.zeros((128 - 2 * levels, cy), jnp.float32)], axis=0)
    sides = both.T
    even_row = lax.rem(lat, 2) == 0

    def joined(ref, at=0):
        return jnp.concatenate([ref[at + c * levels : at + (c + 1) * levels, :] for c in range(cx // cy)], axis=1)

    a, b = joined(rows_a), joined(rows_b)
    flip = ones_at(iota((cx, cx), 0) + iota((cx, cx), 1) == cx - 1)
    north = jnp.where(lat == last, mat(joined(fold, start), flip, EXACT), jnp.where(even_row, a, b))
    south = jnp.where(lat == 0, 0.0, jnp.where(even_row, b, a))

    lane = iota((cy, 128), 1)
    row = iota((cy, cx), 0)
    mask, scale = ocean[...], coef[...]
    some = 2
    copies = []
    for k in range(levels):
        th = theta[k]
        m = mask * th
        east, west = turn(m, -1, 1), turn(m, 1, 1)
        east = jnp.concatenate([east[:, : cx - 128], jnp.where(lane == 127, turn(sides, 127 - k, 1), east[:, cx - 128 :])], axis=1)
        west = jnp.concatenate([jnp.where(lane == 0, turn(sides, -levels - k, 1), west[:, :128]), west[:, 128:]], axis=1)
        above = jnp.where(row == cy - 1, north[k : k + 1], turn(m, -1, 0))
        below = jnp.where(row == 0, south[k : k + 1], turn(m, 1, 0))
        out[k] = th + scale * (east + west + above + below - 4.0 * m)
        if (k + 1) % some == 0:
            n = k // some
            piece = pl.ds(n * some, some)
            copies.append(pltpu.make_async_copy(out.at[piece], out_hbm.at[piece], sems.at[n]))
            copies[-1].start()
    for copy in copies:
        copy.wait()


def per_device(theta, kappa, layer_weight, diag, land_blocks):
    lons, lats = lax.axis_size("lon"), lax.axis_size("lat")
    joint = ("lon", "lat")
    devices = lons * lats
    levels, cy, cx = theta.shape
    width, full = diag.shape
    cell = full // land_blocks.shape[0]
    last = lats - 1
    f32 = jnp.float32
    shape = lambda *dims: jax.ShapeDtypeStruct(dims, f32)

    nt = cx // cy
    head = 2 * EDGE + levels
    own = (2 * nt + 1) * EDGE
    rim = RIM * (full // cy)
    held, ocean, coef, tt, kt, pay_a, pay_b, row_a, row_b = pl.pallas_call(
        functools.partial(sum_kernel, cell),
        in_specs=[HBM] * 5,
        out_specs=[VMEM] * 9,
        out_shape=[
            pltpu.VMEM((levels, cy, cx), f32),
            shape(cy, cx),
            shape(cy, cx),
            shape(cx, cy),
            shape(cx, cy),
            shape(head + 3 * EDGE, cy),
            shape(head + own + nt * levels, cy),
            shape(nt * levels + rim, cy),
            shape(nt * levels + rim, cy),
        ],
        scratch_shapes=[
            pltpu.VMEM((cy, cx), f32),
            pltpu.VMEM((width, 128), f32),
            pltpu.VMEM((2, EDGE, full), f32),
            pltpu.VMEM(land_blocks.shape, jnp.int32),
            pltpu.SMEM((levels,), f32),
            pltpu.SemaphoreType.DMA((10,)),
        ],
        compiler_params=PARAMS,
        name="level_sum",
    )(*map(in_hbm, (layer_weight, land_blocks, theta, kappa, diag)))

    pairs_b = [(i, (i + 1) % lons if i % 2 else (i - 1) % lons) for i in range(lons)]
    mirror = [(i, lons - 1 - i) for i in range(lons)]
    got_a = lax.ppermute(pay_a, "lon", [(i, i ^ 1) for i in range(lons)])
    if pairs_b == mirror:
        got_b = lax.ppermute(jnp.concatenate([pay_b, got_a[head:]], axis=0), "lon", pairs_b)
        fold, at_fold = got_b, head + own
        folds = (got_b, got_b, pay_b)
        corners = (pay_b, got_a, got_b, got_b)
        tail = at_fold + nt * levels
        places = (head, tail, head, (at_fold - EDGE, head + 2 * EDGE, at_fold - EDGE, tail + 2 * EDGE))
    else:
        got_b = lax.ppermute(pay_b, "lon", pairs_b)
        fold = lax.ppermute(jnp.concatenate([pay_b[head:], got_a[head:], got_b[head:]], axis=0), "lon", mirror)
        at_fold = own
        folds = (fold, fold, fold)
        corners = (lax.psum(pay_a[head + 2 * EDGE :], "lon"),)
        tail = own + nt * levels
        places = (0, tail, tail + 3 * EDGE, (0,))
    chunks = pl.pallas_call(
        functools.partial(forcing_kernel, last, width, places),
        in_specs=[VMEM] * (7 + len(corners)),
        out_specs=VMEM,
        out_shape=shape(lats, width + 2 * EDGE, cy),
        compiler_params=PARAMS,
        name="forcing",
    )(tt, kt, got_a, got_b, *folds, *corners)
    chunks, row_a = lax.optimization_barrier((chunks, row_a))
    got = lax.all_to_all(chunks, "lat", split_axis=0, concat_axis=0, tiled=True)

    rows_a = lax.ppermute(row_a, joint, [(i, i ^ 1) for i in range(devices)])
    rows_b = lax.ppermute(row_b, joint, [(i, (i + 1 if i % 2 else i - 1) % devices) for i in range(devices)])
    new_theta = pl.pallas_call(
        functools.partial(tracer_kernel, last, at_fold),
        in_specs=[VMEM] * 8,
        out_specs=HBM,
        out_shape=shape(levels, cy, cx),
        scratch_shapes=[pltpu.VMEM((levels, cy, cx), f32), pltpu.SemaphoreType.DMA((levels // 2,))],
        compiler_params=PARAMS,
        cost_estimate=pl.CostEstimate(flops=12 * levels * cy * cx, bytes_accessed=8 * levels * cy * cx, transcendentals=0),
        name="tracer",
    )(held, ocean, coef, got_a, got_b, rows_a, rows_b, fold)

    basis, gram = pl.pallas_call(
        functools.partial(krylov_kernel, cell, nt * levels),
        in_specs=[VMEM] * 5,
        out_specs=[VMEM, VMEM],
        out_shape=[shape(ITERS, width, full), shape(devices, 128)],
        compiler_params=PARAMS,
        name="krylov",
    )(land_blocks, got, diag, rows_a, rows_b)
    gram = lax.all_to_all(gram, joint, split_axis=0, concat_axis=0, tiled=True)
    psi = pl.pallas_call(
        combine_kernel,
        in_specs=[VMEM, VMEM],
        out_specs=VMEM,
        out_shape=shape(width, full),
        compiler_params=PARAMS,
        name="combine",
    )(gram, basis)
    return new_theta, psi


def solution(mesh):
    return jax.shard_map(
        per_device,
        mesh=mesh,
        in_specs=(P(None, "lat", "lon"), P("lat", "lon"), P(), P(("lon", "lat"), None), P()),
        out_specs=(P(None, "lat", "lon"), P(("lon", "lat"), None)),
        check_vma=False,
    )
```

time: 48.9 us -> 39 us (0.80)
  the two profiles are of different devices: /device:TPU:8 before, /device:TPU:0 now
where the time goes in v2:
time: 39 us; the launch traced here: 38.7 us
  starting transfers between devices  17.4 us (45%)
  waiting for transfers between devices  11.5 us (29%)
  Pallas kernels  9.08 us (23%)
  between operations  0.68 us (2%)
    all_to_all x1, starting transfers between devices, per_device(): got = lax.all_to_all(chunks, 'lat', split_axis=0, concat_axis=0, tiled=True)  6.4 us
    ppermute x1, starting transfers between devices, per_device(): lax.ppermute(row_b, joint, [(i, (i + 1 if i % 2 else i - 1) % devices) fo...  4.88 us
    all_to_all x1, waiting for transfers between devices, per_device(): gram = lax.all_to_all(gram, joint, split_axis=0, concat_axis=0, tiled=True)  4.14 us
    ppermute x1, waiting for transfers between devices, per_device(): lax.ppermute(row_b, joint, [(i, (i + 1 if i % 2 else i - 1) % devices) fo...  4.13 us
    all_to_all x1, starting transfers between devices, per_device(): gram = lax.all_to_all(gram, joint, split_axis=0, concat_axis=0, tiled=True)  2.95 us
    pallas_call x1, Pallas kernels, per_device(): pl.pallas_call(functools.partial(tracer_kernel, last, at_fold), in_specs=...  2.89 us
    ppermute x1, starting transfers between devices, per_device(): lax.ppermute(jnp.concatenate([pay_b, got_a[head:]], axis=0), 'lon', pairs_b)  2.69 us
    pallas_call x1, Pallas kernels, per_device(): pl.pallas_call(functools.partial(sum_kernel, cell), in_specs=[HBM] * 5, o...  2.39 us
  transfers between devices with their start and end apart: 6, of which 5 were waited for; matrix products, arithmetic and copies ran while one was open for 0% of the time, Pallas kernels for 7%

profile of v2, /device:TPU:0, one launch (start us, length us, event | category | flops | bytes accessed | tf_op | source)
XLA Modules:
  0.0 38.7 jit_solution(161661338307018990)
XLA Ops:
  0.6 0.0 copy-start
  0.6 0.0 copy-start.1
  0.7 2.4 %level_sum.1 = (f32[16,128,256]{2,1,0:T(8,128)S(1)}, f32[128,256]{1,0:T(8,128)S(1)}, f32[128,256]{1,0:T(8,128)S(1)}, f32[256,128]{1,0:T(8,128)S(1)}, f32[256,128...) custom-call(f32[16]{0:T(128)} %weight_hbm.1, ...), custom_call_target="tpu_custom_call" | custom-call | tf_op jit(solution)/shard_map/level_sum/pallas_call | solution.py:377
  3.0 0.5 %collective-permute-start = (f32[56,128]{1,0:T(8,128)S(1)}, f32[56,128]{1,0:T(8,128)S(1)}, u32[]{:S(2)}, u32[]{:S(2)}) collective-permute-start(f32[56,128]{1,0:T(8,128)S(1)} %get-tuple-element.18), channel_id=1, source_target_pairs={{0,8},{8,0},{16,24},{24,16},{1,9},{9,1},{17,25},{25,17},{2,10},{10... | collective-permute-start | bytes 86024 | tf_op jit(solution)/shard_map/ppermute | solution.py:406
  3.6 0.9 %collective-permute-done.got_a.rest_1_ = f32[56,128]{1,0:T(8,128)S(1)} collective-permute-done((f32[56,128]{1,0:T(8,128)S(1)}, f32[56,128]{1,0:T(8,128)S(1)}, u32[]{:S(2)}, u32[]{:S(2)}) %collective-permute-start) | collective-permute-done | bytes 28704 | tf_op jit(solution)/shard_map/ppermute | solution.py:406
  4.4 2.7 %collective-permute-start.1 = (f32[128,128]{1,0:T(8,128)S(1)}, f32[128,128]{1,0:T(8,128)S(1)}, u32[]{:S(2)}, u32[]{:S(2)}) collective-permute-start(f32[128,128]{1,0:T(8,128)S(1)} %pad_maximum_fusion), channel_id=1, source_target_pairs={{0,24},{8,16},{16,8},{24,0},{1,25},{9,17},{17,9},{25,1},{2,26},{10... | collective-permute-start | bytes 196616 | tf_op jit(solution)/shard_map/ppermute | solution.py:408
  7.1 2.2 %collective-permute-done.1.got_b.tops_m.tops_a.rest_2_.rest_3_.fold = f32[128,128]{1,0:T(8,128)S(1)} collective-permute-done((f32[128,128]{1,0:T(8,128)S(1)}, f32[128,128]{1,0:T(8,128)S(1)}, u32[]{:S(2)}, u32[]{:S(2)}) %collective-permute-start.1) | collective-permute-done | bytes 65568 | tf_op jit(solution)/shard_map/ppermute | solution.py:408
  9.3 1.4 %forcing.1 = f32[8,48,128]{2,1,0:T(8,128)} custom-call(f32[256,128]{1,0:T(8,128)S(1)} %get-tuple-element.20.tt, f32[256,128]{1,0:T(8,128)S(1)} %get-tuple-element.21.kt, f32[56,128]{1,0:T(8,128)S(1)} %collective-permute-done.got_a.rest_1_, f32[128,128]{1,0:T(8,128)S(1)} %collective-permute-done.1.got_b.tops_m.tops_a.rest_2_.rest_3_.fold, ...), custom_call_target="tpu_custom_call" | custom-call | tf_op jit(solution)/shard_map/forcing/pallas_call | solution.py:422
  10.7 6.4 %all-to-all-start = ((f32[8,48,128]{2,1,0:T(8,128)}), f32[8,48,128]{2,1,0:T(8,128)S(1)}, u32[]{:S(2)}, u32[]{:S(2)}) async-start(f32[8,48,128]{2,1,0:T(8,128)} %forcing.1), calls=%async_computation | async-start | bytes 393216 | tf_op jit(solution)/shard_map/all_to_all | solution.py:431
  17.1 4.9 %collective-permute-start.3 = (f32[56,128]{1,0:T(8,128)S(1)}, f32[56,128]{1,0:T(8,128)S(1)}, u32[]{:S(2)}, u32[]{:S(2)}) collective-permute-start(f32[56,128]{1,0:T(8,128)S(1)} %get-tuple-element.24), channel_id=1, source_target_pairs={{0,31},{1,2},{2,1},{3,4},{4,3},{5,6},{6,5},{7,8},{8,7},{9,10},{10,... | collective-permute-start | bytes 86024 | tf_op jit(solution)/shard_map/ppermute | solution.py:434
  21.9 0.0 collective-permute-start.2
  21.9 4.1 %collective-permute-done.3.rows_b = f32[56,128]{1,0:T(8,128)S(1)} collective-permute-done((f32[56,128]{1,0:T(8,128)S(1)}, f32[56,128]{1,0:T(8,128)S(1)}, u32[]{:S(2)}, u32[]{:S(2)}) %collective-permute-start.3) | collective-permute-done | bytes 28704 | tf_op jit(solution)/shard_map/ppermute | solution.py:434
  26.1 0.2 collective-permute-done.2.rows_a
  26.3 0.0 all-to-all-done.got
  26.3 0.0 copy-done
  26.3 0.0 copy-done.1
  26.3 1.6 %krylov.1 = (f32[4,32,1024]{2,1,0:T(8,128)S(1)}, f32[32,128]{1,0:T(8,128)}) custom-call(s32[32,32]{1,0:T(8,128)S(1)} %copy-done.1, f32[8,48,128]{2,1,0:T(8,128)S(1)} %all-to-all-done.got, f32[32,1024]{1,0:T(8,128)S(1)} %copy-done, f32[56,128]{1,0:T(8,128)S(1)} %collective-permute-done.2.rows_a, f32[56,128]{1,0:T(8,128)S(1)} %collective-permute-done.3.rows_b), custom_call_target="tpu_custom_call" | custom-call | tf_op jit(solution)/shard_map/krylov/pallas_call | solution.py:446
  27.9 2.9 %all-to-all-start.1 = ((f32[32,1,128]{2,1,0:T(1,128)}), f32[32,1,128]{2,1,0:T(1,128)S(1)}, u32[]{:S(2)}, u32[]{:S(2)}) async-start(f32[32,1,128]{2,1,0:T(1,128)} %bitcast.1), calls=%async_computation.1 | async-start | bytes 32768 | tf_op jit(solution)/shard_map/all_to_all | solution.py:454
  30.9 2.9 %tracer.1 = f32[16,128,256]{2,1,0:T(8,128)} custom-call(f32[16,128,256]{2,1,0:T(8,128)S(1)} %get-tuple-element.15.theta, f32[128,256]{1,0:T(8,128)S(1)} %get-tuple-element.16.ocean, f32[128,256]{1,0:T(8,128)S(1)} %get-tuple-element.17.coef, f32[56,128]{1,0:T(8,128)S(1)} %collective-permute-done.got_a.rest_1_, ...), custom_call_target="tpu_custom_call" | custom-call | flops 6291456 | bytes 4194304 | tf_op jit(solution)/shard_map/tracer/pallas_call | solution.py:435
  33.7 4.1 %all-to-all-done.1 = f32[32,1,128]{2,1,0:T(1,128)S(1)} async-done(((f32[32,1,128]{2,1,0:T(1,128)}), f32[32,1,128]{2,1,0:T(1,128)S(1)}, u32[]{:S(2)}, u32[]{:S(2)}) %all-to-all-start.1) | async-done | bytes 16416 | tf_op jit(solution)/shard_map/all_to_all | solution.py:454
  37.9 0.8 %combine.1 = f32[32,1024]{1,0:T(8,128)} custom-call(f32[32,128]{1,0:T(8,128)S(1)} %bitcast.4, f32[4,32,1024]{2,1,0:T(8,128)S(1)} %get-tuple-element.27.basis), custom_call_target="tpu_custom_call" | custom-call | tf_op jit(solution)/shard_map/combine/pallas_call | solution.py:455
  (2 shorter events, 0.0 us)
Async XLA Ops:
  0.6 25.6 %copy-start = (f32[32,1024]{1,0:T(8,128)S(1)}, f32[32,1024]{1,0:T(8,128)}, u32[]{:S(2)}) copy-start(f32[32,1024]{1,0:T(8,128)} %diag.1) | copy-start | bytes 393220
  0.6 25.6 %copy-start.1 = (s32[32,32]{1,0:T(8,128)S(1)}, s32[32,32]{1,0:T(8,128)}, u32[]{:S(2)}) copy-start(s32[32,32]{1,0:T(8,128)} %table.1) | copy-start | bytes 12292
  3.0 1.4 %collective-permute-start = (f32[56,128]{1,0:T(8,128)S(1)}, f32[56,128]{1,0:T(8,128)S(1)}, u32[]{:S(2)}, u32[]{:S(2)}) collective-permute-start(f32[56,128]{1,0:T(8,128)S(1)} %get-tuple-element.18), channel_id=1, source_target_pairs={{0,8},{8,0},{16,24},{24,16},{1,9},{9,1},{17,25},{25,17},{2,10},{10... | collective-permute-start | bytes 86024 | tf_op jit(solution)/shard_map/ppermute | solution.py:406
  4.4 4.9 %collective-permute-start.1 = (f32[128,128]{1,0:T(8,128)S(1)}, f32[128,128]{1,0:T(8,128)S(1)}, u32[]{:S(2)}, u32[]{:S(2)}) collective-permute-start(f32[128,128]{1,0:T(8,128)S(1)} %pad_maximum_fusion), channel_id=1, source_target_pairs={{0,24},{8,16},{16,8},{24,0},{1,25},{9,17},{17,9},{25,1},{2,26},{10... | collective-permute-start | bytes 196616 | tf_op jit(solution)/shard_map/ppermute | solution.py:408
  10.7 15.6 %all-to-all-start = ((f32[8,48,128]{2,1,0:T(8,128)}), f32[8,48,128]{2,1,0:T(8,128)S(1)}, u32[]{:S(2)}, u32[]{:S(2)}) async-start(f32[8,48,128]{2,1,0:T(8,128)} %forcing.1), calls=%async_computation | async-start | bytes 393216 | tf_op jit(solution)/shard_map/all_to_all | solution.py:431
  17.1 9.0 %collective-permute-start.3 = (f32[56,128]{1,0:T(8,128)S(1)}, f32[56,128]{1,0:T(8,128)S(1)}, u32[]{:S(2)}, u32[]{:S(2)}) collective-permute-start(f32[56,128]{1,0:T(8,128)S(1)} %get-tuple-element.24), channel_id=1, source_target_pairs={{0,31},{1,2},{2,1},{3,4},{4,3},{5,6},{6,5},{7,8},{8,7},{9,10},{10,... | collective-permute-start | bytes 86024 | tf_op jit(solution)/shard_map/ppermute | solution.py:434
  21.9 4.3 %collective-permute-start.2 = (f32[56,128]{1,0:T(8,128)S(1)}, f32[56,128]{1,0:T(8,128)S(1)}, u32[]{:S(2)}, u32[]{:S(2)}) collective-permute-start(f32[56,128]{1,0:T(8,128)S(1)} %get-tuple-element.23), channel_id=1, source_target_pairs={{0,1},{1,0},{2,3},{3,2},{4,5},{5,4},{6,7},{7,6},{8,9},{9,8},{10,11... | collective-permute-start | bytes 86024 | tf_op jit(solution)/shard_map/ppermute | solution.py:433
  27.9 10.0 %all-to-all-start.1 = ((f32[32,1,128]{2,1,0:T(1,128)}), f32[32,1,128]{2,1,0:T(1,128)S(1)}, u32[]{:S(2)}, u32[]{:S(2)}) async-start(f32[32,1,128]{2,1,0:T(1,128)} %bitcast.1), calls=%async_computation.1 | async-start | bytes 32768 | tf_op jit(solution)/shard_map/all_to_all | solution.py:454

commit v3 on v2

--- a/solution.py
+++ b/solution.py
@@ -51,7 +51,7 @@
     return mat(mat(pick_rows, table), pick_cols)
 
 
-def sum_kernel(cell, weight_hbm, table_hbm, theta_hbm, kappa_hbm, diag_hbm, theta, ocean, coef, tt, kt, pay_a, pay_b, row_a, row_b, kappa, corner, rim, table, weight, sems):
+def sum_kernel(cell, weight_hbm, table_hbm, theta_hbm, kappa_hbm, diag_hbm, theta, ocean, coef, tt, kt, pay_a, pay_b, pay_c, pay_d, row_a, row_b, kappa, corner, rim, table, weight, sems):
     levels, cy, cx = theta.shape
     width, full = diag_hbm.shape
     copies = [
@@ -107,36 +107,35 @@
     ttv = t.T
     tt[...] = ttv
     sidest = (sides * jnp.where(lane < levels, mask[:, :1], mask[:, cx - 1 :])).T
-    west = (ttv[:EDGE], ktv[:EDGE], sidest[:levels])
-    east = (ttv[cx - EDGE :], ktv[cx - EDGE :], sidest[levels : 2 * levels])
-    at = 0
-    for w, e in zip(west, east):
-        rows = w.shape[0]
-        pay_a[at : at + rows, :] = jnp.where(even, e, w)
-        pay_b[at : at + rows, :] = jnp.where(even, w, e)
-        at += rows
+    west, east = sidest[:levels], sidest[levels : 2 * levels]
+    pay_a[2 * EDGE : 2 * EDGE + levels, :] = jnp.where(even, east, west)
+    pay_d[:levels, :] = jnp.where(even, west, east)
+    for at, turned in ((0, ttv), (EDGE, ktv)):
+        w, e = turned[:EDGE], turned[cx - EDGE :]
+        pay_a[at : at + EDGE, :] = jnp.where(even, e, w)
+        pay_b[at : at + EDGE, :] = jnp.where(even, w, e)
+    at = 2 * EDGE
     flip = ones_at(iota((cx, cx), 0) + iota((cx, cx), 1) == cx - 1)
     both = jnp.concatenate([t[cy - EDGE :], kappas[cy - EDGE :, :]], axis=0)
     turned = mat(both, flip, EXACT)
     nt = cx // cy
-    for base, to in ((0, at), (EDGE, at + EDGE)):
+    for base in (0, EDGE):
         for r in range(EDGE):
             row = turned[base + EDGE - 1 - r : base + EDGE - r]
-            pay_a[to + r : to + r + 1, :] = jnp.where(even, row[:, :cy], row[:, cx - cy :])
+            pay_c[base + r : base + r + 1, :] = jnp.where(even, row[:, :cy], row[:, cx - cy :])
             for c in range(nt):
                 to_b = at + (base // EDGE * nt + c) * EDGE + r
                 pay_b[to_b : to_b + 1, :] = row[:, c * cy : (c + 1) * cy]
-    pay_a[at + 2 * EDGE :, :] = column
-    at += 2 * nt * EDGE
-    pay_b[at : at + EDGE, :] = column
-    at += EDGE
+    pay_a[at + levels :, :] = column
+    pay_c[2 * EDGE :, :] = column
+    pay_b[at + 2 * nt * EDGE :, :] = column
     top = theta[:, cy - 1, :] * mask[cy - 1 :, :]
     bottom = theta[:, 0, :] * mask[:1, :]
     for c in range(nt):
         t, b = top[:, c * cy : (c + 1) * cy], bottom[:, c * cy : (c + 1) * cy]
         row_a[c * levels : (c + 1) * levels, :] = jnp.where(even_row, t, b)
         row_b[c * levels : (c + 1) * levels, :] = jnp.where(even_row, b, t)
-        pay_b[at + c * levels : at + (c + 1) * levels, :] = t
+        pay_d[(c + 1) * levels : (c + 2) * levels, :] = t
 
 
 def forcing_kernel(last, width, places, tt, kt, got_a, got_b, tops_m, tops_a, tops_b, *rest):
@@ -319,11 +318,11 @@
     psi[...] = total
 
 
-def tracer_kernel(last, start, theta, ocean, coef, got_a, got_b, rows_a, rows_b, fold, out_hbm, out, sems):
+def tracer_kernel(last, start, theta, ocean, coef, got_a, got_d, rows_a, rows_b, fold, out_hbm, out, sems):
     levels, cy, cx = theta.shape
     lon, lat = lax.axis_index("lon"), lax.axis_index("lat")
     even = lax.rem(lon, 2) == 0
-    a, b = got_a[2 * EDGE : 2 * EDGE + levels, :], got_b[2 * EDGE : 2 * EDGE + levels, :]
+    a, b = got_a[2 * EDGE : 2 * EDGE + levels, :], got_d[:levels, :]
     both = jnp.concatenate([jnp.where(even, a, b), jnp.where(even, b, a), jnp.zeros((128 - 2 * levels, cy), jnp.float32)], axis=0)
     sides = both.T
     even_row = lax.rem(lat, 2) == 0
@@ -371,21 +370,23 @@
     shape = lambda *dims: jax.ShapeDtypeStruct(dims, f32)
 
     nt = cx // cy
-    head = 2 * EDGE + levels
+    head = 2 * EDGE
     own = (2 * nt + 1) * EDGE
     rim = RIM * (full // cy)
-    held, ocean, coef, tt, kt, pay_a, pay_b, row_a, row_b = pl.pallas_call(
+    held, ocean, coef, tt, kt, pay_a, pay_b, pay_c, pay_d, row_a, row_b = pl.pallas_call(
         functools.partial(sum_kernel, cell),
         in_specs=[HBM] * 5,
-        out_specs=[VMEM] * 9,
+        out_specs=[VMEM] * 11,
         out_shape=[
             pltpu.VMEM((levels, cy, cx), f32),
             shape(cy, cx),
             shape(cy, cx),
             shape(cx, cy),
             shape(cx, cy),
-            shape(head + 3 * EDGE, cy),
-            shape(head + own + nt * levels, cy),
+            shape(head + levels + EDGE, cy),
+            shape(head + own, cy),
+            shape(3 * EDGE, cy),
+            shape((nt + 1) * levels, cy),
             shape(nt * levels + rim, cy),
             shape(nt * levels + rim, cy),
         ],
@@ -404,21 +405,19 @@
     pairs_b = [(i, (i + 1) % lons if i % 2 else (i - 1) % lons) for i in range(lons)]
     mirror = [(i, lons - 1 - i) for i in range(lons)]
     got_a = lax.ppermute(pay_a, "lon", [(i, i ^ 1) for i in range(lons)])
+    got_b = lax.ppermute(pay_b, "lon", pairs_b)
     if pairs_b == mirror:
-        got_b = lax.ppermute(jnp.concatenate([pay_b, got_a[head:]], axis=0), "lon", pairs_b)
-        fold, at_fold = got_b, head + own
-        folds = (got_b, got_b, pay_b)
-        corners = (pay_b, got_a, got_b, got_b)
-        tail = at_fold + nt * levels
-        places = (head, tail, head, (at_fold - EDGE, head + 2 * EDGE, at_fold - EDGE, tail + 2 * EDGE))
+        got_c = lax.ppermute(pay_c, "lon", [(i, i ^ 2) for i in range(lons)])
+        folds = (got_b, got_c, pay_b)
+        corners = (pay_b, got_a, got_b, got_c)
+        tail = head + own - EDGE
+        places = (head, 0, head, (tail, head + levels, tail, 2 * EDGE))
     else:
-        got_b = lax.ppermute(pay_b, "lon", pairs_b)
-        fold = lax.ppermute(jnp.concatenate([pay_b[head:], got_a[head:], got_b[head:]], axis=0), "lon", mirror)
-        at_fold = own
-        folds = (fold, fold, fold)
-        corners = (lax.psum(pay_a[head + 2 * EDGE :], "lon"),)
-        tail = own + nt * levels
-        places = (0, tail, tail + 3 * EDGE, (0,))
+        got_c = lax.ppermute(pay_c, "lon", [(i, i ^ 1) for i in range(lons)])
+        tops = lax.ppermute(jnp.concatenate([pay_b[head:], got_c, got_b[head:]], axis=0), "lon", mirror)
+        folds = (tops, tops, tops)
+        corners = (lax.psum(pay_c[2 * EDGE :], "lon"),)
+        places = (0, own, own + 3 * EDGE, (0,))
     chunks = pl.pallas_call(
         functools.partial(forcing_kernel, last, width, places),
         in_specs=[VMEM] * (7 + len(corners)),
@@ -427,13 +426,16 @@
         compiler_params=PARAMS,
         name="forcing",
     )(tt, kt, got_a, got_b, *folds, *corners)
-    chunks, row_a = lax.optimization_barrier((chunks, row_a))
+    chunks, row_a, pay_d = lax.optimization_barrier((chunks, row_a, pay_d))
     got = lax.all_to_all(chunks, "lat", split_axis=0, concat_axis=0, tiled=True)
 
     rows_a = lax.ppermute(row_a, joint, [(i, i ^ 1) for i in range(devices)])
     rows_b = lax.ppermute(row_b, joint, [(i, (i + 1 if i % 2 else i - 1) % devices) for i in range(devices)])
+    got_d = lax.ppermute(pay_d, "lon", pairs_b)
+    got, got_d = lax.optimization_barrier((got, got_d))
+    fold = got_d if pairs_b == mirror else lax.ppermute(pay_d, "lon", mirror)
     new_theta = pl.pallas_call(
-        functools.partial(tracer_kernel, last, at_fold),
+        functools.partial(tracer_kernel, last, levels),
         in_specs=[VMEM] * 8,
         out_specs=HBM,
         out_shape=shape(levels, cy, cx),
@@ -441,7 +443,7 @@
         compiler_params=PARAMS,
         cost_estimate=pl.CostEstimate(flops=12 * levels * cy * cx, bytes_accessed=8 * levels * cy * cx, transcendentals=0),
         name="tracer",
-    )(held, ocean, coef, got_a, got_b, rows_a, rows_b, fold)
+    )(held, ocean, coef, got_a, got_d, rows_a, rows_b, fold)
 
     basis, gram = pl.pallas_call(
         functools.partial(krylov_kernel, cell, nt * levels),

time: 39 us -> 37.9 us (0.972)
  waiting for transfers between devices: 11.5 us -> 10.8 us
    ppermute x1, waiting for transfers between devices: 4.13 us -> 0.01 us  [per_device(): lax.ppermute(row_b, joint, [(i, (i + 1 if i % 2 else i - 1) % devices) fo...]
    ppermute x1 -> x3, waiting for transfers between devices: 2.18 us -> 5.53 us  [the longest x1 3.65 us: per_device(): got_c = lax.ppermute(pay_c, 'lon', [(i, i ^ 2) for i in range(lons)])]
    ppermute x1, starting transfers between devices: 4.88 us -> 3.09 us  [per_device(): lax.ppermute(row_b, joint, [(i, (i + 1 if i % 2 else i - 1) % devices) fo...]
    ppermute x1 -> x3, starting transfers between devices: 2.69 us -> 3.98 us  [the longest x1 2.47 us: per_device(): got_b = lax.ppermute(pay_b, 'lon', pairs_b)]
    all_to_all x1, waiting for transfers between devices: 0.01 us -> 1.06 us  [per_device(): got = lax.all_to_all(chunks, 'lat', split_axis=0, concat_axis=0, tiled=True)]
    ppermute x1, waiting for transfers between devices: 0.85 us -> 0.01 us  [per_device(): got_a = lax.ppermute(pay_a, 'lon', [(i, i ^ 1) for i in range(lons)])]
    all_to_all x1, starting transfers between devices: 6.4 us -> 5.81 us  [per_device(): got = lax.all_to_all(chunks, 'lat', split_axis=0, concat_axis=0, tiled=True)]
  transfers between devices with their start and end apart: 6 -> 8, of which waited for: 5 -> 4; matrix products, arithmetic and copies ran while one was open for 0% -> 0% of each run, Pallas kernels for 7% -> 8%
where the time goes in v3:
time: 37.9 us; the launch traced here: 37.6 us
  starting transfers between devices  17.1 us (45%)
  waiting for transfers between devices  10.8 us (28%)
  Pallas kernels  9.07 us (24%)
  between operations  0.69 us (2%)
    all_to_all x1, starting transfers between devices, per_device(): got = lax.all_to_all(chunks, 'lat', split_axis=0, concat_axis=0, tiled=True)  5.81 us
    all_to_all x1, waiting for transfers between devices, per_device(): gram = lax.all_to_all(gram, joint, split_axis=0, concat_axis=0, tiled=True)  4.15 us
    ppermute x1, waiting for transfers between devices, per_device(): got_c = lax.ppermute(pay_c, 'lon', [(i, i ^ 2) for i in range(lons)])  3.65 us
    all_to_all x1, starting transfers between devices, per_device(): gram = lax.all_to_all(gram, joint, split_axis=0, concat_axis=0, tiled=True)  3.18 us
    ppermute x1, starting transfers between devices, per_device(): lax.ppermute(row_b, joint, [(i, (i + 1 if i % 2 else i - 1) % devices) fo...  3.09 us
    pallas_call x1, Pallas kernels, per_device(): pl.pallas_call(functools.partial(tracer_kernel, last, levels), in_specs=[...  2.88 us
    ppermute x1, starting transfers between devices, per_device(): got_b = lax.ppermute(pay_b, 'lon', pairs_b)  2.47 us
    pallas_call x1, Pallas kernels, per_device(): pl.pallas_call(functools.partial(sum_kernel, cell), in_specs=[HBM] * 5, o...  2.39 us
  transfers between devices with their start and end apart: 8, of which 4 were waited for; matrix products, arithmetic and copies ran while one was open for 0% of the time, Pallas kernels for 8%

profile of v3, /device:TPU:0, one launch (start us, length us, event | category | flops | bytes accessed | tf_op | source)
XLA Modules:
  0.0 37.6 jit_solution(9278478219919161767)
XLA Ops:
  0.6 0.0 copy-start
  0.6 0.0 copy-start.1
  0.7 2.4 %level_sum.1 = (f32[16,128,256]{2,1,0:T(8,128)S(1)}, f32[128,256]{1,0:T(8,128)S(1)}, f32[128,256]{1,0:T(8,128)S(1)}, f32[256,128]{1,0:T(8,128)S(1)}, f32[256,128...) custom-call(f32[16]{0:T(128)} %weight_hbm.1, ...), custom_call_target="tpu_custom_call" | custom-call | tf_op jit(solution)/shard_map/level_sum/pallas_call | solution.py:376
  3.0 2.5 %collective-permute-start.1 = (f32[56,128]{1,0:T(8,128)S(1)}, f32[56,128]{1,0:T(8,128)S(1)}, u32[]{:S(2)}, u32[]{:S(2)}) collective-permute-start(f32[56,128]{1,0:T(8,128)S(1)} %get-tuple-element.26.tops_b.rest_0_), channel_id=1, source_target_pairs={{0,24},{8,16},{16,8},{24,0},{1,25},{9,17},{17,9},{25,1},{2,26},{10... | collective-permute-start | bytes 86024 | tf_op jit(solution)/shard_map/ppermute | solution.py:408
  5.5 0.7 %collective-permute-start = (f32[40,128]{1,0:T(8,128)S(1)}, f32[40,128]{1,0:T(8,128)S(1)}, u32[]{:S(2)}, u32[]{:S(2)}) collective-permute-start(f32[40,128]{1,0:T(8,128)S(1)} %get-tuple-element.23), channel_id=1, source_target_pairs={{0,8},{8,0},{16,24},{24,16},{1,9},{9,1},{17,25},{25,17},{2,10},{10... | collective-permute-start | bytes 61448 | tf_op jit(solution)/shard_map/ppermute | solution.py:407
  6.2 0.0 collective-permute-start.2
  6.2 3.7 %collective-permute-done.2.tops_a.rest_3_ = f32[24,128]{1,0:T(8,128)S(1)} collective-permute-done((f32[24,128]{1,0:T(8,128)S(1)}, f32[24,128]{1,0:T(8,128)S(1)}, u32[]{:S(2)}, u32[]{:S(2)}) %collective-permute-start.2) | collective-permute-done | bytes 12320 | tf_op jit(solution)/shard_map/ppermute | solution.py:410
  9.9 0.0 collective-permute-done.got_a.rest_1_
  9.9 0.0 collective-permute-done.1.got_b.tops_m.rest_2_
  9.9 1.4 %forcing.1 = f32[8,48,128]{2,1,0:T(8,128)} custom-call(f32[256,128]{1,0:T(8,128)S(1)} %get-tuple-element.24.tt, f32[256,128]{1,0:T(8,128)S(1)} %get-tuple-element.25.kt, f32[40,128]{1,0:T(8,128)S(1)} %collective-permute-done.got_a.rest_1_, f32[56,128]{1,0:T(8,128)S(1)} %collective-permute-done.1.got_b.tops_m.rest_2_, ...), custom_call_target="tpu_custom_call" | custom-call | tf_op jit(solution)/shard_map/forcing/pallas_call | solution.py:421
  11.3 5.8 %all-to-all-start = ((f32[8,48,128]{2,1,0:T(8,128)}), f32[8,48,128]{2,1,0:T(8,128)S(1)}, u32[]{:S(2)}, u32[]{:S(2)}) async-start(f32[8,48,128]{2,1,0:T(8,128)} %forcing.1), calls=%async_computation | async-start | bytes 393216 | tf_op jit(solution)/shard_map/all_to_all | solution.py:430
  17.1 3.1 %collective-permute-start.5 = (f32[56,128]{1,0:T(8,128)S(1)}, f32[56,128]{1,0:T(8,128)S(1)}, u32[]{:S(2)}, u32[]{:S(2)}) collective-permute-start(f32[56,128]{1,0:T(8,128)S(1)} %get-tuple-element.34), channel_id=1, source_target_pairs={{0,31},{1,2},{2,1},{3,4},{4,3},{5,6},{6,5},{7,8},{8,7},{9,10},{10,... | collective-permute-start | bytes 86024 | tf_op jit(solution)/shard_map/ppermute | solution.py:433
  20.2 0.4 %collective-permute-start.4 = (f32[56,128]{1,0:T(8,128)S(1)}, f32[56,128]{1,0:T(8,128)S(1)}, u32[]{:S(2)}, u32[]{:S(2)}) collective-permute-start(f32[56,128]{1,0:T(8,128)S(1)} %get-tuple-element.33), channel_id=1, source_target_pairs={{0,1},{1,0},{2,3},{3,2},{4,5},{5,4},{6,7},{7,6},{8,9},{9,8},{10,11... | collective-permute-start | bytes 86024 | tf_op jit(solution)/shard_map/ppermute | solution.py:432
  20.6 1.5 %collective-permute-start.3 = (f32[48,128]{1,0:T(8,128)S(1)}, f32[48,128]{1,0:T(8,128)S(1)}, u32[]{:S(2)}, u32[]{:S(2)}) collective-permute-start(f32[48,128]{1,0:T(8,128)S(1)} %get-tuple-element.31), channel_id=1, source_target_pairs={{0,24},{8,16},{16,8},{24,0},{1,25},{9,17},{17,9},{25,1},{2,26},{10... | collective-permute-start | bytes 73736 | tf_op jit(solution)/shard_map/ppermute | solution.py:434
  22.0 1.9 %collective-permute-done.3.got_d.fold = f32[48,128]{1,0:T(8,128)S(1)} collective-permute-done((f32[48,128]{1,0:T(8,128)S(1)}, f32[48,128]{1,0:T(8,128)S(1)}, u32[]{:S(2)}, u32[]{:S(2)}) %collective-permute-start.3) | collective-permute-done | bytes 24608 | tf_op jit(solution)/shard_map/ppermute | solution.py:434
  23.9 1.1 %all-to-all-done.got = f32[8,48,128]{2,1,0:T(8,128)S(1)} async-done(((f32[8,48,128]{2,1,0:T(8,128)}), f32[8,48,128]{2,1,0:T(8,128)S(1)}, u32[]{:S(2)}, u32[]{:S(2)}) %all-to-all-start) | async-done | bytes 196640 | tf_op jit(solution)/shard_map/all_to_all | solution.py:430
  25.0 0.0 collective-permute-done.5.rows_b
  25.0 0.0 collective-permute-done.4.rows_a
  25.0 0.0 copy-done
  25.0 0.0 copy-done.1
  25.0 1.6 %krylov.1 = (f32[4,32,1024]{2,1,0:T(8,128)S(1)}, f32[32,128]{1,0:T(8,128)}) custom-call(s32[32,32]{1,0:T(8,128)S(1)} %copy-done.1, f32[8,48,128]{2,1,0:T(8,128)S(1)} %all-to-all-done.got, f32[32,1024]{1,0:T(8,128)S(1)} %copy-done, f32[56,128]{1,0:T(8,128)S(1)} %collective-permute-done.4.rows_a, f32[56,128]{1,0:T(8,128)S(1)} %collective-permute-done.5.rows_b), custom_call_target="tpu_custom_call" | custom-call | tf_op jit(solution)/shard_map/krylov/pallas_call | solution.py:448
  26.6 3.2 %all-to-all-start.1 = ((f32[32,1,128]{2,1,0:T(1,128)}), f32[32,1,128]{2,1,0:T(1,128)S(1)}, u32[]{:S(2)}, u32[]{:S(2)}) async-start(f32[32,1,128]{2,1,0:T(1,128)} %bitcast.1), calls=%async_computation.1 | async-start | bytes 32768 | tf_op jit(solution)/shard_map/all_to_all | solution.py:456
  29.8 2.9 %tracer.1 = f32[16,128,256]{2,1,0:T(8,128)} custom-call(f32[16,128,256]{2,1,0:T(8,128)S(1)} %get-tuple-element.20.theta, f32[128,256]{1,0:T(8,128)S(1)} %get-tuple-element.21.ocean, f32[128,256]{1,0:T(8,128)S(1)} %get-tuple-element.22.coef, f32[40,128]{1,0:T(8,128)S(1)} %collective-permute-done.got_a.rest_1_, ...), custom_call_target="tpu_custom_call" | custom-call | flops 6291456 | bytes 4194304 | tf_op jit(solution)/shard_map/tracer/pallas_call | solution.py:437
  32.7 4.2 %all-to-all-done.1 = f32[32,1,128]{2,1,0:T(1,128)S(1)} async-done(((f32[32,1,128]{2,1,0:T(1,128)}), f32[32,1,128]{2,1,0:T(1,128)S(1)}, u32[]{:S(2)}, u32[]{:S(2)}) %all-to-all-start.1) | async-done | bytes 16416 | tf_op jit(solution)/shard_map/all_to_all | solution.py:456
  36.8 0.8 %combine.1 = f32[32,1024]{1,0:T(8,128)} custom-call(f32[32,128]{1,0:T(8,128)S(1)} %bitcast.4, f32[4,32,1024]{2,1,0:T(8,128)S(1)} %get-tuple-element.37.basis), custom_call_target="tpu_custom_call" | custom-call | tf_op jit(solution)/shard_map/combine/pallas_call | solution.py:457
Async XLA Ops:
  0.6 24.3 %copy-start = (f32[32,1024]{1,0:T(8,128)S(1)}, f32[32,1024]{1,0:T(8,128)}, u32[]{:S(2)}) copy-start(f32[32,1024]{1,0:T(8,128)} %diag.1) | copy-start | bytes 393220
  0.6 24.3 %copy-start.1 = (s32[32,32]{1,0:T(8,128)S(1)}, s32[32,32]{1,0:T(8,128)}, u32[]{:S(2)}) copy-start(s32[32,32]{1,0:T(8,128)} %table.1) | copy-start | bytes 12292
  3.0 6.8 %collective-permute-start.1 = (f32[56,128]{1,0:T(8,128)S(1)}, f32[56,128]{1,0:T(8,128)S(1)}, u32[]{:S(2)}, u32[]{:S(2)}) collective-permute-start(f32[56,128]{1,0:T(8,128)S(1)} %get-tuple-element.26.tops_b.rest_0_), channel_id=1, source_target_pairs={{0,24},{8,16},{16,8},{24,0},{1,25},{9,17},{17,9},{25,1},{2,26},{10... | collective-permute-start | bytes 86024 | tf_op jit(solution)/shard_map/ppermute | solution.py:408
  5.5 4.4 %collective-permute-start = (f32[40,128]{1,0:T(8,128)S(1)}, f32[40,128]{1,0:T(8,128)S(1)}, u32[]{:S(2)}, u32[]{:S(2)}) collective-permute-start(f32[40,128]{1,0:T(8,128)S(1)} %get-tuple-element.23), channel_id=1, source_target_pairs={{0,8},{8,0},{16,24},{24,16},{1,9},{9,1},{17,25},{25,17},{2,10},{10... | collective-permute-start | bytes 61448 | tf_op jit(solution)/shard_map/ppermute | solution.py:407
  6.2 3.7 %collective-permute-start.2 = (f32[24,128]{1,0:T(8,128)S(1)}, f32[24,128]{1,0:T(8,128)S(1)}, u32[]{:S(2)}, u32[]{:S(2)}) collective-permute-start(f32[24,128]{1,0:T(8,128)S(1)} %get-tuple-element.27), channel_id=1, source_target_pairs={{0,16},{8,24},{16,0},{24,8},{1,17},{9,25},{17,1},{25,9},{2,18},{10... | collective-permute-start | bytes 36872 | tf_op jit(solution)/shard_map/ppermute | solution.py:410
  11.3 13.7 %all-to-all-start = ((f32[8,48,128]{2,1,0:T(8,128)}), f32[8,48,128]{2,1,0:T(8,128)S(1)}, u32[]{:S(2)}, u32[]{:S(2)}) async-start(f32[8,48,128]{2,1,0:T(8,128)} %forcing.1), calls=%async_computation | async-start | bytes 393216 | tf_op jit(solution)/shard_map/all_to_all | solution.py:430
  17.1 7.9 %collective-permute-start.5 = (f32[56,128]{1,0:T(8,128)S(1)}, f32[56,128]{1,0:T(8,128)S(1)}, u32[]{:S(2)}, u32[]{:S(2)}) collective-permute-start(f32[56,128]{1,0:T(8,128)S(1)} %get-tuple-element.34), channel_id=1, source_target_pairs={{0,31},{1,2},{2,1},{3,4},{4,3},{5,6},{6,5},{7,8},{8,7},{9,10},{10,... | collective-permute-start | bytes 86024 | tf_op jit(solution)/shard_map/ppermute | solution.py:433
  20.2 4.8 %collective-permute-start.4 = (f32[56,128]{1,0:T(8,128)S(1)}, f32[56,128]{1,0:T(8,128)S(1)}, u32[]{:S(2)}, u32[]{:S(2)}) collective-permute-start(f32[56,128]{1,0:T(8,128)S(1)} %get-tuple-element.33), channel_id=1, source_target_pairs={{0,1},{1,0},{2,3},{3,2},{4,5},{5,4},{6,7},{7,6},{8,9},{9,8},{10,11... | collective-permute-start | bytes 86024 | tf_op jit(solution)/shard_map/ppermute | solution.py:432
  20.6 3.3 %collective-permute-start.3 = (f32[48,128]{1,0:T(8,128)S(1)}, f32[48,128]{1,0:T(8,128)S(1)}, u32[]{:S(2)}, u32[]{:S(2)}) collective-permute-start(f32[48,128]{1,0:T(8,128)S(1)} %get-tuple-element.31), channel_id=1, source_target_pairs={{0,24},{8,16},{16,8},{24,0},{1,25},{9,17},{17,9},{25,1},{2,26},{10... | collective-permute-start | bytes 73736 | tf_op jit(solution)/shard_map/ppermute | solution.py:434
  26.6 10.2 %all-to-all-start.1 = ((f32[32,1,128]{2,1,0:T(1,128)}), f32[32,1,128]{2,1,0:T(1,128)S(1)}, u32[]{:S(2)}, u32[]{:S(2)}) async-start(f32[32,1,128]{2,1,0:T(1,128)} %bitcast.1), calls=%async_computation.1 | async-start | bytes 32768 | tf_op jit(solution)/shard_map/all_to_all | solution.py:456

commit v4 on v3

--- a/solution.py
+++ b/solution.py
@@ -51,7 +51,7 @@
     return mat(mat(pick_rows, table), pick_cols)
 
 
-def sum_kernel(cell, weight_hbm, table_hbm, theta_hbm, kappa_hbm, diag_hbm, theta, ocean, coef, tt, kt, pay_a, pay_b, pay_c, pay_d, row_a, row_b, kappa, corner, rim, table, weight, sems):
+def sum_kernel(cell, weight_hbm, table_hbm, theta_hbm, kappa_hbm, diag_hbm, theta, ocean, coef, tt, kt, pay_a, pay_b, pay_c, row_a, row_b, ns_b, kappa, corner, rim, table, weight, sems):
     levels, cy, cx = theta.shape
     width, full = diag_hbm.shape
     copies = [
@@ -83,7 +83,7 @@
         w = rim[0, :RIM, c * cy : (c + 1) * cy]
         e = rim[1, EDGE - RIM :, c * cy : (c + 1) * cy]
         row_a[at : at + RIM, :] = jnp.where(even_row, e, w)
-        row_b[at : at + RIM, :] = jnp.where(even_row, w, e)
+        row_b[c * RIM : (c + 1) * RIM, :] = jnp.where(even_row, w, e)
         at += RIM
     copies[2].wait()
     kappas = kappa[...]
@@ -109,12 +109,12 @@
     sidest = (sides * jnp.where(lane < levels, mask[:, :1], mask[:, cx - 1 :])).T
     west, east = sidest[:levels], sidest[levels : 2 * levels]
     pay_a[2 * EDGE : 2 * EDGE + levels, :] = jnp.where(even, east, west)
-    pay_d[:levels, :] = jnp.where(even, west, east)
+    pay_b[2 * EDGE : 2 * EDGE + levels, :] = jnp.where(even, west, east)
     for at, turned in ((0, ttv), (EDGE, ktv)):
         w, e = turned[:EDGE], turned[cx - EDGE :]
         pay_a[at : at + EDGE, :] = jnp.where(even, e, w)
         pay_b[at : at + EDGE, :] = jnp.where(even, w, e)
-    at = 2 * EDGE
+    at = 2 * EDGE + levels
     flip = ones_at(iota((cx, cx), 0) + iota((cx, cx), 1) == cx - 1)
     both = jnp.concatenate([t[cy - EDGE :], kappas[cy - EDGE :, :]], axis=0)
     turned = mat(both, flip, EXACT)
@@ -126,7 +126,7 @@
             for c in range(nt):
                 to_b = at + (base // EDGE * nt + c) * EDGE + r
                 pay_b[to_b : to_b + 1, :] = row[:, c * cy : (c + 1) * cy]
-    pay_a[at + levels :, :] = column
+    pay_a[at:, :] = column
     pay_c[2 * EDGE :, :] = column
     pay_b[at + 2 * nt * EDGE :, :] = column
     top = theta[:, cy - 1, :] * mask[cy - 1 :, :]
@@ -134,8 +134,7 @@
     for c in range(nt):
         t, b = top[:, c * cy : (c + 1) * cy], bottom[:, c * cy : (c + 1) * cy]
         row_a[c * levels : (c + 1) * levels, :] = jnp.where(even_row, t, b)
-        row_b[c * levels : (c + 1) * levels, :] = jnp.where(even_row, b, t)
-        pay_d[(c + 1) * levels : (c + 2) * levels, :] = t
+        ns_b[c * levels : (c + 1) * levels, :] = jnp.where(even_row, b, t)
 
 
 def forcing_kernel(last, width, places, tt, kt, got_a, got_b, tops_m, tops_a, tops_b, *rest):
@@ -240,7 +239,7 @@
 
     even_row = lax.rem(lat, 2) == 0
     rim = full // cy * RIM
-    d_a, d_b = rows_a[start : start + rim, :], rows_b[start : start + rim, :]
+    d_a, d_b = rows_a[start : start + rim, :], rows_b[...]
     d_east, d_west = jnp.where(even_row, d_a, d_b), jnp.where(even_row, d_b, d_a)
     unused = jnp.zeros((EDGE - 2 * RIM, cy), jnp.float32)
     d_ends = [
@@ -318,21 +317,25 @@
     psi[...] = total
 
 
-def tracer_kernel(last, start, theta, ocean, coef, got_a, got_d, rows_a, rows_b, fold, out_hbm, out, sems):
+def rim_kernel(rows, out):
+    out[...] = rows[...]
+
+
+def tracer_kernel(last, theta, ocean, coef, got_a, got_b, rows_a, rows_b, out_hbm, out, sems):
     levels, cy, cx = theta.shape
     lon, lat = lax.axis_index("lon"), lax.axis_index("lat")
     even = lax.rem(lon, 2) == 0
-    a, b = got_a[2 * EDGE : 2 * EDGE + levels, :], got_d[:levels, :]
+    a, b = got_a[2 * EDGE : 2 * EDGE + levels, :], got_b[2 * EDGE : 2 * EDGE + levels, :]
     both = jnp.concatenate([jnp.where(even, a, b), jnp.where(even, b, a), jnp.zeros((128 - 2 * levels, cy), jnp.float32)], axis=0)
     sides = both.T
     even_row = lax.rem(lat, 2) == 0
 
-    def joined(ref, at=0):
-        return jnp.concatenate([ref[at + c * levels : at + (c + 1) * levels, :] for c in range(cx // cy)], axis=1)
+    def joined(ref):
+        return jnp.concatenate([ref[c * levels : (c + 1) * levels, :] for c in range(cx // cy)], axis=1)
 
     a, b = joined(rows_a), joined(rows_b)
     flip = ones_at(iota((cx, cx), 0) + iota((cx, cx), 1) == cx - 1)
-    north = jnp.where(lat == last, mat(joined(fold, start), flip, EXACT), jnp.where(even_row, a, b))
+    north = jnp.where(lat == last, mat(b, flip, EXACT), jnp.where(even_row, a, b))
     south = jnp.where(lat == 0, 0.0, jnp.where(even_row, b, a))
 
     lane = iota((cy, 128), 1)
@@ -370,10 +373,10 @@
     shape = lambda *dims: jax.ShapeDtypeStruct(dims, f32)
 
     nt = cx // cy
-    head = 2 * EDGE
+    head = 2 * EDGE + levels
     own = (2 * nt + 1) * EDGE
     rim = RIM * (full // cy)
-    held, ocean, coef, tt, kt, pay_a, pay_b, pay_c, pay_d, row_a, row_b = pl.pallas_call(
+    held, ocean, coef, tt, kt, pay_a, pay_b, pay_c, row_a, row_b, ns_b = pl.pallas_call(
         functools.partial(sum_kernel, cell),
         in_specs=[HBM] * 5,
         out_specs=[VMEM] * 11,
@@ -383,12 +386,12 @@
             shape(cy, cx),
             shape(cx, cy),
             shape(cx, cy),
-            shape(head + levels + EDGE, cy),
+            shape(head + EDGE, cy),
             shape(head + own, cy),
             shape(3 * EDGE, cy),
-            shape((nt + 1) * levels, cy),
             shape(nt * levels + rim, cy),
-            shape(nt * levels + rim, cy),
+            shape(rim, cy),
+            shape(nt * levels, cy),
         ],
         scratch_shapes=[
             pltpu.VMEM((cy, cx), f32),
@@ -411,7 +414,7 @@
         folds = (got_b, got_c, pay_b)
         corners = (pay_b, got_a, got_b, got_c)
         tail = head + own - EDGE
-        places = (head, 0, head, (tail, head + levels, tail, 2 * EDGE))
+        places = (head, 0, head, (tail, head, tail, 2 * EDGE))
     else:
         got_c = lax.ppermute(pay_c, "lon", [(i, i ^ 1) for i in range(lons)])
         tops = lax.ppermute(jnp.concatenate([pay_b[head:], got_c, got_b[head:]], axis=0), "lon", mirror)
@@ -426,24 +429,37 @@
         compiler_params=PARAMS,
         name="forcing",
     )(tt, kt, got_a, got_b, *folds, *corners)
-    chunks, row_a, pay_d = lax.optimization_barrier((chunks, row_a, pay_d))
+    chunks, row_a, ns_b = lax.optimization_barrier((chunks, row_a, ns_b))
     got = lax.all_to_all(chunks, "lat", split_axis=0, concat_axis=0, tiled=True)
 
+    rows_b = lax.ppermute(row_b, joint, [(i, (i + 1 if i % 2 else i - 1) % devices) for i in range(devices)])
+    rim_b = pl.pallas_call(
+        rim_kernel,
+        in_specs=[VMEM],
+        out_specs=VMEM,
+        out_shape=shape(rim, cy),
+        compiler_params=PARAMS,
+        cost_estimate=pl.CostEstimate(flops=10**11, bytes_accessed=0, transcendentals=0),
+        name="rim",
+    )(rows_b)
+    row_a, ns_b, rim_b = lax.optimization_barrier((row_a, ns_b, rim_b))
     rows_a = lax.ppermute(row_a, joint, [(i, i ^ 1) for i in range(devices)])
-    rows_b = lax.ppermute(row_b, joint, [(i, (i + 1 if i % 2 else i - 1) % devices) for i in range(devices)])
-    got_d = lax.ppermute(pay_d, "lon", pairs_b)
-    got, got_d = lax.optimization_barrier((got, got_d))
-    fold = got_d if pairs_b == mirror else lax.ppermute(pay_d, "lon", mirror)
+    second = []
+    for lon in range(lons):
+        second += [(lon * lats + lat, (lons - 1 - lon) * lats + lat) for lat in (0, last)]
+        second += [(lon * lats + lat, lon * lats + (lat + 1 if lat % 2 else lat - 1)) for lat in range(1, last)]
+    beyond = lax.ppermute(ns_b, joint, second)
+    got, beyond = lax.optimization_barrier((got, beyond))
     new_theta = pl.pallas_call(
-        functools.partial(tracer_kernel, last, levels),
-        in_specs=[VMEM] * 8,
+        functools.partial(tracer_kernel, last),
+        in_specs=[VMEM] * 7,
         out_specs=HBM,
         out_shape=shape(levels, cy, cx),
         scratch_shapes=[pltpu.VMEM((levels, cy, cx), f32), pltpu.SemaphoreType.DMA((levels // 2,))],
         compiler_params=PARAMS,
         cost_estimate=pl.CostEstimate(flops=12 * levels * cy * cx, bytes_accessed=8 * levels * cy * cx, transcendentals=0),
         name="tracer",
-    )(held, ocean, coef, got_a, got_d, rows_a, rows_b, fold)
+    )(held, ocean, coef, got_a, got_b, rows_a, beyond)
 
     basis, gram = pl.pallas_call(
         functools.partial(krylov_kernel, cell, nt * levels),
@@ -452,7 +468,7 @@
         out_shape=[shape(ITERS, width, full), shape(devices, 128)],
         compiler_params=PARAMS,
         name="krylov",
-    )(land_blocks, got, diag, rows_a, rows_b)
+    )(land_blocks, got, diag, rows_a, rim_b)
     gram = lax.all_to_all(gram, joint, split_axis=0, concat_axis=0, tiled=True)
     psi = pl.pallas_call(
         combine_kernel,

time: 37.9 us -> 37.5 us (0.989)
  waiting for transfers between devices: 10.8 us -> 9.8 us
  starting transfers between devices: 17.1 us -> 17.6 us
    ppermute x1, waiting for transfers between devices: 3.65 us -> 0.01 us  [per_device(): got_c = lax.ppermute(pay_c, 'lon', [(i, i ^ 2) for i in range(lons)])]
    ppermute x1, starting transfers between devices: 3.09 us -> 5.28 us  [per_device(): lax.ppermute(row_b, joint, [(i, (i + 1 if i % 2 else i - 1) % devices) fo...]
    ppermute x1, starting transfers between devices: 0.39 us -> 2.07 us  [per_device(): rows_a = lax.ppermute(row_a, joint, [(i, i ^ 1) for i in range(devices)])]
    all_to_all x1, starting transfers between devices: 5.81 us -> 4.17 us  [per_device(): got = lax.all_to_all(chunks, 'lat', split_axis=0, concat_axis=0, tiled=True)]
    ppermute x1, starting transfers between devices: 1.47 us -> 0.01 us  [per_device(): beyond = lax.ppermute(ns_b, joint, second)]
    all_to_all x1, waiting for transfers between devices: 1.06 us -> 2.52 us  [per_device(): got = lax.all_to_all(chunks, 'lat', split_axis=0, concat_axis=0, tiled=True)]
    ppermute x1, waiting for transfers between devices: 1.88 us -> 3.16 us  [per_device(): beyond = lax.ppermute(ns_b, joint, second)]
    pallas_call x1 -> x2, Pallas kernels: 2.88 us -> 2.92 us  [the longest x1 2.92 us: per_device(): pl.pallas_call(functools.partial(tracer_kernel, last), in_specs=[VMEM] *...]
  transfers between devices with their start and end apart: 8 -> 8, of which waited for: 4 -> 3; matrix products, arithmetic and copies ran while one was open for 0% -> 0% of each run, Pallas kernels for 8% -> 12%
where the time goes in v4:
time: 37.5 us; the launch traced here: 37.3 us
  starting transfers between devices  17.6 us (47%)
  waiting for transfers between devices  9.8 us (26%)
  Pallas kernels  9.11 us (24%)
  between operations  0.7 us (2%)
    ppermute x1, starting transfers between devices, per_device(): lax.ppermute(row_b, joint, [(i, (i + 1 if i % 2 else i - 1) % devices) fo...  5.28 us
    all_to_all x1, starting transfers between devices, per_device(): got = lax.all_to_all(chunks, 'lat', split_axis=0, concat_axis=0, tiled=True)  4.17 us
    all_to_all x1, waiting for transfers between devices, per_device(): gram = lax.all_to_all(gram, joint, split_axis=0, concat_axis=0, tiled=True)  4.11 us
    ppermute x1, waiting for transfers between devices, per_device(): beyond = lax.ppermute(ns_b, joint, second)  3.16 us
    all_to_all x1, starting transfers between devices, per_device(): gram = lax.all_to_all(gram, joint, split_axis=0, concat_axis=0, tiled=True)  2.93 us
    pallas_call x1, Pallas kernels, per_device(): pl.pallas_call(functools.partial(tracer_kernel, last), in_specs=[VMEM] *...  2.92 us
    all_to_all x1, waiting for transfers between devices, per_device(): got = lax.all_to_all(chunks, 'lat', split_axis=0, concat_axis=0, tiled=True)  2.52 us
    ppermute x1, starting transfers between devices, per_device(): got_b = lax.ppermute(pay_b, 'lon', pairs_b)  2.47 us
  transfers between devices with their start and end apart: 8, of which 3 were waited for; matrix products, arithmetic and copies ran while one was open for 0% of the time, Pallas kernels for 12%

profile of v4, /device:TPU:0, one launch (start us, length us, event | category | flops | bytes accessed | tf_op | source)
XLA Modules:
  0.0 37.3 jit_solution(17370565591898955825)
XLA Ops:
  0.6 2.3 %level_sum.1 = (f32[16,128,256]{2,1,0:T(8,128)S(1)}, f32[128,256]{1,0:T(8,128)S(1)}, f32[128,256]{1,0:T(8,128)S(1)}, f32[256,128]{1,0:T(8,128)S(1)}, f32[256,128...) custom-call(f32[16]{0:T(128)} %weight_hbm.1, ...), custom_call_target="tpu_custom_call" | custom-call | tf_op jit(solution)/shard_map/level_sum/pallas_call | solution.py:379
  3.0 2.5 %collective-permute-start.1 = (f32[72,128]{1,0:T(8,128)S(1)}, f32[72,128]{1,0:T(8,128)S(1)}, u32[]{:S(2)}, u32[]{:S(2)}) collective-permute-start(f32[72,128]{1,0:T(8,128)S(1)} %get-tuple-element.27.tops_b.rest_0_), channel_id=1, source_target_pairs={{0,24},{8,16},{16,8},{24,0},{1,25},{9,17},{17,9},{25,1},{2,26},{10... | collective-permute-start | bytes 110600 | tf_op jit(solution)/shard_map/ppermute | solution.py:411
  5.4 0.7 %collective-permute-start = (f32[40,128]{1,0:T(8,128)S(1)}, f32[40,128]{1,0:T(8,128)S(1)}, u32[]{:S(2)}, u32[]{:S(2)}) collective-permute-start(f32[40,128]{1,0:T(8,128)S(1)} %get-tuple-element.26), channel_id=1, source_target_pairs={{0,8},{8,0},{16,24},{24,16},{1,9},{9,1},{17,25},{25,17},{2,10},{10... | collective-permute-start | bytes 61448 | tf_op jit(solution)/shard_map/ppermute | solution.py:410
  6.1 0.0 collective-permute-start.2
  6.2 5.3 %collective-permute-start.3 = (f32[24,128]{1,0:T(8,128)S(1)}, f32[24,128]{1,0:T(8,128)S(1)}, u32[]{:S(2)}, u32[]{:S(2)}) collective-permute-start(f32[24,128]{1,0:T(8,128)S(1)} %get-tuple-element.35), channel_id=1, source_target_pairs={{0,31},{1,2},{2,1},{3,4},{4,3},{5,6},{6,5},{7,8},{8,7},{9,10},{10,... | collective-permute-start | bytes 36872 | tf_op jit(solution)/shard_map/ppermute | solution.py:435
  11.4 0.0 collective-permute-done.2.tops_a.rest_3_
  11.4 0.0 collective-permute-done.got_a.rest_1_
  11.4 0.0 collective-permute-done.1.got_b.tops_m.rest_2_
  11.5 1.4 %forcing.1 = f32[8,48,128]{2,1,0:T(8,128)} custom-call(f32[256,128]{1,0:T(8,128)S(1)} %get-tuple-element.28.tt, f32[256,128]{1,0:T(8,128)S(1)} %get-tuple-element.29.kt, f32[40,128]{1,0:T(8,128)S(1)} %collective-permute-done.got_a.rest_1_, f32[72,128]{1,0:T(8,128)S(1)} %collective-permute-done.1.got_b.tops_m.rest_2_, ...), custom_call_target="tpu_custom_call" | custom-call | tf_op jit(solution)/shard_map/forcing/pallas_call | solution.py:424
  12.8 4.2 %all-to-all-start = ((f32[8,48,128]{2,1,0:T(8,128)}), f32[8,48,128]{2,1,0:T(8,128)S(1)}, u32[]{:S(2)}, u32[]{:S(2)}) async-start(f32[8,48,128]{2,1,0:T(8,128)} %forcing.1), calls=%async_computation | async-start | bytes 393216 | tf_op jit(solution)/shard_map/all_to_all | solution.py:433
  17.0 0.0 copy-start
  17.0 0.0 copy-start.1
  17.0 0.0 collective-permute-done.3.rows
  17.0 2.1 %collective-permute-start.4 = (f32[56,128]{1,0:T(8,128)S(1)}, f32[56,128]{1,0:T(8,128)S(1)}, u32[]{:S(2)}, u32[]{:S(2)}) collective-permute-start(f32[56,128]{1,0:T(8,128)S(1)} %get-tuple-element.36), channel_id=1, source_target_pairs={{0,1},{1,0},{2,3},{3,2},{4,5},{5,4},{6,7},{7,6},{8,9},{9,8},{10,11... | collective-permute-start | bytes 86024 | tf_op jit(solution)/shard_map/ppermute | solution.py:446
  19.1 0.0 collective-permute-start.5
  19.1 3.2 %collective-permute-done.5.rows_b = f32[32,128]{1,0:T(8,128)S(1)} collective-permute-done((f32[32,128]{1,0:T(8,128)S(1)}, f32[32,128]{1,0:T(8,128)S(1)}, u32[]{:S(2)}, u32[]{:S(2)}) %collective-permute-start.5) | collective-permute-done | bytes 16416 | tf_op jit(solution)/shard_map/ppermute | solution.py:451
  22.3 2.5 %all-to-all-done.got = f32[8,48,128]{2,1,0:T(8,128)S(1)} async-done(((f32[8,48,128]{2,1,0:T(8,128)}), f32[8,48,128]{2,1,0:T(8,128)S(1)}, u32[]{:S(2)}, u32[]{:S(2)}) %all-to-all-start) | async-done | bytes 196640 | tf_op jit(solution)/shard_map/all_to_all | solution.py:433
  24.8 0.0 collective-permute-done.4.rows_a
  24.8 0.0 copy-done
  24.8 0.0 copy-done.1
  24.8 1.7 %krylov.1 = (f32[4,32,1024]{2,1,0:T(8,128)S(1)}, f32[32,128]{1,0:T(8,128)}) custom-call(s32[32,32]{1,0:T(8,128)S(1)} %copy-done.1, f32[8,48,128]{2,1,0:T(8,128)S(1)} %all-to-all-done.got, f32[32,1024]{1,0:T(8,128)S(1)} %copy-done, f32[56,128]{1,0:T(8,128)S(1)} %collective-permute-done.4.rows_a, f32[24,128]{1,0:T(8,128)S(1)} %rim.1.rows_b), custom_call_target="tpu_custom_call" | custom-call | tf_op jit(solution)/shard_map/krylov/pallas_call | solution.py:464
  26.5 2.9 %all-to-all-start.1 = ((f32[32,1,128]{2,1,0:T(1,128)}), f32[32,1,128]{2,1,0:T(1,128)S(1)}, u32[]{:S(2)}, u32[]{:S(2)}) async-start(f32[32,1,128]{2,1,0:T(1,128)} %bitcast.1), calls=%async_computation.1 | async-start | bytes 32768 | tf_op jit(solution)/shard_map/all_to_all | solution.py:472
  29.4 2.9 %tracer.1 = f32[16,128,256]{2,1,0:T(8,128)} custom-call(f32[16,128,256]{2,1,0:T(8,128)S(1)} %get-tuple-element.23.theta, f32[128,256]{1,0:T(8,128)S(1)} %get-tuple-element.24.ocean, f32[128,256]{1,0:T(8,128)S(1)} %get-tuple-element.25.coef, f32[40,128]{1,0:T(8,128)S(1)} %collective-permute-done.got_a.rest_1_, ...), custom_call_target="tpu_custom_call" | custom-call | flops 6291456 | bytes 4194304 | tf_op jit(solution)/shard_map/tracer/pallas_call | solution.py:453
  32.3 4.1 %all-to-all-done.1 = f32[32,1,128]{2,1,0:T(1,128)S(1)} async-done(((f32[32,1,128]{2,1,0:T(1,128)}), f32[32,1,128]{2,1,0:T(1,128)S(1)}, u32[]{:S(2)}, u32[]{:S(2)}) %all-to-all-start.1) | async-done | bytes 16416 | tf_op jit(solution)/shard_map/all_to_all | solution.py:472
  36.4 0.8 %combine.1 = f32[32,1024]{1,0:T(8,128)} custom-call(f32[32,128]{1,0:T(8,128)S(1)} %bitcast.4, f32[4,32,1024]{2,1,0:T(8,128)S(1)} %get-tuple-element.43.basis), custom_call_target="tpu_custom_call" | custom-call | tf_op jit(solution)/shard_map/combine/pallas_call | solution.py:473
  (1 shorter events, 0.0 us)
Async XLA Ops:
  3.0 8.5 %collective-permute-start.1 = (f32[72,128]{1,0:T(8,128)S(1)}, f32[72,128]{1,0:T(8,128)S(1)}, u32[]{:S(2)}, u32[]{:S(2)}) collective-permute-start(f32[72,128]{1,0:T(8,128)S(1)} %get-tuple-element.27.tops_b.rest_0_), channel_id=1, source_target_pairs={{0,24},{8,16},{16,8},{24,0},{1,25},{9,17},{17,9},{25,1},{2,26},{10... | collective-permute-start | bytes 110600 | tf_op jit(solution)/shard_map/ppermute | solution.py:411
  5.4 6.0 %collective-permute-start = (f32[40,128]{1,0:T(8,128)S(1)}, f32[40,128]{1,0:T(8,128)S(1)}, u32[]{:S(2)}, u32[]{:S(2)}) collective-permute-start(f32[40,128]{1,0:T(8,128)S(1)} %get-tuple-element.26), channel_id=1, source_target_pairs={{0,8},{8,0},{16,24},{24,16},{1,9},{9,1},{17,25},{25,17},{2,10},{10... | collective-permute-start | bytes 61448 | tf_op jit(solution)/shard_map/ppermute | solution.py:410
  6.1 5.3 %collective-permute-start.2 = (f32[24,128]{1,0:T(8,128)S(1)}, f32[24,128]{1,0:T(8,128)S(1)}, u32[]{:S(2)}, u32[]{:S(2)}) collective-permute-start(f32[24,128]{1,0:T(8,128)S(1)} %get-tuple-element.30), channel_id=1, source_target_pairs={{0,16},{8,24},{16,0},{24,8},{1,17},{9,25},{17,1},{25,9},{2,18},{10... | collective-permute-start | bytes 36872 | tf_op jit(solution)/shard_map/ppermute | solution.py:413
  6.2 10.9 %collective-permute-start.3 = (f32[24,128]{1,0:T(8,128)S(1)}, f32[24,128]{1,0:T(8,128)S(1)}, u32[]{:S(2)}, u32[]{:S(2)}) collective-permute-start(f32[24,128]{1,0:T(8,128)S(1)} %get-tuple-element.35), channel_id=1, source_target_pairs={{0,31},{1,2},{2,1},{3,4},{4,3},{5,6},{6,5},{7,8},{8,7},{9,10},{10,... | collective-permute-start | bytes 36872 | tf_op jit(solution)/shard_map/ppermute | solution.py:435
  12.8 12.0 %all-to-all-start = ((f32[8,48,128]{2,1,0:T(8,128)}), f32[8,48,128]{2,1,0:T(8,128)S(1)}, u32[]{:S(2)}, u32[]{:S(2)}) async-start(f32[8,48,128]{2,1,0:T(8,128)} %forcing.1), calls=%async_computation | async-start | bytes 393216 | tf_op jit(solution)/shard_map/all_to_all | solution.py:433
  17.0 7.8 %copy-start = (f32[32,1024]{1,0:T(8,128)S(1)}, f32[32,1024]{1,0:T(8,128)}, u32[]{:S(2)}) copy-start(f32[32,1024]{1,0:T(8,128)} %diag.1) | copy-start | bytes 393220
  17.0 7.8 %copy-start.1 = (s32[32,32]{1,0:T(8,128)S(1)}, s32[32,32]{1,0:T(8,128)}, u32[]{:S(2)}) copy-start(s32[32,32]{1,0:T(8,128)} %table.1) | copy-start | bytes 12292
  17.0 7.8 %collective-permute-start.4 = (f32[56,128]{1,0:T(8,128)S(1)}, f32[56,128]{1,0:T(8,128)S(1)}, u32[]{:S(2)}, u32[]{:S(2)}) collective-permute-start(f32[56,128]{1,0:T(8,128)S(1)} %get-tuple-element.36), channel_id=1, source_target_pairs={{0,1},{1,0},{2,3},{3,2},{4,5},{5,4},{6,7},{7,6},{8,9},{9,8},{10,11... | collective-permute-start | bytes 86024 | tf_op jit(solution)/shard_map/ppermute | solution.py:446
  19.1 3.2 %collective-permute-start.5 = (f32[32,128]{1,0:T(8,128)S(1)}, f32[32,128]{1,0:T(8,128)S(1)}, u32[]{:S(2)}, u32[]{:S(2)}) collective-permute-start(f32[32,128]{1,0:T(8,128)S(1)} %get-tuple-element.38), channel_id=1, source_target_pairs={{0,24},{7,31},{1,2},{2,1},{3,4},{4,3},{5,6},{6,5},{8,16},{15,23},{... | collective-permute-start | bytes 49160 | tf_op jit(solution)/shard_map/ppermute | solution.py:451
  26.5 10.0 %all-to-all-start.1 = ((f32[32,1,128]{2,1,0:T(1,128)}), f32[32,1,128]{2,1,0:T(1,128)S(1)}, u32[]{:S(2)}, u32[]{:S(2)}) async-start(f32[32,1,128]{2,1,0:T(1,128)} %bitcast.1), calls=%async_computation.1 | async-start | bytes 32768 | tf_op jit(solution)/shard_map/all_to_all | solution.py:472

commit v5 on v4

--- a/solution.py
+++ b/solution.py
@@ -51,7 +51,7 @@
     return mat(mat(pick_rows, table), pick_cols)
 
 
-def sum_kernel(cell, weight_hbm, table_hbm, theta_hbm, kappa_hbm, diag_hbm, theta, ocean, coef, tt, kt, pay_a, pay_b, pay_c, row_a, row_b, ns_b, kappa, corner, rim, table, weight, sems):
+def sum_kernel(cell, weight_hbm, table_hbm, theta_hbm, kappa_hbm, diag_hbm, theta, ocean, coef, tt, kt, ends, pay_a, pay_b, pay_c, row_a, row_b, ns_b, kappa, corner, rim, table, weight, sems):
     levels, cy, cx = theta.shape
     width, full = diag_hbm.shape
     copies = [
@@ -115,6 +115,11 @@
         pay_a[at : at + EDGE, :] = jnp.where(even, e, w)
         pay_b[at : at + EDGE, :] = jnp.where(even, w, e)
     at = 2 * EDGE + levels
+    rows = jnp.concatenate([t[:1], t[cy - 1 :], kappas[:1], kappas[cy - 1 :], jnp.zeros((EDGE - 4, cx), jnp.float32)], axis=0)
+    ends[...] = rows
+    pay_a[at : at + EDGE, :] = jnp.where(even, rows[:, cx - cy :], rows[:, :cy])
+    pay_b[at : at + EDGE, :] = jnp.where(even, rows[:, :cy], rows[:, cx - cy :])
+    at += EDGE
     flip = ones_at(iota((cx, cx), 0) + iota((cx, cx), 1) == cx - 1)
     both = jnp.concatenate([t[cy - EDGE :], kappas[cy - EDGE :, :]], axis=0)
     turned = mat(both, flip, EXACT)
@@ -137,49 +142,44 @@
         ns_b[c * levels : (c + 1) * levels, :] = jnp.where(even_row, b, t)
 
 
-def forcing_kernel(last, width, places, tt, kt, got_a, got_b, tops_m, tops_a, tops_b, *rest):
+def forcing_kernel(last, width, places, tt, kt, ends, got_a, got_b, tops_m, tops_a, tops_b, *rest):
     *corners, out = rest
-    at_m, at_a, at_b, at_corners = places
+    at_ends, at_m, at_a, at_b, at_corners = places
     cx, cy = tt.shape
     lon, lat = lax.axis_index("lon"), lax.axis_index("lat")
     even = lax.rem(lon, 2) == 0
     nt = cx // cy
 
-    stack = []
-    for which in (0, 1):
+    def sides(at):
+        a, b = got_a[at : at + EDGE, :], got_b[at : at + EDGE, :]
+        return jnp.where(even, b, a), jnp.where(even, a, b)
+
+    def extended(own, at):
+        left, right = sides(at)
+        return jnp.concatenate([left, own, right], axis=0)
+
+    t = extended(tt[...], 0)
+    k = extended(kt[...], EDGE)
+    lane = iota((cx + 2 * EDGE, cy), 1)
+    south = jnp.where(lane == 0, 0.0, turn(t, 1, 1))
+    north = jnp.where(lane == cy - 1, 0.0, turn(t, -1, 1))
+    f = t + k * (turn(t, 1, 0) + turn(t, -1, 0) + south + north - 4.0 * t)
+
+    def beyond(which):
         a = tops_a[at_a + which * EDGE : at_a + (which + 1) * EDGE, :]
         b_first = tops_b[at_b + which * nt * EDGE : at_b + (which * nt + 1) * EDGE, :]
         b_last = tops_b[at_b + (which * nt + nt - 1) * EDGE : at_b + (which * nt + nt) * EDGE, :]
-        stack.append(jnp.where(even, b_last, a))
-        for c in range(nt):
-            stack.append(tops_m[at_m + (which * nt + c) * EDGE : at_m + (which * nt + c + 1) * EDGE, :])
-        stack.append(jnp.where(even, a, b_first))
-    used = len(stack) * EDGE
-    stack = jnp.concatenate(stack + [jnp.zeros((cy - used, cy), jnp.float32)], axis=0).T
-    fold_lane = (iota((cy, cy), 1) < EDGE) & (lat == last)
-
-    def extended(own, at, which):
-        a = got_a[at : at + EDGE, :]
-        b = got_b[at : at + EDGE, :]
-        rows = jnp.concatenate([jnp.where(even, b, a), own, jnp.where(even, a, b)], axis=0)
-        first = which * (nt + 2)
-        tiles = [jnp.where(fold_lane, turn(stack, -(first + n) * EDGE, 1), 0.0) for n in range(nt + 2)]
-        fold = jnp.concatenate([tiles[0][cy - EDGE :]] + tiles[1:-1] + [tiles[-1][:EDGE]], axis=0)
-        return jnp.concatenate([rows, fold], axis=1)
-
-    t = extended(tt[...], 0, 0)
-    k = extended(kt[...], EDGE, 1)
-    f = t + k * (beside(t) - 4.0 * t)
-    rows = cx + 2 * EDGE
-    lane = iota((rows, cy), 1)
-    t0, k0 = t[:, :cy], k[:, :cy]
-    pack = jnp.where(lane == 0, t0, 0.0)
-    pack = jnp.where(lane == 1, turn(t0, 2, 1), pack)
-    pack = jnp.where(lane == 2, turn(k0, 2, 1), pack)
-    pack = jnp.where(lane == 3, turn(k0, 4, 1), pack)
-    pack = jnp.where((lane >= 4) & (lane < 8), turn(f[:, cy:], 4, 1), pack)
-    wide = -(-rows // 128) * 128
-    pack = jnp.concatenate([pack, jnp.zeros((wide - rows, cy), jnp.float32)], axis=0).T[:8]
+        middle = [tops_m[at_m + (which * nt + c) * EDGE : at_m + (which * nt + c + 1) * EDGE, :] for c in range(nt)]
+        return jnp.concatenate([jnp.where(even, b_last, a)] + middle + [jnp.where(even, a, b_first)], axis=1)
+
+    left, right = sides(at_ends)
+    row_ends = jnp.concatenate([left, ends[...], right], axis=1)
+    over, over_k = beyond(0), beyond(1)
+    row = iota(over.shape, 0)
+    below = jnp.where(row == 0, row_ends[1:2], turn(over, 1, 0))
+    over_f = over + over_k * (turn(over, 1, 1) + turn(over, -1, 1) + turn(over, -1, 0) + below - 4.0 * over)
+    row_ends = jnp.where((row == 1) & (lat == last), over[:1], row_ends)
+    pack = jnp.where(row < 4, row_ends, turn(over_f, 4, 0))
     low = iota((EDGE, cy), 0) < HALO
     corner = sum(ref[at : at + EDGE, :] for ref, at in zip(corners, at_corners))
     corner = jnp.where(low, turn(turn(corner, HALO, 0), 64, 1), corner)
@@ -188,7 +188,7 @@
         at = EDGE + d * width
         out[d, :width, :] = f[at : at + width, :cy]
         out[d, width : width + EDGE, :] = jnp.where(low, f[at + width : at + width + EDGE, :cy], f[at - EDGE : at, :cy])
-        out[d, width + EDGE :, :] = jnp.where(in_pack, turn(pack, -d * width, 1)[:, :128], corner)
+        out[d, width + EDGE :, :] = jnp.where(in_pack, turn(pack, EDGE - cy - d * width, 1)[:, :128], corner)
 
 
 def strip_order(columns, width):
@@ -213,14 +213,15 @@
     edges = strip_order(edges.T, width)
     from_south = edges * turn(edges, 9, 1)
     from_north = edges * turn(edges, -5, 1)
+    from_fold = edges * turn(edges, 2, 1)
     lane = iota((rows, cy), 1)
     parts = []
     for s in range(count):
         part = got[s, :rows, :]
         if s > 0:
             part = part + jnp.where(lane == 0, turn(from_south, -(8 * s + 2), 1), 0.0)
-        if s < count - 1:
-            part = part + jnp.where(lane == cy - 1, turn(from_north, cy - 1 - (8 * s + 3), 1), 0.0)
+        above = from_north if s < count - 1 else from_fold
+        part = part + jnp.where(lane == cy - 1, turn(above, cy - 1 - (8 * s + 3), 1), 0.0)
         parts.append(part)
     parts.append(jnp.where(lane < HALO, turn(edges, -(8 * (count - 1) + 4), 1), 0.0))
     f = jnp.concatenate(parts, axis=1)
@@ -373,19 +374,20 @@
     shape = lambda *dims: jax.ShapeDtypeStruct(dims, f32)
 
     nt = cx // cy
-    head = 2 * EDGE + levels
+    head = 3 * EDGE + levels
     own = (2 * nt + 1) * EDGE
     rim = RIM * (full // cy)
-    held, ocean, coef, tt, kt, pay_a, pay_b, pay_c, row_a, row_b, ns_b = pl.pallas_call(
+    held, ocean, coef, tt, kt, ends, pay_a, pay_b, pay_c, row_a, row_b, ns_b = pl.pallas_call(
         functools.partial(sum_kernel, cell),
         in_specs=[HBM] * 5,
-        out_specs=[VMEM] * 11,
+        out_specs=[VMEM] * 12,
         out_shape=[
             pltpu.VMEM((levels, cy, cx), f32),
             shape(cy, cx),
             shape(cy, cx),
             shape(cx, cy),
             shape(cx, cy),
+            shape(EDGE, cx),
             shape(head + EDGE, cy),
             shape(head + own, cy),
             shape(3 * EDGE, cy),
@@ -414,21 +416,21 @@
         folds = (got_b, got_c, pay_b)
         corners = (pay_b, got_a, got_b, got_c)
         tail = head + own - EDGE
-        places = (head, 0, head, (tail, head, tail, 2 * EDGE))
+        places = (head - EDGE, head, 0, head, (tail, head, tail, 2 * EDGE))
     else:
         got_c = lax.ppermute(pay_c, "lon", [(i, i ^ 1) for i in range(lons)])
         tops = lax.ppermute(jnp.concatenate([pay_b[head:], got_c, got_b[head:]], axis=0), "lon", mirror)
         folds = (tops, tops, tops)
         corners = (lax.psum(pay_c[2 * EDGE :], "lon"),)
-        places = (0, own, own + 3 * EDGE, (0,))
+        places = (head - EDGE, 0, own, own + 3 * EDGE, (0,))
     chunks = pl.pallas_call(
         functools.partial(forcing_kernel, last, width, places),
-        in_specs=[VMEM] * (7 + len(corners)),
+        in_specs=[VMEM] * (8 + len(corners)),
         out_specs=VMEM,
         out_shape=shape(lats, width + 2 * EDGE, cy),
         compiler_params=PARAMS,
         name="forcing",
-    )(tt, kt, got_a, got_b, *folds, *corners)
+    )(tt, kt, ends, got_a, got_b, *folds, *corners)
     chunks, row_a, ns_b = lax.optimization_barrier((chunks, row_a, ns_b))
     got = lax.all_to_all(chunks, "lat", split_axis=0, concat_axis=0, tiled=True)
 
@@ -442,14 +444,13 @@
         cost_estimate=pl.CostEstimate(flops=10**11, bytes_accessed=0, transcendentals=0),
         name="rim",
     )(rows_b)
-    row_a, ns_b, rim_b = lax.optimization_barrier((row_a, ns_b, rim_b))
+    row_a, rim_b = lax.optimization_barrier((row_a, rim_b))
     rows_a = lax.ppermute(row_a, joint, [(i, i ^ 1) for i in range(devices)])
     second = []
     for lon in range(lons):
         second += [(lon * lats + lat, (lons - 1 - lon) * lats + lat) for lat in (0, last)]
         second += [(lon * lats + lat, lon * lats + (lat + 1 if lat % 2 else lat - 1)) for lat in range(1, last)]
     beyond = lax.ppermute(ns_b, joint, second)
-    got, beyond = lax.optimization_barrier((got, beyond))
     new_theta = pl.pallas_call(
         functools.partial(tracer_kernel, last),
         in_specs=[VMEM] * 7,

time: 37.5 us -> 36.9 us (0.984)
  starting transfers between devices: 17.6 us -> 19.1 us
  waiting for transfers between devices: 9.8 us -> 8.38 us
  Pallas kernels: 9.11 us -> 8.43 us
    all_to_all x1, waiting for transfers between devices: 4.11 us -> 1.05 us  [per_device(): gram = lax.all_to_all(gram, joint, split_axis=0, concat_axis=0, tiled=True)]
    ppermute x1, waiting for transfers between devices: 0.01 us -> 2.3 us  [per_device(): rows_a = lax.ppermute(row_a, joint, [(i, i ^ 1) for i in range(devices)])]
    ppermute x1, starting transfers between devices: 0.01 us -> 1.59 us  [per_device(): beyond = lax.ppermute(ns_b, joint, second)]
    ppermute x1, waiting for transfers between devices: 3.16 us -> 1.64 us  [per_device(): beyond = lax.ppermute(ns_b, joint, second)]
    all_to_all x1, waiting for transfers between devices: 2.52 us -> 3.37 us  [per_device(): got = lax.all_to_all(chunks, 'lat', split_axis=0, concat_axis=0, tiled=True)]
    pallas_call x1, Pallas kernels: 1.37 us -> 0.86 us  [per_device(): pl.pallas_call(functools.partial(forcing_kernel, last, width, places), in...]
  transfers between devices with their start and end apart: 8 -> 8, of which waited for: 3 -> 4; matrix products, arithmetic and copies ran while one was open for 0% -> 0% of each run, Pallas kernels for 12% -> 10%
where the time goes in v5:
time: 36.9 us; the launch traced here: 36.6 us
  starting transfers between devices  19.1 us (52%)
  Pallas kernels  8.43 us (23%)
  waiting for transfers between devices  8.38 us (23%)
  between operations  0.69 us (2%)
    ppermute x1, starting transfers between devices, per_device(): lax.ppermute(row_b, joint, [(i, (i + 1 if i % 2 else i - 1) % devices) fo...  5.28 us
    all_to_all x1, starting transfers between devices, per_device(): got = lax.all_to_all(chunks, 'lat', split_axis=0, concat_axis=0, tiled=True)  4.17 us
    all_to_all x1, waiting for transfers between devices, per_device(): got = lax.all_to_all(chunks, 'lat', split_axis=0, concat_axis=0, tiled=True)  3.37 us
    all_to_all x1, starting transfers between devices, per_device(): gram = lax.all_to_all(gram, joint, split_axis=0, concat_axis=0, tiled=True)  2.76 us
    pallas_call x1, Pallas kernels, per_device(): pl.pallas_call(functools.partial(tracer_kernel, last), in_specs=[VMEM] *...  2.75 us
    ppermute x1, starting transfers between devices, per_device(): got_b = lax.ppermute(pay_b, 'lon', pairs_b)  2.47 us
    pallas_call x1, Pallas kernels, per_device(): pl.pallas_call(functools.partial(sum_kernel, cell), in_specs=[HBM] * 5, o...  2.34 us
    ppermute x1, waiting for transfers between devices, per_device(): rows_a = lax.ppermute(row_a, joint, [(i, i ^ 1) for i in range(devices)])  2.3 us
  transfers between devices with their start and end apart: 8, of which 4 were waited for; matrix products, arithmetic and copies ran while one was open for 0% of the time, Pallas kernels for 10%

profile of v5, /device:TPU:0, one launch (start us, length us, event | category | flops | bytes accessed | tf_op | source)
XLA Modules:
  0.0 36.6 jit_solution(17162330848849132989)
XLA Ops:
  0.6 2.3 %level_sum.1 = (f32[16,128,256]{2,1,0:T(8,128)S(1)}, f32[128,256]{1,0:T(8,128)S(1)}, f32[128,256]{1,0:T(8,128)S(1)}, f32[256,128]{1,0:T(8,128)S(1)}, f32[256,128...) custom-call(f32[16]{0:T(128)} %weight_hbm.1, ...), custom_call_target="tpu_custom_call" | custom-call | tf_op jit(solution)/shard_map/level_sum/pallas_call | solution.py:380
  3.0 2.5 %collective-permute-start.1 = (f32[80,128]{1,0:T(8,128)S(1)}, f32[80,128]{1,0:T(8,128)S(1)}, u32[]{:S(2)}, u32[]{:S(2)}) collective-permute-start(f32[80,128]{1,0:T(8,128)S(1)} %get-tuple-element.25.tops_b.rest_0_), channel_id=1, source_target_pairs={{0,24},{8,16},{16,8},{24,0},{1,25},{9,17},{17,9},{25,1},{2,26},{10... | collective-permute-start | bytes 122888 | tf_op jit(solution)/shard_map/ppermute | solution.py:413
  5.4 0.7 %collective-permute-start = (f32[48,128]{1,0:T(8,128)S(1)}, f32[48,128]{1,0:T(8,128)S(1)}, u32[]{:S(2)}, u32[]{:S(2)}) collective-permute-start(f32[48,128]{1,0:T(8,128)S(1)} %get-tuple-element.24), channel_id=1, source_target_pairs={{0,8},{8,0},{16,24},{24,16},{1,9},{9,1},{17,25},{25,17},{2,10},{10... | collective-permute-start | bytes 73736 | tf_op jit(solution)/shard_map/ppermute | solution.py:412
  6.1 0.0 collective-permute-start.2
  6.2 5.3 %collective-permute-start.3 = (f32[24,128]{1,0:T(8,128)S(1)}, f32[24,128]{1,0:T(8,128)S(1)}, u32[]{:S(2)}, u32[]{:S(2)}) collective-permute-start(f32[24,128]{1,0:T(8,128)S(1)} %get-tuple-element.33), channel_id=1, source_target_pairs={{0,31},{1,2},{2,1},{3,4},{4,3},{5,6},{6,5},{7,8},{8,7},{9,10},{10,... | collective-permute-start | bytes 36872 | tf_op jit(solution)/shard_map/ppermute | solution.py:437
  11.4 0.0 collective-permute-done.2.tops_a.rest_3_
  11.4 0.0 collective-permute-done.got_a.rest_1_
  11.4 0.0 collective-permute-done.1.got_b.tops_m.rest_2_
  11.5 0.9 %forcing.1 = f32[8,48,128]{2,1,0:T(8,128)} custom-call(f32[256,128]{1,0:T(8,128)S(1)} %get-tuple-element.26.tt, f32[256,128]{1,0:T(8,128)S(1)} %get-tuple-element.27.kt, f32[8,256]{1,0:T(8,128)S(1)} %get-tuple-element.28.ends, f32[48,128]{1,0:T(8,128)S(1)} %collective-permute-done.got_a.rest_1_, f32[80,128]{1,0:T(8,128)S(1)} %collective-permute-done.1.got_b.tops_m.rest_2_, ...), custom_call_target="tpu_custom_call" | custom-call | tf_op jit(solution)/shard_map/forcing/pallas_call | solution.py:426
  12.3 4.2 %all-to-all-start = ((f32[8,48,128]{2,1,0:T(8,128)}), f32[8,48,128]{2,1,0:T(8,128)S(1)}, u32[]{:S(2)}, u32[]{:S(2)}) async-start(f32[8,48,128]{2,1,0:T(8,128)} %forcing.1), calls=%async_computation | async-start | bytes 393216 | tf_op jit(solution)/shard_map/all_to_all | solution.py:435
  16.5 0.0 copy-start
  16.5 0.0 copy-start.1
  16.5 0.0 collective-permute-done.3.rows
  16.5 2.1 %collective-permute-start.4 = (f32[56,128]{1,0:T(8,128)S(1)}, f32[56,128]{1,0:T(8,128)S(1)}, u32[]{:S(2)}, u32[]{:S(2)}) collective-permute-start(f32[56,128]{1,0:T(8,128)S(1)} %get-tuple-element.34), channel_id=1, source_target_pairs={{0,1},{1,0},{2,3},{3,2},{4,5},{5,4},{6,7},{7,6},{8,9},{9,8},{10,11... | collective-permute-start | bytes 86024 | tf_op jit(solution)/shard_map/ppermute | solution.py:448
  18.6 2.3 %collective-permute-done.4.rows_a = f32[56,128]{1,0:T(8,128)S(1)} collective-permute-done((f32[56,128]{1,0:T(8,128)S(1)}, f32[56,128]{1,0:T(8,128)S(1)}, u32[]{:S(2)}, u32[]{:S(2)}) %collective-permute-start.4) | collective-permute-done | bytes 28704 | tf_op jit(solution)/shard_map/ppermute | solution.py:448
  20.9 3.4 %all-to-all-done.got = f32[8,48,128]{2,1,0:T(8,128)S(1)} async-done(((f32[8,48,128]{2,1,0:T(8,128)}), f32[8,48,128]{2,1,0:T(8,128)S(1)}, u32[]{:S(2)}, u32[]{:S(2)}) %all-to-all-start) | async-done | bytes 196640 | tf_op jit(solution)/shard_map/all_to_all | solution.py:435
  24.3 0.0 copy-done
  24.3 0.0 copy-done.1
  24.3 1.7 %krylov.1 = (f32[4,32,1024]{2,1,0:T(8,128)S(1)}, f32[32,128]{1,0:T(8,128)}) custom-call(s32[32,32]{1,0:T(8,128)S(1)} %copy-done.1, f32[8,48,128]{2,1,0:T(8,128)S(1)} %all-to-all-done.got, f32[32,1024]{1,0:T(8,128)S(1)} %copy-done, f32[56,128]{1,0:T(8,128)S(1)} %collective-permute-done.4.rows_a, f32[24,128]{1,0:T(8,128)S(1)} %rim.1.rows_b), custom_call_target="tpu_custom_call" | custom-call | tf_op jit(solution)/shard_map/krylov/pallas_call | solution.py:465
  25.9 2.8 %all-to-all-start.1 = ((f32[32,1,128]{2,1,0:T(1,128)}), f32[32,1,128]{2,1,0:T(1,128)S(1)}, u32[]{:S(2)}, u32[]{:S(2)}) async-start(f32[32,1,128]{2,1,0:T(1,128)} %bitcast.1), calls=%async_computation.1 | async-start | bytes 32768 | tf_op jit(solution)/shard_map/all_to_all | solution.py:473
  28.7 1.6 %collective-permute-start.5 = (f32[32,128]{1,0:T(8,128)S(1)}, f32[32,128]{1,0:T(8,128)S(1)}, u32[]{:S(2)}, u32[]{:S(2)}) collective-permute-start(f32[32,128]{1,0:T(8,128)S(1)} %get-tuple-element.35), channel_id=1, source_target_pairs={{0,24},{7,31},{1,2},{2,1},{3,4},{4,3},{5,6},{6,5},{8,16},{15,23},{... | collective-permute-start | bytes 49160 | tf_op jit(solution)/shard_map/ppermute | solution.py:453
  30.3 1.6 %collective-permute-done.5.rows_b = f32[32,128]{1,0:T(8,128)S(1)} collective-permute-done((f32[32,128]{1,0:T(8,128)S(1)}, f32[32,128]{1,0:T(8,128)S(1)}, u32[]{:S(2)}, u32[]{:S(2)}) %collective-permute-start.5) | collective-permute-done | bytes 16416 | tf_op jit(solution)/shard_map/ppermute | solution.py:453
  31.9 2.8 %tracer.1 = f32[16,128,256]{2,1,0:T(8,128)} custom-call(f32[16,128,256]{2,1,0:T(8,128)S(1)} %get-tuple-element.21.theta, f32[128,256]{1,0:T(8,128)S(1)} %get-tuple-element.22.ocean, f32[128,256]{1,0:T(8,128)S(1)} %get-tuple-element.23.coef, f32[48,128]{1,0:T(8,128)S(1)} %collective-permute-done.got_a.rest_1_, ...), custom_call_target="tpu_custom_call" | custom-call | flops 6291456 | bytes 4194304 | tf_op jit(solution)/shard_map/tracer/pallas_call | solution.py:454
  34.7 1.1 %all-to-all-done.1 = f32[32,1,128]{2,1,0:T(1,128)S(1)} async-done(((f32[32,1,128]{2,1,0:T(1,128)}), f32[32,1,128]{2,1,0:T(1,128)S(1)}, u32[]{:S(2)}, u32[]{:S(2)}) %all-to-all-start.1) | async-done | bytes 16416 | tf_op jit(solution)/shard_map/all_to_all | solution.py:473
  35.8 0.8 %combine.1 = f32[32,1024]{1,0:T(8,128)} custom-call(f32[32,128]{1,0:T(8,128)S(1)} %bitcast.4, f32[4,32,1024]{2,1,0:T(8,128)S(1)} %get-tuple-element.39.basis), custom_call_target="tpu_custom_call" | custom-call | tf_op jit(solution)/shard_map/combine/pallas_call | solution.py:474
  (1 shorter events, 0.0 us)
Async XLA Ops:
  3.0 8.5 %collective-permute-start.1 = (f32[80,128]{1,0:T(8,128)S(1)}, f32[80,128]{1,0:T(8,128)S(1)}, u32[]{:S(2)}, u32[]{:S(2)}) collective-permute-start(f32[80,128]{1,0:T(8,128)S(1)} %get-tuple-element.25.tops_b.rest_0_), channel_id=1, source_target_pairs={{0,24},{8,16},{16,8},{24,0},{1,25},{9,17},{17,9},{25,1},{2,26},{10... | collective-permute-start | bytes 122888 | tf_op jit(solution)/shard_map/ppermute | solution.py:413
  5.4 6.0 %collective-permute-start = (f32[48,128]{1,0:T(8,128)S(1)}, f32[48,128]{1,0:T(8,128)S(1)}, u32[]{:S(2)}, u32[]{:S(2)}) collective-permute-start(f32[48,128]{1,0:T(8,128)S(1)} %get-tuple-element.24), channel_id=1, source_target_pairs={{0,8},{8,0},{16,24},{24,16},{1,9},{9,1},{17,25},{25,17},{2,10},{10... | collective-permute-start | bytes 73736 | tf_op jit(solution)/shard_map/ppermute | solution.py:412
  6.1 5.3 %collective-permute-start.2 = (f32[24,128]{1,0:T(8,128)S(1)}, f32[24,128]{1,0:T(8,128)S(1)}, u32[]{:S(2)}, u32[]{:S(2)}) collective-permute-start(f32[24,128]{1,0:T(8,128)S(1)} %get-tuple-element.29), channel_id=1, source_target_pairs={{0,16},{8,24},{16,0},{24,8},{1,17},{9,25},{17,1},{25,9},{2,18},{10... | collective-permute-start | bytes 36872 | tf_op jit(solution)/shard_map/ppermute | solution.py:415
  6.2 10.3 %collective-permute-start.3 = (f32[24,128]{1,0:T(8,128)S(1)}, f32[24,128]{1,0:T(8,128)S(1)}, u32[]{:S(2)}, u32[]{:S(2)}) collective-permute-start(f32[24,128]{1,0:T(8,128)S(1)} %get-tuple-element.33), channel_id=1, source_target_pairs={{0,31},{1,2},{2,1},{3,4},{4,3},{5,6},{6,5},{7,8},{8,7},{9,10},{10,... | collective-permute-start | bytes 36872 | tf_op jit(solution)/shard_map/ppermute | solution.py:437
  12.3 12.0 %all-to-all-start = ((f32[8,48,128]{2,1,0:T(8,128)}), f32[8,48,128]{2,1,0:T(8,128)S(1)}, u32[]{:S(2)}, u32[]{:S(2)}) async-start(f32[8,48,128]{2,1,0:T(8,128)} %forcing.1), calls=%async_computation | async-start | bytes 393216 | tf_op jit(solution)/shard_map/all_to_all | solution.py:435
  16.5 7.8 %copy-start = (f32[32,1024]{1,0:T(8,128)S(1)}, f32[32,1024]{1,0:T(8,128)}, u32[]{:S(2)}) copy-start(f32[32,1024]{1,0:T(8,128)} %diag.1) | copy-start | bytes 393220
  16.5 7.8 %copy-start.1 = (s32[32,32]{1,0:T(8,128)S(1)}, s32[32,32]{1,0:T(8,128)}, u32[]{:S(2)}) copy-start(s32[32,32]{1,0:T(8,128)} %table.1) | copy-start | bytes 12292
  16.5 4.4 %collective-permute-start.4 = (f32[56,128]{1,0:T(8,128)S(1)}, f32[56,128]{1,0:T(8,128)S(1)}, u32[]{:S(2)}, u32[]{:S(2)}) collective-permute-start(f32[56,128]{1,0:T(8,128)S(1)} %get-tuple-element.34), channel_id=1, source_target_pairs={{0,1},{1,0},{2,3},{3,2},{4,5},{5,4},{6,7},{7,6},{8,9},{9,8},{10,11... | collective-permute-start | bytes 86024 | tf_op jit(solution)/shard_map/ppermute | solution.py:448
  25.9 9.8 %all-to-all-start.1 = ((f32[32,1,128]{2,1,0:T(1,128)}), f32[32,1,128]{2,1,0:T(1,128)S(1)}, u32[]{:S(2)}, u32[]{:S(2)}) async-start(f32[32,1,128]{2,1,0:T(1,128)} %bitcast.1), calls=%async_computation.1 | async-start | bytes 32768 | tf_op jit(solution)/shard_map/all_to_all | solution.py:473
  28.7 3.2 %collective-permute-start.5 = (f32[32,128]{1,0:T(8,128)S(1)}, f32[32,128]{1,0:T(8,128)S(1)}, u32[]{:S(2)}, u32[]{:S(2)}) collective-permute-start(f32[32,128]{1,0:T(8,128)S(1)} %get-tuple-element.35), channel_id=1, source_target_pairs={{0,24},{7,31},{1,2},{2,1},{3,4},{4,3},{5,6},{6,5},{8,16},{15,23},{... | collective-permute-start | bytes 49160 | tf_op jit(solution)/shard_map/ppermute | solution.py:453

commit v6 on v5

--- a/solution.py
+++ b/solution.py
@@ -11,8 +11,8 @@
 EDGE = 8
 HALO = ITERS
 RIM = HALO - 1
-CENTRE = 5.1
-WIDTH = 4.9
+SCALE = 4.0
+STATS = 48
 VMEM = pl.BlockSpec(memory_space=pltpu.VMEM)
 SMEM = pl.BlockSpec(memory_space=pltpu.SMEM)
 HBM = pl.BlockSpec(memory_space=pltpu.HBM)
@@ -44,6 +44,10 @@
     return turn(v, 1, 0) + turn(v, -1, 0) + turn(v, 1, 1) + turn(v, -1, 1)
 
 
+def total_of(v):
+    return jnp.sum(jnp.sum(v, axis=0, keepdims=True), axis=1, keepdims=True)
+
+
 def block_mask(table, row0, rows, col0, cols, cell):
     down, across = table.shape
     pick_rows = ones_at(lax.div(row0 + iota((rows, down), 0), cell) == iota((rows, down), 1))
@@ -51,21 +55,19 @@
     return mat(mat(pick_rows, table), pick_cols)
 
 
-def sum_kernel(cell, weight_hbm, table_hbm, theta_hbm, kappa_hbm, diag_hbm, theta, ocean, coef, tt, kt, ends, pay_a, pay_b, pay_c, row_a, row_b, ns_b, kappa, corner, rim, table, weight, sems):
+def sum_kernel(cell, weight_hbm, table_hbm, theta_hbm, kappa_hbm, diag_hbm, theta, ocean, coef, tt, kt, ends, pay_a, pay_b, pay_c, row_a, row_b, ns_b, kappa, strip, table, weight, sems):
     levels, cy, cx = theta.shape
     width, full = diag_hbm.shape
     copies = [
         pltpu.make_async_copy(table_hbm, table, sems.at[0]),
         pltpu.make_async_copy(weight_hbm, weight, sems.at[1]),
         pltpu.make_async_copy(kappa_hbm, kappa, sems.at[2]),
-        pltpu.make_async_copy(diag_hbm.at[:, pl.ds(full - 128, 128)], corner, sems.at[3]),
-        pltpu.make_async_copy(diag_hbm.at[pl.ds(0, EDGE)], rim.at[0], sems.at[4]),
-        pltpu.make_async_copy(diag_hbm.at[pl.ds(width - EDGE, EDGE)], rim.at[1], sems.at[5]),
+        pltpu.make_async_copy(diag_hbm, strip, sems.at[3]),
     ]
     pieces = 4
     some = levels // pieces
     for n in range(pieces):
-        copies.append(pltpu.make_async_copy(theta_hbm.at[pl.ds(n * some, some)], theta.at[pl.ds(n * some, some)], sems.at[6 + n]))
+        copies.append(pltpu.make_async_copy(theta_hbm.at[pl.ds(n * some, some)], theta.at[pl.ds(n * some, some)], sems.at[4 + n]))
     for copy in copies:
         copy.start()
     lon, lat = lax.axis_index("lon"), lax.axis_index("lat")
@@ -74,14 +76,18 @@
     copies[0].wait()
     mask = block_mask(table[...].astype(jnp.float32), lat * cy, cy, lon * cx, cx, cell)
     copies[3].wait()
-    column = jnp.concatenate([corner[...], jnp.zeros((128 - width, 128), jnp.float32)], axis=0).T
+    column = jnp.concatenate([strip[:, full - 128 :], jnp.zeros((128 - width, 128), jnp.float32)], axis=0).T
     column = turn(column[128 - EDGE :], lon * width, 1)
-    copies[4].wait()
-    copies[5].wait()
+    down, across = table.shape
+    x0 = (lon * (cx // width) + lat) * width
+    land = table[...].astype(jnp.float32)
+    pick = ones_at(lax.div(x0 + iota((width, across), 0), cell) == iota((width, across), 1))
+    pick = lax.dot_general(pick, land, (((1,), (1,)), ((), ())), preferred_element_type=jnp.float32)
+    wet = mat(pick, ones_at(lax.div(iota((down, full), 1), cell) == iota((down, full), 0)))
     at = cx // cy * levels
     for c in range(full // cy):
-        w = rim[0, :RIM, c * cy : (c + 1) * cy]
-        e = rim[1, EDGE - RIM :, c * cy : (c + 1) * cy]
+        w = strip[:RIM, c * cy : (c + 1) * cy]
+        e = strip[width - RIM :, c * cy : (c + 1) * cy]
         row_a[at : at + RIM, :] = jnp.where(even_row, e, w)
         row_b[c * RIM : (c + 1) * RIM, :] = jnp.where(even_row, w, e)
         at += RIM
@@ -97,13 +103,20 @@
     sides = jnp.zeros((cy, 128), jnp.float32)
     copies[1].wait()
     for n in range(pieces):
-        copies[6 + n].wait()
+        copies[4 + n].wait()
         for k in range(n * some, n * some + some):
             th = theta[k]
             total = total + weight[k] * th
             sides = jnp.where(lane == k, turn(th[:, :128], k, 1), sides)
             sides = jnp.where(lane == levels + k, turn(th[:, cx - 128 :], levels + k + 1, 1), sides)
     t = mask * total
+    inner = (iota((cy, cx), 0) > 0) & (iota((cy, cx), 0) < cy - 1) & (iota((cy, cx), 1) > 0) & (iota((cy, cx), 1) < cx - 1)
+    kept = jnp.where(inner, t, 0.0)
+    stats = [total_of(v) for v in (kept * t, kept * (4.0 * t - beside(t)), wet, wet * strip[...])]
+    spot = iota((EDGE, 128), 1)
+    mine = (spot >= lon * width) & (spot < (lon + 1) * width)
+    for n, value in enumerate(stats):
+        column = jnp.where(iota((EDGE, 128), 0) == n, jnp.where(mine, value, 0.0), column)
     ttv = t.T
     tt[...] = ttv
     sidest = (sides * jnp.where(lane < levels, mask[:, :1], mask[:, cx - 1 :])).T
@@ -182,8 +195,11 @@
     pack = jnp.where(row < 4, row_ends, turn(over_f, 4, 0))
     low = iota((EDGE, cy), 0) < HALO
     corner = sum(ref[at : at + EDGE, :] for ref, at in zip(corners, at_corners))
+    stats = jnp.sum(corner, axis=1, keepdims=True)
     corner = jnp.where(low, turn(turn(corner, HALO, 0), 64, 1), corner)
-    in_pack = iota((EDGE, cy), 1) < 64
+    spot = iota((EDGE, cy), 1)
+    corner = jnp.where(spot < 64, stats, corner)
+    in_pack = spot < STATS
     for d in range(cx // width):
         at = EDGE + d * width
         out[d, :width, :] = f[at : at + width, :cy]
@@ -266,12 +282,14 @@
     fold = [fold[EDGE - 1 - r : EDGE - r] for r in range(HALO)] + [jnp.zeros((128 - HALO, 128), jnp.float32)]
     d_all = jnp.concatenate([d_main, jnp.concatenate(fold, axis=0).T[:rows]], axis=1)
 
-    near = mask * (1.0 / WIDTH)
-    centre = near * ((4.0 - CENTRE) + d_all)
+    stats = sum(got[s, rows : rows + EDGE, :] for s in range(count))[:, STATS : STATS + 1]
+    share = stats[1:2] / stats[0:1]
+    shift = jnp.where(stats[0:1] > 0.0, share, 0.0) + jnp.where(stats[2:3] > 0.0, stats[3:4] / stats[2:3], 0.0)
+    near = mask * (1.0 / SCALE)
+    centre = near * (4.0 + d_all - shift)
     p = [mask * f]
-    p.append(centre * p[0] - near * beside(p[0]))
-    for j in range(2, ITERS + 1):
-        p.append(2.0 * (centre * p[j - 1] - near * beside(p[j - 1])) - p[j - 2])
+    for j in range(ITERS):
+        p.append(centre * p[j] - near * beside(p[j]))
     for j in range(ITERS):
         basis[j] = p[j][:width, :full]
     sums = []
@@ -280,8 +298,12 @@
             both = p[i][:width, :full] * p[j][:width, :full]
             both = sum(both[:, c : c + 128] for c in range(0, full, 128))
             sums.append(jnp.sum(both, axis=0, keepdims=True))
-    sums = jnp.concatenate(sums + [jnp.zeros((128 - len(sums), 128), jnp.float32)], axis=0)
-    gram[...] = jnp.broadcast_to(jnp.sum(sums.T, axis=0, keepdims=True), gram.shape)
+    pairs = len(sums)
+    sums = jnp.concatenate(sums + [jnp.zeros((16 - pairs, 128), jnp.float32)], axis=0)
+    sums = jnp.where(iota((16, 128), 0) == iota((16, 128), 1), jnp.sum(sums, axis=1, keepdims=True), 0.0)
+    sums = jnp.sum(sums, axis=0, keepdims=True)
+    sums = jnp.where(iota((1, 128), 1) == pairs, shift, sums)
+    gram[...] = jnp.broadcast_to(sums, gram.shape)
 
 
 def combine_kernel(gram, basis, psi):
@@ -291,10 +313,10 @@
     for n, (i, j) in enumerate(pairs):
         at[i, j] = at[j, i] = jnp.broadcast_to(g[:, n : n + 1], (8, 128))
 
+    shift = jnp.broadcast_to(gram[:1, len(pairs) : len(pairs) + 1], (8, 128))
+
     def applied(i, j):
-        if j == 0:
-            return CENTRE * at[i, 0] + WIDTH * at[i, 1]
-        return CENTRE * at[i, j] + (0.5 * WIDTH) * (at[i, j + 1] + at[i, j - 1])
+        return shift * at[i, j] + SCALE * at[i, j + 1]
 
     a = {(i, j): applied(i, j) for i in range(ITERS) for j in range(i, ITERS)}
     b = [at[i, 0] for i in range(ITERS)]
@@ -397,11 +419,10 @@
         ],
         scratch_shapes=[
             pltpu.VMEM((cy, cx), f32),
-            pltpu.VMEM((width, 128), f32),
-            pltpu.VMEM((2, EDGE, full), f32),
+            pltpu.VMEM((width, full), f32),
             pltpu.VMEM(land_blocks.shape, jnp.int32),
             pltpu.SMEM((levels,), f32),
-            pltpu.SemaphoreType.DMA((10,)),
+            pltpu.SemaphoreType.DMA((8,)),
         ],
         compiler_params=PARAMS,
         name="level_sum",

time: 36.9 us -> 37.1 us (level)
  no operation moved by 1% of the time
where the time goes in v6:
time: 37.1 us; the launch traced here: 36.8 us
  starting transfers between devices  19.1 us (51%)
  Pallas kernels  8.65 us (23%)
  waiting for transfers between devices  8.38 us (23%)
  between operations  0.69 us (2%)
    ppermute x1, starting transfers between devices, per_device(): lax.ppermute(row_b, joint, [(i, (i + 1 if i % 2 else i - 1) % devices) fo...  5.28 us
    all_to_all x1, starting transfers between devices, per_device(): got = lax.all_to_all(chunks, 'lat', split_axis=0, concat_axis=0, tiled=True)  4.17 us
    all_to_all x1, waiting for transfers between devices, per_device(): got = lax.all_to_all(chunks, 'lat', split_axis=0, concat_axis=0, tiled=True)  3.37 us
    all_to_all x1, starting transfers between devices, per_device(): gram = lax.all_to_all(gram, joint, split_axis=0, concat_axis=0, tiled=True)  2.76 us
    pallas_call x1, Pallas kernels, per_device(): pl.pallas_call(functools.partial(tracer_kernel, last), in_specs=[VMEM] *...  2.75 us
    pallas_call x1, Pallas kernels, per_device(): pl.pallas_call(functools.partial(sum_kernel, cell), in_specs=[HBM] * 5, o...  2.54 us
    ppermute x1, starting transfers between devices, per_device(): got_b = lax.ppermute(pay_b, 'lon', pairs_b)  2.47 us
    ppermute x1, waiting for transfers between devices, per_device(): rows_a = lax.ppermute(row_a, joint, [(i, i ^ 1) for i in range(devices)])  2.3 us
  transfers between devices with their start and end apart: 8, of which 4 were waited for; matrix products, arithmetic and copies ran while one was open for 0% of the time, Pallas kernels for 10%

profile of v6, /device:TPU:0, one launch (start us, length us, event | category | flops | bytes accessed | tf_op | source)
XLA Modules:
  0.0 36.8 jit_solution(4190627056262443300)
XLA Ops:
  0.6 2.5 %level_sum.1 = (f32[16,128,256]{2,1,0:T(8,128)S(1)}, f32[128,256]{1,0:T(8,128)S(1)}, f32[128,256]{1,0:T(8,128)S(1)}, f32[256,128]{1,0:T(8,128)S(1)}, f32[256,128...) custom-call(f32[16]{0:T(128)} %weight_hbm.1, ...), custom_call_target="tpu_custom_call" | custom-call | tf_op jit(solution)/shard_map/level_sum/pallas_call | solution.py:402
  3.2 2.5 %collective-permute-start.1 = (f32[80,128]{1,0:T(8,128)S(1)}, f32[80,128]{1,0:T(8,128)S(1)}, u32[]{:S(2)}, u32[]{:S(2)}) collective-permute-start(f32[80,128]{1,0:T(8,128)S(1)} %get-tuple-element.25.tops_b.rest_0_), channel_id=1, source_target_pairs={{0,24},{8,16},{16,8},{24,0},{1,25},{9,17},{17,9},{25,1},{2,26},{10... | collective-permute-start | bytes 122888 | tf_op jit(solution)/shard_map/ppermute | solution.py:434
  5.7 0.7 %collective-permute-start = (f32[48,128]{1,0:T(8,128)S(1)}, f32[48,128]{1,0:T(8,128)S(1)}, u32[]{:S(2)}, u32[]{:S(2)}) collective-permute-start(f32[48,128]{1,0:T(8,128)S(1)} %get-tuple-element.24), channel_id=1, source_target_pairs={{0,8},{8,0},{16,24},{24,16},{1,9},{9,1},{17,25},{25,17},{2,10},{10... | collective-permute-start | bytes 73736 | tf_op jit(solution)/shard_map/ppermute | solution.py:433
  6.3 0.0 collective-permute-start.2
  6.4 5.3 %collective-permute-start.3 = (f32[24,128]{1,0:T(8,128)S(1)}, f32[24,128]{1,0:T(8,128)S(1)}, u32[]{:S(2)}, u32[]{:S(2)}) collective-permute-start(f32[24,128]{1,0:T(8,128)S(1)} %get-tuple-element.33), channel_id=1, source_target_pairs={{0,31},{1,2},{2,1},{3,4},{4,3},{5,6},{6,5},{7,8},{8,7},{9,10},{10,... | collective-permute-start | bytes 36872 | tf_op jit(solution)/shard_map/ppermute | solution.py:458
  11.6 0.0 collective-permute-done.2.tops_a.rest_3_
  11.7 0.0 collective-permute-done.got_a.rest_1_
  11.7 0.0 collective-permute-done.1.got_b.tops_m.rest_2_
  11.7 0.9 %forcing.1 = f32[8,48,128]{2,1,0:T(8,128)} custom-call(f32[256,128]{1,0:T(8,128)S(1)} %get-tuple-element.26.tt, f32[256,128]{1,0:T(8,128)S(1)} %get-tuple-element.27.kt, f32[8,256]{1,0:T(8,128)S(1)} %get-tuple-element.28.ends, f32[48,128]{1,0:T(8,128)S(1)} %collective-permute-done.got_a.rest_1_, f32[80,128]{1,0:T(8,128)S(1)} %collective-permute-done.1.got_b.tops_m.rest_2_, ...), custom_call_target="tpu_custom_call" | custom-call | tf_op jit(solution)/shard_map/forcing/pallas_call | solution.py:447
  12.5 4.2 %all-to-all-start = ((f32[8,48,128]{2,1,0:T(8,128)}), f32[8,48,128]{2,1,0:T(8,128)S(1)}, u32[]{:S(2)}, u32[]{:S(2)}) async-start(f32[8,48,128]{2,1,0:T(8,128)} %forcing.1), calls=%async_computation | async-start | bytes 393216 | tf_op jit(solution)/shard_map/all_to_all | solution.py:456
  16.7 0.0 copy-start
  16.7 0.0 copy-start.1
  16.7 0.0 collective-permute-done.3.rows
  16.8 2.1 %collective-permute-start.4 = (f32[56,128]{1,0:T(8,128)S(1)}, f32[56,128]{1,0:T(8,128)S(1)}, u32[]{:S(2)}, u32[]{:S(2)}) collective-permute-start(f32[56,128]{1,0:T(8,128)S(1)} %get-tuple-element.34), channel_id=1, source_target_pairs={{0,1},{1,0},{2,3},{3,2},{4,5},{5,4},{6,7},{7,6},{8,9},{9,8},{10,11... | collective-permute-start | bytes 86024 | tf_op jit(solution)/shard_map/ppermute | solution.py:469
  18.8 2.3 %collective-permute-done.4.rows_a = f32[56,128]{1,0:T(8,128)S(1)} collective-permute-done((f32[56,128]{1,0:T(8,128)S(1)}, f32[56,128]{1,0:T(8,128)S(1)}, u32[]{:S(2)}, u32[]{:S(2)}) %collective-permute-start.4) | collective-permute-done | bytes 28704 | tf_op jit(solution)/shard_map/ppermute | solution.py:469
  21.1 3.4 %all-to-all-done.got = f32[8,48,128]{2,1,0:T(8,128)S(1)} async-done(((f32[8,48,128]{2,1,0:T(8,128)}), f32[8,48,128]{2,1,0:T(8,128)S(1)}, u32[]{:S(2)}, u32[]{:S(2)}) %all-to-all-start) | async-done | bytes 196640 | tf_op jit(solution)/shard_map/all_to_all | solution.py:456
  24.5 0.0 copy-done
  24.5 0.0 copy-done.1
  24.5 1.6 %krylov.1 = (f32[4,32,1024]{2,1,0:T(8,128)S(1)}, f32[32,128]{1,0:T(8,128)}) custom-call(s32[32,32]{1,0:T(8,128)S(1)} %copy-done.1, f32[8,48,128]{2,1,0:T(8,128)S(1)} %all-to-all-done.got, f32[32,1024]{1,0:T(8,128)S(1)} %copy-done, f32[56,128]{1,0:T(8,128)S(1)} %collective-permute-done.4.rows_a, f32[24,128]{1,0:T(8,128)S(1)} %rim.1.rows_b), custom_call_target="tpu_custom_call" | custom-call | tf_op jit(solution)/shard_map/krylov/pallas_call | solution.py:486
  26.1 2.8 %all-to-all-start.1 = ((f32[32,1,128]{2,1,0:T(1,128)}), f32[32,1,128]{2,1,0:T(1,128)S(1)}, u32[]{:S(2)}, u32[]{:S(2)}) async-start(f32[32,1,128]{2,1,0:T(1,128)} %bitcast.1), calls=%async_computation.1 | async-start | bytes 32768 | tf_op jit(solution)/shard_map/all_to_all | solution.py:494
  28.9 1.6 %collective-permute-start.5 = (f32[32,128]{1,0:T(8,128)S(1)}, f32[32,128]{1,0:T(8,128)S(1)}, u32[]{:S(2)}, u32[]{:S(2)}) collective-permute-start(f32[32,128]{1,0:T(8,128)S(1)} %get-tuple-element.35), channel_id=1, source_target_pairs={{0,24},{7,31},{1,2},{2,1},{3,4},{4,3},{5,6},{6,5},{8,16},{15,23},{... | collective-permute-start | bytes 49160 | tf_op jit(solution)/shard_map/ppermute | solution.py:474
  30.5 1.6 %collective-permute-done.5.rows_b = f32[32,128]{1,0:T(8,128)S(1)} collective-permute-done((f32[32,128]{1,0:T(8,128)S(1)}, f32[32,128]{1,0:T(8,128)S(1)}, u32[]{:S(2)}, u32[]{:S(2)}) %collective-permute-start.5) | collective-permute-done | bytes 16416 | tf_op jit(solution)/shard_map/ppermute | solution.py:474
  32.1 2.8 %tracer.1 = f32[16,128,256]{2,1,0:T(8,128)} custom-call(f32[16,128,256]{2,1,0:T(8,128)S(1)} %get-tuple-element.21.theta, f32[128,256]{1,0:T(8,128)S(1)} %get-tuple-element.22.ocean, f32[128,256]{1,0:T(8,128)S(1)} %get-tuple-element.23.coef, f32[48,128]{1,0:T(8,128)S(1)} %collective-permute-done.got_a.rest_1_, ...), custom_call_target="tpu_custom_call" | custom-call | flops 6291456 | bytes 4194304 | tf_op jit(solution)/shard_map/tracer/pallas_call | solution.py:475
  34.9 1.1 %all-to-all-done.1 = f32[32,1,128]{2,1,0:T(1,128)S(1)} async-done(((f32[32,1,128]{2,1,0:T(1,128)}), f32[32,1,128]{2,1,0:T(1,128)S(1)}, u32[]{:S(2)}, u32[]{:S(2)}) %all-to-all-start.1) | async-done | bytes 16416 | tf_op jit(solution)/shard_map/all_to_all | solution.py:494
  35.9 0.8 %combine.1 = f32[32,1024]{1,0:T(8,128)} custom-call(f32[32,128]{1,0:T(8,128)S(1)} %bitcast.4, f32[4,32,1024]{2,1,0:T(8,128)S(1)} %get-tuple-element.39.basis), custom_call_target="tpu_custom_call" | custom-call | tf_op jit(solution)/shard_map/combine/pallas_call | solution.py:495
  (1 shorter events, 0.0 us)
Async XLA Ops:
  3.2 8.5 %collective-permute-start.1 = (f32[80,128]{1,0:T(8,128)S(1)}, f32[80,128]{1,0:T(8,128)S(1)}, u32[]{:S(2)}, u32[]{:S(2)}) collective-permute-start(f32[80,128]{1,0:T(8,128)S(1)} %get-tuple-element.25.tops_b.rest_0_), channel_id=1, source_target_pairs={{0,24},{8,16},{16,8},{24,0},{1,25},{9,17},{17,9},{25,1},{2,26},{10... | collective-permute-start | bytes 122888 | tf_op jit(solution)/shard_map/ppermute | solution.py:434
  5.7 6.0 %collective-permute-start = (f32[48,128]{1,0:T(8,128)S(1)}, f32[48,128]{1,0:T(8,128)S(1)}, u32[]{:S(2)}, u32[]{:S(2)}) collective-permute-start(f32[48,128]{1,0:T(8,128)S(1)} %get-tuple-element.24), channel_id=1, source_target_pairs={{0,8},{8,0},{16,24},{24,16},{1,9},{9,1},{17,25},{25,17},{2,10},{10... | collective-permute-start | bytes 73736 | tf_op jit(solution)/shard_map/ppermute | solution.py:433
  6.3 5.3 %collective-permute-start.2 = (f32[24,128]{1,0:T(8,128)S(1)}, f32[24,128]{1,0:T(8,128)S(1)}, u32[]{:S(2)}, u32[]{:S(2)}) collective-permute-start(f32[24,128]{1,0:T(8,128)S(1)} %get-tuple-element.29), channel_id=1, source_target_pairs={{0,16},{8,24},{16,0},{24,8},{1,17},{9,25},{17,1},{25,9},{2,18},{10... | collective-permute-start | bytes 36872 | tf_op jit(solution)/shard_map/ppermute | solution.py:436
  6.4 10.4 %collective-permute-start.3 = (f32[24,128]{1,0:T(8,128)S(1)}, f32[24,128]{1,0:T(8,128)S(1)}, u32[]{:S(2)}, u32[]{:S(2)}) collective-permute-start(f32[24,128]{1,0:T(8,128)S(1)} %get-tuple-element.33), channel_id=1, source_target_pairs={{0,31},{1,2},{2,1},{3,4},{4,3},{5,6},{6,5},{7,8},{8,7},{9,10},{10,... | collective-permute-start | bytes 36872 | tf_op jit(solution)/shard_map/ppermute | solution.py:458
  12.5 12.0 %all-to-all-start = ((f32[8,48,128]{2,1,0:T(8,128)}), f32[8,48,128]{2,1,0:T(8,128)S(1)}, u32[]{:S(2)}, u32[]{:S(2)}) async-start(f32[8,48,128]{2,1,0:T(8,128)} %forcing.1), calls=%async_computation | async-start | bytes 393216 | tf_op jit(solution)/shard_map/all_to_all | solution.py:456
  16.7 7.8 %copy-start = (f32[32,1024]{1,0:T(8,128)S(1)}, f32[32,1024]{1,0:T(8,128)}, u32[]{:S(2)}) copy-start(f32[32,1024]{1,0:T(8,128)} %diag.1) | copy-start | bytes 393220
  16.7 7.8 %copy-start.1 = (s32[32,32]{1,0:T(8,128)S(1)}, s32[32,32]{1,0:T(8,128)}, u32[]{:S(2)}) copy-start(s32[32,32]{1,0:T(8,128)} %table.1) | copy-start | bytes 12292
  16.8 4.4 %collective-permute-start.4 = (f32[56,128]{1,0:T(8,128)S(1)}, f32[56,128]{1,0:T(8,128)S(1)}, u32[]{:S(2)}, u32[]{:S(2)}) collective-permute-start(f32[56,128]{1,0:T(8,128)S(1)} %get-tuple-element.34), channel_id=1, source_target_pairs={{0,1},{1,0},{2,3},{3,2},{4,5},{5,4},{6,7},{7,6},{8,9},{9,8},{10,11... | collective-permute-start | bytes 86024 | tf_op jit(solution)/shard_map/ppermute | solution.py:469
  26.1 9.8 %all-to-all-start.1 = ((f32[32,1,128]{2,1,0:T(1,128)}), f32[32,1,128]{2,1,0:T(1,128)S(1)}, u32[]{:S(2)}, u32[]{:S(2)}) async-start(f32[32,1,128]{2,1,0:T(1,128)} %bitcast.1), calls=%async_computation.1 | async-start | bytes 32768 | tf_op jit(solution)/shard_map/all_to_all | solution.py:494
  28.9 3.2 %collective-permute-start.5 = (f32[32,128]{1,0:T(8,128)S(1)}, f32[32,128]{1,0:T(8,128)S(1)}, u32[]{:S(2)}, u32[]{:S(2)}) collective-permute-start(f32[32,128]{1,0:T(8,128)S(1)} %get-tuple-element.35), channel_id=1, source_target_pairs={{0,24},{7,31},{1,2},{2,1},{3,4},{4,3},{5,6},{6,5},{8,16},{15,23},{... | collective-permute-start | bytes 49160 | tf_op jit(solution)/shard_map/ppermute | solution.py:474

commit v7 on v6

--- a/solution.py
+++ b/solution.py
@@ -155,7 +155,7 @@
         ns_b[c * levels : (c + 1) * levels, :] = jnp.where(even_row, b, t)
 
 
-def forcing_kernel(last, width, places, tt, kt, ends, got_a, got_b, tops_m, tops_a, tops_b, *rest):
+def forcing_kernel(last, lons, width, places, tt, kt, ends, got_a, got_b, tops_m, tops_a, tops_b, *rest):
     *corners, out = rest
     at_ends, at_m, at_a, at_b, at_corners = places
     cx, cy = tt.shape
@@ -195,10 +195,12 @@
     pack = jnp.where(row < 4, row_ends, turn(over_f, 4, 0))
     low = iota((EDGE, cy), 0) < HALO
     corner = sum(ref[at : at + EDGE, :] for ref, at in zip(corners, at_corners))
-    stats = jnp.sum(corner, axis=1, keepdims=True)
+    spread = corner
     corner = jnp.where(low, turn(turn(corner, HALO, 0), 64, 1), corner)
     spot = iota((EDGE, cy), 1)
-    corner = jnp.where(spot < 64, stats, corner)
+    for n in range(lons):
+        first = STATS + n * ((64 - STATS) // lons)
+        corner = jnp.where((spot >= first) & (spot < 64), turn(spread, first - n * width, 1), corner)
     in_pack = spot < STATS
     for d in range(cx // width):
         at = EDGE + d * width
@@ -282,9 +284,11 @@
     fold = [fold[EDGE - 1 - r : EDGE - r] for r in range(HALO)] + [jnp.zeros((128 - HALO, 128), jnp.float32)]
     d_all = jnp.concatenate([d_main, jnp.concatenate(fold, axis=0).T[:rows]], axis=1)
 
-    stats = sum(got[s, rows : rows + EDGE, :] for s in range(count))[:, STATS : STATS + 1]
-    share = stats[1:2] / stats[0:1]
-    shift = jnp.where(stats[0:1] > 0.0, share, 0.0) + jnp.where(stats[2:3] > 0.0, stats[3:4] / stats[2:3], 0.0)
+    spot = iota((EDGE, cy), 1)
+    stats = jnp.where((spot >= STATS) & (spot < 64), sum(got[s, rows : rows + EDGE, :] for s in range(count)), 0.0)
+    means = jnp.where(stats[2:3] > 0.0, stats[3:4] / stats[2:3], 0.0)
+    totals = [total_of(v) for v in (stats[:1], stats[1:2] + stats[:1] * means, stats[2:3], stats[3:4])]
+    shift = jnp.where(totals[0] > 0.0, totals[1] / totals[0], jnp.where(totals[2] > 0.0, totals[3] / totals[2], 0.0))
     near = mask * (1.0 / SCALE)
     centre = near * (4.0 + d_all - shift)
     p = [mask * f]
@@ -445,7 +449,7 @@
         corners = (lax.psum(pay_c[2 * EDGE :], "lon"),)
         places = (head - EDGE, 0, own, own + 3 * EDGE, (0,))
     chunks = pl.pallas_call(
-        functools.partial(forcing_kernel, last, width, places),
+        functools.partial(forcing_kernel, last, lons, width, places),
         in_specs=[VMEM] * (8 + len(corners)),
         out_specs=VMEM,
         out_shape=shape(lats, width + 2 * EDGE, cy),

time: 37.1 us -> 37 us (level)
  no operation moved by 1% of the time
where the time goes in v7:
time: 37 us; the launch traced here: 36.8 us
  starting transfers between devices  19.1 us (52%)
  Pallas kernels  8.62 us (23%)
  waiting for transfers between devices  8.38 us (23%)
  between operations  0.69 us (2%)
    ppermute x1, starting transfers between devices, per_device(): lax.ppermute(row_b, joint, [(i, (i + 1 if i % 2 else i - 1) % devices) fo...  5.28 us
    all_to_all x1, starting transfers between devices, per_device(): got = lax.all_to_all(chunks, 'lat', split_axis=0, concat_axis=0, tiled=True)  4.17 us
    all_to_all x1, waiting for transfers between devices, per_device(): got = lax.all_to_all(chunks, 'lat', split_axis=0, concat_axis=0, tiled=True)  3.37 us
    all_to_all x1, starting transfers between devices, per_device(): gram = lax.all_to_all(gram, joint, split_axis=0, concat_axis=0, tiled=True)  2.76 us
    pallas_call x1, Pallas kernels, per_device(): pl.pallas_call(functools.partial(tracer_kernel, last), in_specs=[VMEM] *...  2.75 us
    pallas_call x1, Pallas kernels, per_device(): pl.pallas_call(functools.partial(sum_kernel, cell), in_specs=[HBM] * 5, o...  2.54 us
    ppermute x1, starting transfers between devices, per_device(): got_b = lax.ppermute(pay_b, 'lon', pairs_b)  2.47 us
    ppermute x1, waiting for transfers between devices, per_device(): rows_a = lax.ppermute(row_a, joint, [(i, i ^ 1) for i in range(devices)])  2.3 us
  transfers between devices with their start and end apart: 8, of which 4 were waited for; matrix products, arithmetic and copies ran while one was open for 0% of the time, Pallas kernels for 10%

profile of v7, /device:TPU:0, one launch (start us, length us, event | category | flops | bytes accessed | tf_op | source)
XLA Modules:
  0.0 36.8 jit_solution(12295605630030819383)
XLA Ops:
  0.6 2.5 %level_sum.1 = (f32[16,128,256]{2,1,0:T(8,128)S(1)}, f32[128,256]{1,0:T(8,128)S(1)}, f32[128,256]{1,0:T(8,128)S(1)}, f32[256,128]{1,0:T(8,128)S(1)}, f32[256,128...) custom-call(f32[16]{0:T(128)} %weight_hbm.1, ...), custom_call_target="tpu_custom_call" | custom-call | tf_op jit(solution)/shard_map/level_sum/pallas_call | solution.py:406
  3.2 2.5 %collective-permute-start.1 = (f32[80,128]{1,0:T(8,128)S(1)}, f32[80,128]{1,0:T(8,128)S(1)}, u32[]{:S(2)}, u32[]{:S(2)}) collective-permute-start(f32[80,128]{1,0:T(8,128)S(1)} %get-tuple-element.25.tops_b.rest_0_), channel_id=1, source_target_pairs={{0,24},{8,16},{16,8},{24,0},{1,25},{9,17},{17,9},{25,1},{2,26},{10... | collective-permute-start | bytes 122888 | tf_op jit(solution)/shard_map/ppermute | solution.py:438
  5.7 0.7 %collective-permute-start = (f32[48,128]{1,0:T(8,128)S(1)}, f32[48,128]{1,0:T(8,128)S(1)}, u32[]{:S(2)}, u32[]{:S(2)}) collective-permute-start(f32[48,128]{1,0:T(8,128)S(1)} %get-tuple-element.24), channel_id=1, source_target_pairs={{0,8},{8,0},{16,24},{24,16},{1,9},{9,1},{17,25},{25,17},{2,10},{10... | collective-permute-start | bytes 73736 | tf_op jit(solution)/shard_map/ppermute | solution.py:437
  6.3 0.0 collective-permute-start.2
  6.4 5.3 %collective-permute-start.3 = (f32[24,128]{1,0:T(8,128)S(1)}, f32[24,128]{1,0:T(8,128)S(1)}, u32[]{:S(2)}, u32[]{:S(2)}) collective-permute-start(f32[24,128]{1,0:T(8,128)S(1)} %get-tuple-element.33), channel_id=1, source_target_pairs={{0,31},{1,2},{2,1},{3,4},{4,3},{5,6},{6,5},{7,8},{8,7},{9,10},{10,... | collective-permute-start | bytes 36872 | tf_op jit(solution)/shard_map/ppermute | solution.py:462
  11.6 0.0 collective-permute-done.2.tops_a.rest_3_
  11.7 0.0 collective-permute-done.got_a.rest_1_
  11.7 0.0 collective-permute-done.1.got_b.tops_m.rest_2_
  11.7 0.9 %forcing.1 = f32[8,48,128]{2,1,0:T(8,128)} custom-call(f32[256,128]{1,0:T(8,128)S(1)} %get-tuple-element.26.tt, f32[256,128]{1,0:T(8,128)S(1)} %get-tuple-element.27.kt, f32[8,256]{1,0:T(8,128)S(1)} %get-tuple-element.28.ends, f32[48,128]{1,0:T(8,128)S(1)} %collective-permute-done.got_a.rest_1_, f32[80,128]{1,0:T(8,128)S(1)} %collective-permute-done.1.got_b.tops_m.rest_2_, ...), custom_call_target="tpu_custom_call" | custom-call | tf_op jit(solution)/shard_map/forcing/pallas_call | solution.py:451
  12.5 4.2 %all-to-all-start = ((f32[8,48,128]{2,1,0:T(8,128)}), f32[8,48,128]{2,1,0:T(8,128)S(1)}, u32[]{:S(2)}, u32[]{:S(2)}) async-start(f32[8,48,128]{2,1,0:T(8,128)} %forcing.1), calls=%async_computation | async-start | bytes 393216 | tf_op jit(solution)/shard_map/all_to_all | solution.py:460
  16.7 0.0 copy-start
  16.7 0.0 copy-start.1
  16.7 0.0 collective-permute-done.3.rows
  16.7 2.1 %collective-permute-start.4 = (f32[56,128]{1,0:T(8,128)S(1)}, f32[56,128]{1,0:T(8,128)S(1)}, u32[]{:S(2)}, u32[]{:S(2)}) collective-permute-start(f32[56,128]{1,0:T(8,128)S(1)} %get-tuple-element.34), channel_id=1, source_target_pairs={{0,1},{1,0},{2,3},{3,2},{4,5},{5,4},{6,7},{7,6},{8,9},{9,8},{10,11... | collective-permute-start | bytes 86024 | tf_op jit(solution)/shard_map/ppermute | solution.py:473
  18.8 2.3 %collective-permute-done.4.rows_a = f32[56,128]{1,0:T(8,128)S(1)} collective-permute-done((f32[56,128]{1,0:T(8,128)S(1)}, f32[56,128]{1,0:T(8,128)S(1)}, u32[]{:S(2)}, u32[]{:S(2)}) %collective-permute-start.4) | collective-permute-done | bytes 28704 | tf_op jit(solution)/shard_map/ppermute | solution.py:473
  21.1 3.4 %all-to-all-done.got = f32[8,48,128]{2,1,0:T(8,128)S(1)} async-done(((f32[8,48,128]{2,1,0:T(8,128)}), f32[8,48,128]{2,1,0:T(8,128)S(1)}, u32[]{:S(2)}, u32[]{:S(2)}) %all-to-all-start) | async-done | bytes 196640 | tf_op jit(solution)/shard_map/all_to_all | solution.py:460
  24.5 0.0 copy-done
  24.5 0.0 copy-done.1
  24.5 1.6 %krylov.1 = (f32[4,32,1024]{2,1,0:T(8,128)S(1)}, f32[32,128]{1,0:T(8,128)}) custom-call(s32[32,32]{1,0:T(8,128)S(1)} %copy-done.1, f32[8,48,128]{2,1,0:T(8,128)S(1)} %all-to-all-done.got, f32[32,1024]{1,0:T(8,128)S(1)} %copy-done, f32[56,128]{1,0:T(8,128)S(1)} %collective-permute-done.4.rows_a, f32[24,128]{1,0:T(8,128)S(1)} %rim.1.rows_b), custom_call_target="tpu_custom_call" | custom-call | tf_op jit(solution)/shard_map/krylov/pallas_call | solution.py:490
  26.1 2.8 %all-to-all-start.1 = ((f32[32,1,128]{2,1,0:T(1,128)}), f32[32,1,128]{2,1,0:T(1,128)S(1)}, u32[]{:S(2)}, u32[]{:S(2)}) async-start(f32[32,1,128]{2,1,0:T(1,128)} %bitcast.1), calls=%async_computation.1 | async-start | bytes 32768 | tf_op jit(solution)/shard_map/all_to_all | solution.py:498
  28.9 1.6 %collective-permute-start.5 = (f32[32,128]{1,0:T(8,128)S(1)}, f32[32,128]{1,0:T(8,128)S(1)}, u32[]{:S(2)}, u32[]{:S(2)}) collective-permute-start(f32[32,128]{1,0:T(8,128)S(1)} %get-tuple-element.35), channel_id=1, source_target_pairs={{0,24},{7,31},{1,2},{2,1},{3,4},{4,3},{5,6},{6,5},{8,16},{15,23},{... | collective-permute-start | bytes 49160 | tf_op jit(solution)/shard_map/ppermute | solution.py:478
  30.5 1.6 %collective-permute-done.5.rows_b = f32[32,128]{1,0:T(8,128)S(1)} collective-permute-done((f32[32,128]{1,0:T(8,128)S(1)}, f32[32,128]{1,0:T(8,128)S(1)}, u32[]{:S(2)}, u32[]{:S(2)}) %collective-permute-start.5) | collective-permute-done | bytes 16416 | tf_op jit(solution)/shard_map/ppermute | solution.py:478
  32.1 2.8 %tracer.1 = f32[16,128,256]{2,1,0:T(8,128)} custom-call(f32[16,128,256]{2,1,0:T(8,128)S(1)} %get-tuple-element.21.theta, f32[128,256]{1,0:T(8,128)S(1)} %get-tuple-element.22.ocean, f32[128,256]{1,0:T(8,128)S(1)} %get-tuple-element.23.coef, f32[48,128]{1,0:T(8,128)S(1)} %collective-permute-done.got_a.rest_1_, ...), custom_call_target="tpu_custom_call" | custom-call | flops 6291456 | bytes 4194304 | tf_op jit(solution)/shard_map/tracer/pallas_call | solution.py:479
  34.9 1.1 %all-to-all-done.1 = f32[32,1,128]{2,1,0:T(1,128)S(1)} async-done(((f32[32,1,128]{2,1,0:T(1,128)}), f32[32,1,128]{2,1,0:T(1,128)S(1)}, u32[]{:S(2)}, u32[]{:S(2)}) %all-to-all-start.1) | async-done | bytes 16416 | tf_op jit(solution)/shard_map/all_to_all | solution.py:498
  35.9 0.8 %combine.1 = f32[32,1024]{1,0:T(8,128)} custom-call(f32[32,128]{1,0:T(8,128)S(1)} %bitcast.4, f32[4,32,1024]{2,1,0:T(8,128)S(1)} %get-tuple-element.39.basis), custom_call_target="tpu_custom_call" | custom-call | tf_op jit(solution)/shard_map/combine/pallas_call | solution.py:499
  (1 shorter events, 0.0 us)
Async XLA Ops:
  3.2 8.5 %collective-permute-start.1 = (f32[80,128]{1,0:T(8,128)S(1)}, f32[80,128]{1,0:T(8,128)S(1)}, u32[]{:S(2)}, u32[]{:S(2)}) collective-permute-start(f32[80,128]{1,0:T(8,128)S(1)} %get-tuple-element.25.tops_b.rest_0_), channel_id=1, source_target_pairs={{0,24},{8,16},{16,8},{24,0},{1,25},{9,17},{17,9},{25,1},{2,26},{10... | collective-permute-start | bytes 122888 | tf_op jit(solution)/shard_map/ppermute | solution.py:438
  5.7 6.0 %collective-permute-start = (f32[48,128]{1,0:T(8,128)S(1)}, f32[48,128]{1,0:T(8,128)S(1)}, u32[]{:S(2)}, u32[]{:S(2)}) collective-permute-start(f32[48,128]{1,0:T(8,128)S(1)} %get-tuple-element.24), channel_id=1, source_target_pairs={{0,8},{8,0},{16,24},{24,16},{1,9},{9,1},{17,25},{25,17},{2,10},{10... | collective-permute-start | bytes 73736 | tf_op jit(solution)/shard_map/ppermute | solution.py:437
  6.3 5.3 %collective-permute-start.2 = (f32[24,128]{1,0:T(8,128)S(1)}, f32[24,128]{1,0:T(8,128)S(1)}, u32[]{:S(2)}, u32[]{:S(2)}) collective-permute-start(f32[24,128]{1,0:T(8,128)S(1)} %get-tuple-element.29), channel_id=1, source_target_pairs={{0,16},{8,24},{16,0},{24,8},{1,17},{9,25},{17,1},{25,9},{2,18},{10... | collective-permute-start | bytes 36872 | tf_op jit(solution)/shard_map/ppermute | solution.py:440
  6.4 10.3 %collective-permute-start.3 = (f32[24,128]{1,0:T(8,128)S(1)}, f32[24,128]{1,0:T(8,128)S(1)}, u32[]{:S(2)}, u32[]{:S(2)}) collective-permute-start(f32[24,128]{1,0:T(8,128)S(1)} %get-tuple-element.33), channel_id=1, source_target_pairs={{0,31},{1,2},{2,1},{3,4},{4,3},{5,6},{6,5},{7,8},{8,7},{9,10},{10,... | collective-permute-start | bytes 36872 | tf_op jit(solution)/shard_map/ppermute | solution.py:462
  12.5 12.0 %all-to-all-start = ((f32[8,48,128]{2,1,0:T(8,128)}), f32[8,48,128]{2,1,0:T(8,128)S(1)}, u32[]{:S(2)}, u32[]{:S(2)}) async-start(f32[8,48,128]{2,1,0:T(8,128)} %forcing.1), calls=%async_computation | async-start | bytes 393216 | tf_op jit(solution)/shard_map/all_to_all | solution.py:460
  16.7 7.8 %copy-start = (f32[32,1024]{1,0:T(8,128)S(1)}, f32[32,1024]{1,0:T(8,128)}, u32[]{:S(2)}) copy-start(f32[32,1024]{1,0:T(8,128)} %diag.1) | copy-start | bytes 393220
  16.7 7.8 %copy-start.1 = (s32[32,32]{1,0:T(8,128)S(1)}, s32[32,32]{1,0:T(8,128)}, u32[]{:S(2)}) copy-start(s32[32,32]{1,0:T(8,128)} %table.1) | copy-start | bytes 12292
  16.7 4.4 %collective-permute-start.4 = (f32[56,128]{1,0:T(8,128)S(1)}, f32[56,128]{1,0:T(8,128)S(1)}, u32[]{:S(2)}, u32[]{:S(2)}) collective-permute-start(f32[56,128]{1,0:T(8,128)S(1)} %get-tuple-element.34), channel_id=1, source_target_pairs={{0,1},{1,0},{2,3},{3,2},{4,5},{5,4},{6,7},{7,6},{8,9},{9,8},{10,11... | collective-permute-start | bytes 86024 | tf_op jit(solution)/shard_map/ppermute | solution.py:473
  26.1 9.8 %all-to-all-start.1 = ((f32[32,1,128]{2,1,0:T(1,128)}), f32[32,1,128]{2,1,0:T(1,128)S(1)}, u32[]{:S(2)}, u32[]{:S(2)}) async-start(f32[32,1,128]{2,1,0:T(1,128)} %bitcast.1), calls=%async_computation.1 | async-start | bytes 32768 | tf_op jit(solution)/shard_map/all_to_all | solution.py:498
  28.9 3.2 %collective-permute-start.5 = (f32[32,128]{1,0:T(8,128)S(1)}, f32[32,128]{1,0:T(8,128)S(1)}, u32[]{:S(2)}, u32[]{:S(2)}) collective-permute-start(f32[32,128]{1,0:T(8,128)S(1)} %get-tuple-element.35), channel_id=1, source_target_pairs={{0,24},{7,31},{1,2},{2,1},{3,4},{4,3},{5,6},{6,5},{8,16},{15,23},{... | collective-permute-start | bytes 49160 | tf_op jit(solution)/shard_map/ppermute | solution.py:478

commit v8 on v7

--- a/solution.py
+++ b/solution.py
@@ -112,7 +112,10 @@
     t = mask * total
     inner = (iota((cy, cx), 0) > 0) & (iota((cy, cx), 0) < cy - 1) & (iota((cy, cx), 1) > 0) & (iota((cy, cx), 1) < cx - 1)
     kept = jnp.where(inner, t, 0.0)
-    stats = [total_of(v) for v in (kept * t, kept * (4.0 * t - beside(t)), wet, wet * strip[...])]
+    stats = []
+    for pair in ((wet, wet * strip[...]), (kept * t, kept * (4.0 * t - beside(t)))):
+        pair = jnp.sum(jnp.concatenate([jnp.sum(v, axis=0, keepdims=True) for v in pair], axis=0), axis=1, keepdims=True)
+        stats = [pair[:1], pair[1:]] + stats
     spot = iota((EDGE, 128), 1)
     mine = (spot >= lon * width) & (spot < (lon + 1) * width)
     for n, value in enumerate(stats):

time: 37 us -> 37 us (level)
  no operation moved by 1% of the time
where the time goes in v8:
time: 37 us; the launch traced here: 36.8 us
  starting transfers between devices  19.1 us (52%)
  Pallas kernels  8.61 us (23%)
  waiting for transfers between devices  8.38 us (23%)
  between operations  0.69 us (2%)
    ppermute x1, starting transfers between devices, per_device(): lax.ppermute(row_b, joint, [(i, (i + 1 if i % 2 else i - 1) % devices) fo...  5.28 us
    all_to_all x1, starting transfers between devices, per_device(): got = lax.all_to_all(chunks, 'lat', split_axis=0, concat_axis=0, tiled=True)  4.17 us
    all_to_all x1, waiting for transfers between devices, per_device(): got = lax.all_to_all(chunks, 'lat', split_axis=0, concat_axis=0, tiled=True)  3.37 us
    all_to_all x1, starting transfers between devices, per_device(): gram = lax.all_to_all(gram, joint, split_axis=0, concat_axis=0, tiled=True)  2.76 us
    pallas_call x1, Pallas kernels, per_device(): pl.pallas_call(functools.partial(tracer_kernel, last), in_specs=[VMEM] *...  2.75 us
    pallas_call x1, Pallas kernels, per_device(): pl.pallas_call(functools.partial(sum_kernel, cell), in_specs=[HBM] * 5, o...  2.54 us
    ppermute x1, starting transfers between devices, per_device(): got_b = lax.ppermute(pay_b, 'lon', pairs_b)  2.47 us
    ppermute x1, waiting for transfers between devices, per_device(): rows_a = lax.ppermute(row_a, joint, [(i, i ^ 1) for i in range(devices)])  2.3 us
  transfers between devices with their start and end apart: 8, of which 4 were waited for; matrix products, arithmetic and copies ran while one was open for 0% of the time, Pallas kernels for 10%

profile of v8, /device:TPU:0, one launch (start us, length us, event | category | flops | bytes accessed | tf_op | source)
XLA Modules:
  0.0 36.8 jit_solution(12976120209364570339)
XLA Ops:
  0.6 2.5 %level_sum.1 = (f32[16,128,256]{2,1,0:T(8,128)S(1)}, f32[128,256]{1,0:T(8,128)S(1)}, f32[128,256]{1,0:T(8,128)S(1)}, f32[256,128]{1,0:T(8,128)S(1)}, f32[256,128...) custom-call(f32[16]{0:T(128)} %weight_hbm.1, ...), custom_call_target="tpu_custom_call" | custom-call | tf_op jit(solution)/shard_map/level_sum/pallas_call | solution.py:409
  3.2 2.5 %collective-permute-start.1 = (f32[80,128]{1,0:T(8,128)S(1)}, f32[80,128]{1,0:T(8,128)S(1)}, u32[]{:S(2)}, u32[]{:S(2)}) collective-permute-start(f32[80,128]{1,0:T(8,128)S(1)} %get-tuple-element.25.tops_b.rest_0_), channel_id=1, source_target_pairs={{0,24},{8,16},{16,8},{24,0},{1,25},{9,17},{17,9},{25,1},{2,26},{10... | collective-permute-start | bytes 122888 | tf_op jit(solution)/shard_map/ppermute | solution.py:441
  5.6 0.7 %collective-permute-start = (f32[48,128]{1,0:T(8,128)S(1)}, f32[48,128]{1,0:T(8,128)S(1)}, u32[]{:S(2)}, u32[]{:S(2)}) collective-permute-start(f32[48,128]{1,0:T(8,128)S(1)} %get-tuple-element.24), channel_id=1, source_target_pairs={{0,8},{8,0},{16,24},{24,16},{1,9},{9,1},{17,25},{25,17},{2,10},{10... | collective-permute-start | bytes 73736 | tf_op jit(solution)/shard_map/ppermute | solution.py:440
  6.3 0.0 collective-permute-start.2
  6.4 5.3 %collective-permute-start.3 = (f32[24,128]{1,0:T(8,128)S(1)}, f32[24,128]{1,0:T(8,128)S(1)}, u32[]{:S(2)}, u32[]{:S(2)}) collective-permute-start(f32[24,128]{1,0:T(8,128)S(1)} %get-tuple-element.33), channel_id=1, source_target_pairs={{0,31},{1,2},{2,1},{3,4},{4,3},{5,6},{6,5},{7,8},{8,7},{9,10},{10,... | collective-permute-start | bytes 36872 | tf_op jit(solution)/shard_map/ppermute | solution.py:465
  11.6 0.0 collective-permute-done.2.tops_a.rest_3_
  11.6 0.0 collective-permute-done.got_a.rest_1_
  11.6 0.0 collective-permute-done.1.got_b.tops_m.rest_2_
  11.7 0.9 %forcing.1 = f32[8,48,128]{2,1,0:T(8,128)} custom-call(f32[256,128]{1,0:T(8,128)S(1)} %get-tuple-element.26.tt, f32[256,128]{1,0:T(8,128)S(1)} %get-tuple-element.27.kt, f32[8,256]{1,0:T(8,128)S(1)} %get-tuple-element.28.ends, f32[48,128]{1,0:T(8,128)S(1)} %collective-permute-done.got_a.rest_1_, f32[80,128]{1,0:T(8,128)S(1)} %collective-permute-done.1.got_b.tops_m.rest_2_, ...), custom_call_target="tpu_custom_call" | custom-call | tf_op jit(solution)/shard_map/forcing/pallas_call | solution.py:454
  12.5 4.2 %all-to-all-start = ((f32[8,48,128]{2,1,0:T(8,128)}), f32[8,48,128]{2,1,0:T(8,128)S(1)}, u32[]{:S(2)}, u32[]{:S(2)}) async-start(f32[8,48,128]{2,1,0:T(8,128)} %forcing.1), calls=%async_computation | async-start | bytes 393216 | tf_op jit(solution)/shard_map/all_to_all | solution.py:463
  16.7 0.0 copy-start
  16.7 0.0 copy-start.1
  16.7 0.0 collective-permute-done.3.rows
  16.7 2.1 %collective-permute-start.4 = (f32[56,128]{1,0:T(8,128)S(1)}, f32[56,128]{1,0:T(8,128)S(1)}, u32[]{:S(2)}, u32[]{:S(2)}) collective-permute-start(f32[56,128]{1,0:T(8,128)S(1)} %get-tuple-element.34), channel_id=1, source_target_pairs={{0,1},{1,0},{2,3},{3,2},{4,5},{5,4},{6,7},{7,6},{8,9},{9,8},{10,11... | collective-permute-start | bytes 86024 | tf_op jit(solution)/shard_map/ppermute | solution.py:476
  18.8 2.3 %collective-permute-done.4.rows_a = f32[56,128]{1,0:T(8,128)S(1)} collective-permute-done((f32[56,128]{1,0:T(8,128)S(1)}, f32[56,128]{1,0:T(8,128)S(1)}, u32[]{:S(2)}, u32[]{:S(2)}) %collective-permute-start.4) | collective-permute-done | bytes 28704 | tf_op jit(solution)/shard_map/ppermute | solution.py:476
  21.1 3.4 %all-to-all-done.got = f32[8,48,128]{2,1,0:T(8,128)S(1)} async-done(((f32[8,48,128]{2,1,0:T(8,128)}), f32[8,48,128]{2,1,0:T(8,128)S(1)}, u32[]{:S(2)}, u32[]{:S(2)}) %all-to-all-start) | async-done | bytes 196640 | tf_op jit(solution)/shard_map/all_to_all | solution.py:463
  24.5 0.0 copy-done
  24.5 0.0 copy-done.1
  24.5 1.6 %krylov.1 = (f32[4,32,1024]{2,1,0:T(8,128)S(1)}, f32[32,128]{1,0:T(8,128)}) custom-call(s32[32,32]{1,0:T(8,128)S(1)} %copy-done.1, f32[8,48,128]{2,1,0:T(8,128)S(1)} %all-to-all-done.got, f32[32,1024]{1,0:T(8,128)S(1)} %copy-done, f32[56,128]{1,0:T(8,128)S(1)} %collective-permute-done.4.rows_a, f32[24,128]{1,0:T(8,128)S(1)} %rim.1.rows_b), custom_call_target="tpu_custom_call" | custom-call | tf_op jit(solution)/shard_map/krylov/pallas_call | solution.py:493
  26.1 2.8 %all-to-all-start.1 = ((f32[32,1,128]{2,1,0:T(1,128)}), f32[32,1,128]{2,1,0:T(1,128)S(1)}, u32[]{:S(2)}, u32[]{:S(2)}) async-start(f32[32,1,128]{2,1,0:T(1,128)} %bitcast.1), calls=%async_computation.1 | async-start | bytes 32768 | tf_op jit(solution)/shard_map/all_to_all | solution.py:501
  28.9 1.6 %collective-permute-start.5 = (f32[32,128]{1,0:T(8,128)S(1)}, f32[32,128]{1,0:T(8,128)S(1)}, u32[]{:S(2)}, u32[]{:S(2)}) collective-permute-start(f32[32,128]{1,0:T(8,128)S(1)} %get-tuple-element.35), channel_id=1, source_target_pairs={{0,24},{7,31},{1,2},{2,1},{3,4},{4,3},{5,6},{6,5},{8,16},{15,23},{... | collective-permute-start | bytes 49160 | tf_op jit(solution)/shard_map/ppermute | solution.py:481
  30.5 1.6 %collective-permute-done.5.rows_b = f32[32,128]{1,0:T(8,128)S(1)} collective-permute-done((f32[32,128]{1,0:T(8,128)S(1)}, f32[32,128]{1,0:T(8,128)S(1)}, u32[]{:S(2)}, u32[]{:S(2)}) %collective-permute-start.5) | collective-permute-done | bytes 16416 | tf_op jit(solution)/shard_map/ppermute | solution.py:481
  32.1 2.8 %tracer.1 = f32[16,128,256]{2,1,0:T(8,128)} custom-call(f32[16,128,256]{2,1,0:T(8,128)S(1)} %get-tuple-element.21.theta, f32[128,256]{1,0:T(8,128)S(1)} %get-tuple-element.22.ocean, f32[128,256]{1,0:T(8,128)S(1)} %get-tuple-element.23.coef, f32[48,128]{1,0:T(8,128)S(1)} %collective-permute-done.got_a.rest_1_, ...), custom_call_target="tpu_custom_call" | custom-call | flops 6291456 | bytes 4194304 | tf_op jit(solution)/shard_map/tracer/pallas_call | solution.py:482
  34.9 1.1 %all-to-all-done.1 = f32[32,1,128]{2,1,0:T(1,128)S(1)} async-done(((f32[32,1,128]{2,1,0:T(1,128)}), f32[32,1,128]{2,1,0:T(1,128)S(1)}, u32[]{:S(2)}, u32[]{:S(2)}) %all-to-all-start.1) | async-done | bytes 16416 | tf_op jit(solution)/shard_map/all_to_all | solution.py:501
  35.9 0.8 %combine.1 = f32[32,1024]{1,0:T(8,128)} custom-call(f32[32,128]{1,0:T(8,128)S(1)} %bitcast.4, f32[4,32,1024]{2,1,0:T(8,128)S(1)} %get-tuple-element.39.basis), custom_call_target="tpu_custom_call" | custom-call | tf_op jit(solution)/shard_map/combine/pallas_call | solution.py:502
  (1 shorter events, 0.0 us)
Async XLA Ops:
  3.2 8.5 %collective-permute-start.1 = (f32[80,128]{1,0:T(8,128)S(1)}, f32[80,128]{1,0:T(8,128)S(1)}, u32[]{:S(2)}, u32[]{:S(2)}) collective-permute-start(f32[80,128]{1,0:T(8,128)S(1)} %get-tuple-element.25.tops_b.rest_0_), channel_id=1, source_target_pairs={{0,24},{8,16},{16,8},{24,0},{1,25},{9,17},{17,9},{25,1},{2,26},{10... | collective-permute-start | bytes 122888 | tf_op jit(solution)/shard_map/ppermute | solution.py:441
  5.6 6.0 %collective-permute-start = (f32[48,128]{1,0:T(8,128)S(1)}, f32[48,128]{1,0:T(8,128)S(1)}, u32[]{:S(2)}, u32[]{:S(2)}) collective-permute-start(f32[48,128]{1,0:T(8,128)S(1)} %get-tuple-element.24), channel_id=1, source_target_pairs={{0,8},{8,0},{16,24},{24,16},{1,9},{9,1},{17,25},{25,17},{2,10},{10... | collective-permute-start | bytes 73736 | tf_op jit(solution)/shard_map/ppermute | solution.py:440
  6.3 5.3 %collective-permute-start.2 = (f32[24,128]{1,0:T(8,128)S(1)}, f32[24,128]{1,0:T(8,128)S(1)}, u32[]{:S(2)}, u32[]{:S(2)}) collective-permute-start(f32[24,128]{1,0:T(8,128)S(1)} %get-tuple-element.29), channel_id=1, source_target_pairs={{0,16},{8,24},{16,0},{24,8},{1,17},{9,25},{17,1},{25,9},{2,18},{10... | collective-permute-start | bytes 36872 | tf_op jit(solution)/shard_map/ppermute | solution.py:443
  6.4 10.3 %collective-permute-start.3 = (f32[24,128]{1,0:T(8,128)S(1)}, f32[24,128]{1,0:T(8,128)S(1)}, u32[]{:S(2)}, u32[]{:S(2)}) collective-permute-start(f32[24,128]{1,0:T(8,128)S(1)} %get-tuple-element.33), channel_id=1, source_target_pairs={{0,31},{1,2},{2,1},{3,4},{4,3},{5,6},{6,5},{7,8},{8,7},{9,10},{10,... | collective-permute-start | bytes 36872 | tf_op jit(solution)/shard_map/ppermute | solution.py:465
  12.5 12.0 %all-to-all-start = ((f32[8,48,128]{2,1,0:T(8,128)}), f32[8,48,128]{2,1,0:T(8,128)S(1)}, u32[]{:S(2)}, u32[]{:S(2)}) async-start(f32[8,48,128]{2,1,0:T(8,128)} %forcing.1), calls=%async_computation | async-start | bytes 393216 | tf_op jit(solution)/shard_map/all_to_all | solution.py:463
  16.7 7.8 %copy-start = (f32[32,1024]{1,0:T(8,128)S(1)}, f32[32,1024]{1,0:T(8,128)}, u32[]{:S(2)}) copy-start(f32[32,1024]{1,0:T(8,128)} %diag.1) | copy-start | bytes 393220
  16.7 7.8 %copy-start.1 = (s32[32,32]{1,0:T(8,128)S(1)}, s32[32,32]{1,0:T(8,128)}, u32[]{:S(2)}) copy-start(s32[32,32]{1,0:T(8,128)} %table.1) | copy-start | bytes 12292
  16.7 4.4 %collective-permute-start.4 = (f32[56,128]{1,0:T(8,128)S(1)}, f32[56,128]{1,0:T(8,128)S(1)}, u32[]{:S(2)}, u32[]{:S(2)}) collective-permute-start(f32[56,128]{1,0:T(8,128)S(1)} %get-tuple-element.34), channel_id=1, source_target_pairs={{0,1},{1,0},{2,3},{3,2},{4,5},{5,4},{6,7},{7,6},{8,9},{9,8},{10,11... | collective-permute-start | bytes 86024 | tf_op jit(solution)/shard_map/ppermute | solution.py:476
  26.1 9.8 %all-to-all-start.1 = ((f32[32,1,128]{2,1,0:T(1,128)}), f32[32,1,128]{2,1,0:T(1,128)S(1)}, u32[]{:S(2)}, u32[]{:S(2)}) async-start(f32[32,1,128]{2,1,0:T(1,128)} %bitcast.1), calls=%async_computation.1 | async-start | bytes 32768 | tf_op jit(solution)/shard_map/all_to_all | solution.py:501
  28.9 3.2 %collective-permute-start.5 = (f32[32,128]{1,0:T(8,128)S(1)}, f32[32,128]{1,0:T(8,128)S(1)}, u32[]{:S(2)}, u32[]{:S(2)}) collective-permute-start(f32[32,128]{1,0:T(8,128)S(1)} %get-tuple-element.35), channel_id=1, source_target_pairs={{0,24},{7,31},{1,2},{2,1},{3,4},{4,3},{5,6},{6,5},{8,16},{15,23},{... | collective-permute-start | bytes 49160 | tf_op jit(solution)/shard_map/ppermute | solution.py:481
